TPU v7x, 128 devices: a whole 4x4x4 slice. The times are simulated.
128 devices in a mesh: fsdp: 32 (over z, x_hi, y), tp: 4 (over x_lo, core).
Axes of the slice: x: 4 (x_hi: 2, x_lo: 2; x = x_hi * 2 + x_lo), y: 4, z: 4, core: 2. Of those that a mesh axis runs over, the one named last changes fastest.
Arguments:
- inputs: bfloat16 [16384, 1024], P(('fsdp', 'tp')), may hold values from -24 to 24
- segments: int32 [32, 512], P('fsdp'), may hold values from 0 to 3, never falling along the last dimension, each value on 1 to 400 neighbouring positions
- routes: int32 [16384, 8], P('fsdp'), may hold values from 0 to 31, all different within a row; in each aligned block of 128 rows (0 to 127, 128 to 255, ...) at most 33 rows name the same one
- query_weight: bfloat16 [1024, 1024], P('fsdp', 'tp'), may hold values from -0.25 to 0.25
- key_projection_weight: bfloat16 [1024, 512], P('fsdp', 'tp'), may hold values from -0.1875 to 0.1875
- value_projection_weight: bfloat16 [1024, 512], P('fsdp', 'tp'), may hold values from -0.1875 to 0.1875
- out_weight: bfloat16 [1024, 1024], P('tp', 'fsdp'), may hold values from -1.25 to 1.25
- router_weight: bfloat16 [1024, 32], P('fsdp'), may hold values from -0.09375 to 0.09375
- first_gain: bfloat16 [1024], P('fsdp'), may hold values from 0.5 to 1.5
- second_gain: bfloat16 [1024], P('fsdp'), may hold values from 0.5 to 1.5
- gate_weight: bfloat16 [32, 1024, 512], P(None, 'fsdp', 'tp'), may hold values from -0.1875 to 0.1875
- up_weight: bfloat16 [32, 1024, 512], P(None, 'fsdp', 'tp'), may hold values from -0.1875 to 0.1875
- down_weight: bfloat16 [32, 512, 1024], P(None, 'tp', 'fsdp'), may hold values from -1.25 to 1.25
- cotangent: bfloat16 [16384, 1024], P(('fsdp', 'tp')), may hold values from -24 to 24
Outputs:
- output: bfloat16 [16384, 1024], P(('fsdp', 'tp'))
- grad_inputs: float32 [16384, 1024], P(('fsdp', 'tp'))
- grad_query: float32 [1024, 1024], P('fsdp', 'tp')
- grad_key: float32 [1024, 512], P('fsdp', 'tp')
- grad_value: float32 [1024, 512], P('fsdp', 'tp')
- grad_out: float32 [1024, 1024], P('tp', 'fsdp')
- grad_router: float32 [1024, 32], P('fsdp')
- grad_first: float32 [1024], P('fsdp')
- grad_second: float32 [1024], P('fsdp')
- grad_gate: float32 [32, 1024, 512], P(None, 'fsdp', 'tp')
- grad_up: float32 [32, 1024, 512], P(None, 'fsdp', 'tp')
- grad_down: float32 [32, 512, 1024], P(None, 'tp', 'fsdp')
Inputs may be any that keep to these rules, and one draw needn't show every extreme that they name: `segments`: each row is one sequence; its document numbers never fall, each document has 1 to 400 tokens, and one document of each row has exactly 400. `routes`: each row names 8 different experts. In each aligned block of rows held by one device, no expert is named by more than 33 rows, a bound that some block reaches.
All inputs are finite; a program needn't handle non-finite values.
Results may differ from a plain program's by a relative error of at most 0.029.
Values may be sent and summed in bfloat16 or wider, within the bound.
A program may use at most 192 MiB of HBM per device.

v0:
```python
import math

import jax
import jax.numpy as jnp
from jax import lax
from jax.sharding import PartitionSpec as P

HEAD_SIZE = 64
EXPERTS = 32
TOP = 8


EPSILON = 1e-06
ROPE_BASE = 10000.0
MASKED = -1e30


def turned_gather(arrays, axis, dims):
    turned = [jnp.moveaxis(a, dim, 0) for a, dim in zip(arrays, dims)]
    widths = [t[0].size for t in turned]
    both = jnp.concatenate([t.reshape(-1, w) for t, w in zip(turned, widths)], axis=1)
    out = lax.all_gather(both, axis, axis=0, tiled=True)
    parts = jnp.split(out, [sum(widths[:k]) for k in range(1, len(widths))], axis=1)
    return tuple(
        (
            jnp.moveaxis(b.reshape(-1, *t.shape[1:]), 0, dim)
            for b, t, dim in zip(parts, turned, dims)
        )
    )


def from_everyone(shard, axis):
    copies = jnp.broadcast_to(shard, (lax.axis_size(axis), *shard.shape))
    return lax.all_to_all(copies, axis, split_axis=0, concat_axis=0, tiled=True)


def laid_out(parts, dim):
    lengths = list(parts.shape[1:])
    lengths[dim] *= parts.shape[0]
    return jnp.moveaxis(parts, 0, dim).reshape(lengths)


def gathered_copies(shard, axis, dim):
    parts = from_everyone(shard, axis)
    return laid_out(parts, dim)


def in_blocks(shard, dim, peers):
    lengths = shard.shape
    parts = shard.reshape(*lengths[:dim], peers, lengths[dim] // peers, *lengths[dim + 1 :])
    return jnp.moveaxis(parts, dim, 0)


def sent_and_summed(shard, axis, dim):
    parts = in_blocks(shard, dim, lax.axis_size(axis))
    arrived = lax.all_to_all(parts, axis, split_axis=0, concat_axis=0, tiled=True)
    return arrived.sum(axis=0)


def sent_together(arrays, axis, dim, along):
    widths = [a.shape[along] for a in arrays]
    both = jnp.concatenate(arrays, axis=along)
    out = lax.all_gather(both, axis, axis=dim, tiled=True)
    return tuple(jnp.split(out, [sum(widths[:k]) for k in range(1, len(widths))], axis=along))


def side_by_side(arrays, axis, split_dim, concat_dim, along):
    widths = [a.shape[along] for a in arrays]
    both = jnp.concatenate(arrays, axis=along)
    out = lax.all_to_all(both, axis, split_axis=split_dim, concat_axis=concat_dim, tiled=True)
    return tuple(jnp.split(out, [sum(widths[:k]) for k in range(1, len(widths))], axis=along))


def side_by_side_2(arrays, axis, split_dim, concat_dim, along):
    widths = [math.prod(a.shape[along:]) for a in arrays]
    both = jnp.concatenate(
        [a.reshape(*a.shape[:along], w) for a, w in zip(arrays, widths)], axis=along
    )
    out = lax.all_to_all(both, axis, split_axis=split_dim, concat_axis=concat_dim, tiled=True)
    parts = jnp.split(out, [sum(widths[:k]) for k in range(1, len(widths))], axis=along)
    return tuple((b.reshape(*out.shape[:along], *a.shape[along:]) for a, b in zip(arrays, parts)))


def summed_on_arrival(shard, axis, dim):
    peers = lax.axis_size(axis)
    parts = lax.all_to_all(in_blocks(shard, dim, peers), axis, 0, 0, tiled=True)
    return jnp.sum(parts.astype(jnp.float32), axis=0)


def of_everyone(shard, axis):
    everything = from_everyone(shard, axis)
    return jnp.sum(everything, axis=0)


def together(arrays, axis):
    ravelled, at, gathered = (jnp.concatenate([a.reshape(-1) for a in arrays]), 0, [])
    running = of_everyone(ravelled, axis)
    for a in arrays:
        gathered.append(running[at : at + a.size].reshape(a.shape))
        at += a.size
    return tuple(gathered)


def in_one_piece(arrays, axis, dim, along):
    widths = [a.shape[along] for a in arrays]
    both = jnp.concatenate(arrays, axis=along)
    out = lax.psum_scatter(both, axis, scatter_dimension=dim, tiled=True)
    return tuple(jnp.split(out, [sum(widths[:k]) for k in range(1, len(widths))], axis=along))


def sent_together_2(arrays, axis, dim, along):
    columns = [a.reshape(*a.shape[:along], -1) for a in arrays]
    both = jnp.concatenate(columns, axis=along)
    out, at, gathered = (lax.psum_scatter(both, axis, scatter_dimension=dim, tiled=True), 0, [])
    for a, column in zip(arrays, columns):
        piece = out[..., at : at + column.shape[along]]
        gathered.append(piece.reshape(*piece.shape[:along], *a.shape[along:]))
        at += column.shape[along]
    return tuple(gathered)


def dot_right(left_mat, right_mat):
    return lax.dot_general(
        left_mat, right_mat, (((1,), (1,)), ((), ())), preferred_element_type=jnp.float32
    )


def dot_left(left_mat, right_mat):
    return lax.dot_general(
        left_mat, right_mat, (((0,), (0,)), ((), ())), preferred_element_type=jnp.float32
    )


def rope_tables(seg_ids):
    length_total = seg_ids.shape[-1]
    places = jnp.arange(length_total, dtype=jnp.int32)
    starts_new = jnp.concatenate(
        [
            jnp.ones(seg_ids.shape[:-1] + (1,), dtype=jnp.bool_),
            seg_ids[..., 1:] != seg_ids[..., :-1],
        ],
        axis=-1,
    )
    doc_start = lax.cummax(jnp.where(starts_new, places, 0), axis=seg_ids.ndim - 1)
    position = (places - doc_start).astype(jnp.float32)
    halves = jnp.arange(HEAD_SIZE // 2, dtype=jnp.int32).astype(jnp.float32)
    rate_list = jnp.exp(halves * (-2.0 * math.log(ROPE_BASE) / HEAD_SIZE))
    angles = position[..., None] * rate_list
    return (jnp.cos(angles), jnp.sin(angles))


def rotary_apply(values, cosine_lookup, sine_lookup):
    half_dim = values.shape[-1] // 2
    front_half = values[..., :half_dim]
    back_half = values[..., half_dim:]
    cos_wide = cosine_lookup[..., None, :]
    sin_wide = sine_lookup[..., None, :]
    return jnp.concatenate(
        [
            front_half * cos_wide - back_half * sin_wide,
            back_half * cos_wide + front_half * sin_wide,
        ],
        axis=-1,
    )


def rotate_back(values, cosine_lookup, sine_lookup):
    half_dim = values.shape[-1] // 2
    front_half = values[..., :half_dim]
    back_half = values[..., half_dim:]
    cos_wide = cosine_lookup[..., None, :]
    sin_wide = sine_lookup[..., None, :]
    return jnp.concatenate(
        [
            front_half * cos_wide + back_half * sin_wide,
            back_half * cos_wide - front_half * sin_wide,
        ],
        axis=-1,
    )


def dispatch(route_ids, capacity):
    flat_ids = route_ids.reshape(-1)
    entry_count = flat_ids.shape[0]
    onehot = (flat_ids[:, None] == jnp.arange(EXPERTS, dtype=jnp.int32)[None, :]).astype(jnp.int32)
    earlier = jnp.cumsum(onehot, axis=0) - onehot
    slot_of = jnp.sum(earlier * onehot, axis=1)
    places = flat_ids * capacity + slot_of
    slot_table = jnp.full((EXPERTS * capacity,), entry_count, dtype=jnp.int32)
    slot_table = slot_table.at[places].set(jnp.arange(entry_count, dtype=jnp.int32))
    return slot_table.reshape(EXPERTS, capacity)


def norm_back(values, inverse, gain_vec, grad_out):
    scaled = grad_out * gain_vec
    grad_gain = jnp.sum(grad_out * values * inverse, axis=0)
    grad_vals = inverse * scaled - values * inverse * inverse * inverse * jnp.mean(
        scaled * values, axis=-1, keepdims=True
    )
    return (grad_vals, grad_gain)


def block_scores(block_of_queries, keys_seq, seg_query, seg_keys, offset):
    rows_of_queries = block_of_queries.shape[0]
    grouped_heads = block_of_queries.reshape(rows_of_queries, keys_seq.shape[1], -1, HEAD_SIZE)
    scores = jnp.einsum(
        "qkgd,tkd->kgqt", grouped_heads, keys_seq, preferred_element_type=jnp.float32
    ) * HEAD_SIZE ** (-0.5)
    query_place = offset + jnp.arange(rows_of_queries, dtype=jnp.int32)
    key_place = jnp.arange(keys_seq.shape[0], dtype=jnp.int32)
    allowed = (seg_query[:, None] == seg_keys[None, :]) & (
        query_place[:, None] >= key_place[None, :]
    )
    return (grouped_heads, jnp.where(allowed, scores, MASKED))


def attention_forward(queries, every_key, every_value, seg_ids):
    length_total = seg_ids.shape[1]
    block_len = min(512, length_total)
    block_count = length_total // block_len

    def one_sequence(pieces):
        query_seq, keys_seq, values_seq, seg_seq = pieces

        def one_block(block_id):
            offset = block_id * block_len
            grouped_heads, scores = block_scores(query_seq, keys_seq, seg_seq, seg_seq, offset)
            top_score = jnp.max(scores, axis=-1, keepdims=True)
            log_total = top_score + jnp.log(
                jnp.sum(jnp.exp(scores - top_score), axis=-1, keepdims=True)
            )
            shares = jnp.exp(scores - log_total).astype(jnp.bfloat16)
            mixed_vals = jnp.einsum(
                "kgqt,tkd->qkgd", shares, values_seq, preferred_element_type=jnp.float32
            )
            return (mixed_vals.reshape(block_len, -1, HEAD_SIZE), log_total)

        block_outs, block_totals = lax.map(one_block, jnp.arange(block_count, dtype=jnp.int32))
        return (block_outs.reshape(length_total, -1, HEAD_SIZE), block_totals)

    return lax.map(one_sequence, (queries, every_key, every_value, seg_ids))


def attention_backward(queries, every_key, every_value, seg_ids, grad_mixed, log_totals):
    length_total = seg_ids.shape[1]
    block_len = min(512, length_total)
    block_count = length_total // block_len

    def one_sequence(pieces):
        query_seq, keys_seq, values_seq, seg_seq, grad_seq, totals_seq = pieces

        def one_block(grad_sums, block_id):
            grad_keys, grad_values = grad_sums
            offset = block_id * block_len
            log_total = lax.dynamic_index_in_dim(totals_seq, block_id, 0, keepdims=False)
            grouped_heads, scores = block_scores(query_seq, keys_seq, seg_seq, seg_seq, offset)
            shares = jnp.exp(scores - log_total)
            grad_group = grad_seq.reshape(block_len, keys_seq.shape[1], -1, HEAD_SIZE)
            grad_shares = jnp.einsum(
                "qkgd,tkd->kgqt", grad_group, values_seq, preferred_element_type=jnp.float32
            )
            inner_sum = jnp.sum(shares * grad_shares, axis=-1, keepdims=True)
            grad_scores = (shares * (grad_shares - inner_sum)).astype(jnp.bfloat16)
            grad_query = jnp.einsum(
                "kgqt,tkd->qkgd", grad_scores, keys_seq, preferred_element_type=jnp.float32
            ) * HEAD_SIZE ** (-0.5)
            grad_keys = grad_keys + jnp.einsum(
                "kgqt,qkgd->tkd", grad_scores, grouped_heads, preferred_element_type=jnp.float32
            ) * HEAD_SIZE ** (-0.5)
            grad_values = grad_values + jnp.einsum(
                "kgqt,qkgd->tkd",
                shares.astype(jnp.bfloat16),
                grad_group,
                preferred_element_type=jnp.float32,
            )
            return ((grad_keys, grad_values), grad_query.reshape(block_len, -1, HEAD_SIZE))

        zero_keys = jnp.zeros(keys_seq.shape, jnp.float32)
        (grad_keys, grad_values), grad_queries = lax.scan(
            one_block, (zero_keys, zero_keys), jnp.arange(block_count, dtype=jnp.int32)
        )
        return (grad_queries.reshape(length_total, -1, HEAD_SIZE), grad_keys, grad_values)

    return lax.map(one_sequence, (queries, every_key, every_value, seg_ids, grad_mixed, log_totals))


def per_device(
    inputs,
    segments,
    routes,
    query_weight,
    key_projection_weight,
    value_projection_weight,
    out_weight,
    router_weight,
    first_gain,
    second_gain,
    gate_weight,
    up_weight,
    down_weight,
    cotangent,
):
    row_count, model_width = inputs.shape
    sequence_count, length_total = segments.shape
    group_rows = sequence_count * length_total
    my_offset = lax.axis_index("tp") * row_count
    tp_count = lax.axis_size("tp")
    query_mat, key_matrix, value_matrix, out_mat, router_mat, gain_one, gain_two = turned_gather(
        (
            query_weight,
            key_projection_weight,
            value_projection_weight,
            out_weight,
            router_weight,
            first_gain,
            second_gain,
        ),
        "fsdp",
        (0, 0, 0, 1, 0, 0, 0),
    )
    gain_one = gain_one.astype(jnp.float32)
    gain_two = gain_two.astype(jnp.float32)
    query_heads = query_mat.shape[1] // HEAD_SIZE
    key_heads = key_matrix.shape[1] // HEAD_SIZE
    inputs_wide = inputs.astype(jnp.float32)
    inverse_one = lax.rsqrt(jnp.mean(inputs_wide * inputs_wide, axis=-1, keepdims=True) + EPSILON)
    normalized_input = (inputs_wide * inverse_one * gain_one).astype(jnp.bfloat16)
    normed_all = gathered_copies(normalized_input, "tp", 0)
    cosine_lookup, sine_lookup = rope_tables(segments)
    query_lin = jnp.dot(normed_all, query_mat, preferred_element_type=jnp.float32).reshape(
        sequence_count, length_total, query_heads, HEAD_SIZE
    )
    key_lin = jnp.dot(normed_all, key_matrix, preferred_element_type=jnp.float32).reshape(
        sequence_count, length_total, key_heads, HEAD_SIZE
    )
    queries = rotary_apply(query_lin, cosine_lookup, sine_lookup).astype(jnp.bfloat16)
    every_key = rotary_apply(key_lin, cosine_lookup, sine_lookup).astype(jnp.bfloat16)
    every_value = (
        jnp.dot(normed_all, value_matrix, preferred_element_type=jnp.float32)
        .astype(jnp.bfloat16)
        .reshape(sequence_count, length_total, key_heads, HEAD_SIZE)
    )
    mixed_vals, log_totals = attention_forward(queries, every_key, every_value, segments)
    attended = mixed_vals.reshape(group_rows, query_heads * HEAD_SIZE).astype(jnp.bfloat16)
    middle = inputs_wide + sent_and_summed(
        jnp.dot(attended, out_mat, preferred_element_type=jnp.float32), "tp", 0
    )
    inverse_two = lax.rsqrt(jnp.mean(middle * middle, axis=-1, keepdims=True) + EPSILON)
    normed_two = (middle * inverse_two * gain_two).astype(jnp.bfloat16)
    logits = jnp.dot(normed_two, router_mat, preferred_element_type=jnp.float32)
    my_routes = lax.dynamic_slice_in_dim(routes, my_offset, row_count, 0)
    picker = (
        my_routes[:, :, None] == jnp.arange(router_mat.shape[1], dtype=jnp.int32)[None, None, :]
    ).astype(jnp.float32)
    chosen = jnp.sum(picker * logits[:, None, :], axis=-1)
    gate_values = jax.nn.softmax(chosen, axis=-1)
    gates_low = gate_values.astype(jnp.bfloat16)
    cap_dev = row_count * TOP * 33 // (EXPERTS * 32)
    expert_count, width_shard, hidden_shard = gate_weight.shape
    first_item = gate_weight.reshape(expert_count * width_shard, hidden_shard)
    second_item = up_weight.reshape(expert_count * width_shard, hidden_shard)
    third_item = down_weight.reshape(expert_count * hidden_shard, width_shard)
    first_all, second_all, third_all = (
        *sent_together((first_item, second_item), "tp", 0, 1),
        lax.all_gather(third_item, "tp", axis=0, tiled=True),
    )
    full_hidden = tp_count * hidden_shard
    gate_wide = jnp.transpose(
        first_all.reshape(tp_count, expert_count, width_shard, hidden_shard), (1, 2, 0, 3)
    ).reshape(expert_count, width_shard, full_hidden)
    up_wide = jnp.transpose(
        second_all.reshape(tp_count, expert_count, width_shard, hidden_shard), (1, 2, 0, 3)
    ).reshape(expert_count, width_shard, full_hidden)
    down_wide = jnp.transpose(
        third_all.reshape(tp_count, expert_count, hidden_shard, width_shard), (1, 3, 0, 2)
    ).reshape(expert_count, width_shard, full_hidden)
    slot_mine = dispatch(my_routes, cap_dev)
    token_mine = slot_mine // TOP
    rows_mine = jnp.concatenate([normed_two, jnp.zeros((1, model_width), jnp.bfloat16)], axis=0)[
        token_mine
    ]
    gates_mine = jnp.concatenate([gates_low.reshape(-1), jnp.zeros((1,), jnp.bfloat16)], axis=0)[
        slot_mine
    ]
    cot_mine = jnp.concatenate([cotangent, jnp.zeros((1, model_width), jnp.bfloat16)], axis=0)[
        token_mine
    ]
    gate_local, up_local, down_local, rows_local, gates_local, cot_local = (
        *side_by_side((gate_wide, up_wide, down_wide), "fsdp", 0, 1, 2),
        *side_by_side_2((rows_mine, gates_mine, cot_mine), "fsdp", 0, 1, 2),
    )
    local_count = gate_local.shape[0]
    gate_sel = gates_local.astype(jnp.float32)
    gate_act = jnp.einsum(
        "ncd,ndf->ncf", rows_local, gate_local, preferred_element_type=jnp.float32
    )
    up_act = jnp.einsum("ncd,ndf->ncf", rows_local, up_local, preferred_element_type=jnp.float32)
    sigmoid_gate = jax.nn.sigmoid(gate_act)
    silu_gate = gate_act * sigmoid_gate
    hidden = (silu_gate * up_act * gate_sel[..., None]).astype(jnp.bfloat16)
    expert_out = jnp.einsum("ncf,ndf->ncd", hidden, down_local, preferred_element_type=jnp.float32)
    grad_hidden = jnp.einsum(
        "ncd,ndf->ncf", cot_local, down_local, preferred_element_type=jnp.float32
    )
    grad_down_local = jnp.einsum(
        "ncf,ncd->ndf", hidden, cot_local, preferred_element_type=jnp.float32
    )
    grad_sel = jnp.sum(silu_gate * up_act * grad_hidden, axis=-1)
    grad_prod = grad_hidden * gate_sel[..., None]
    grad_gate_pre = (
        grad_prod * up_act * sigmoid_gate * (1.0 + gate_act * (1.0 - sigmoid_gate))
    ).astype(jnp.bfloat16)
    grad_up_pre = (grad_prod * silu_gate).astype(jnp.bfloat16)
    grad_gate_local = jnp.einsum(
        "ncd,ncf->ndf", rows_local, grad_gate_pre, preferred_element_type=jnp.float32
    )
    grad_up_local = jnp.einsum(
        "ncd,ncf->ndf", rows_local, grad_up_pre, preferred_element_type=jnp.float32
    )
    grad_in_local = jnp.einsum(
        "ncf,ndf->ncd", grad_gate_pre, gate_local, preferred_element_type=jnp.float32
    ) + jnp.einsum("ncf,ndf->ncd", grad_up_pre, up_local, preferred_element_type=jnp.float32)
    paired = jnp.stack([grad_gate_local, grad_up_local], axis=0).reshape(
        2, local_count, model_width, tp_count, hidden_shard
    )
    sum_first = jnp.transpose(paired, (3, 0, 1, 2, 4)).reshape(
        tp_count * 2 * local_count * model_width, hidden_shard
    )
    sum_second = jnp.transpose(
        grad_down_local.reshape(local_count, model_width, tp_count, hidden_shard), (2, 0, 1, 3)
    ).reshape(tp_count * local_count * model_width, hidden_shard)
    summed_first, summed_second = (
        lax.psum_scatter(sum_first, "tp", scatter_dimension=0, tiled=True),
        lax.psum_scatter(sum_second, "tp", scatter_dimension=0, tiled=True),
    )
    pair_sums = summed_first.reshape(2, local_count, model_width, hidden_shard)
    down_sums = summed_second.reshape(local_count, model_width, hidden_shard)
    out_slots, row_slots, gate_slots, grad_gate_out, grad_up_out, down_back = (
        lax.all_to_all(expert_out, "fsdp", split_axis=1, concat_axis=0, tiled=True),
        lax.all_to_all(grad_in_local, "fsdp", split_axis=1, concat_axis=0, tiled=True),
        lax.all_to_all(grad_sel, "fsdp", split_axis=1, concat_axis=0, tiled=True),
        lax.all_to_all(pair_sums[0], "fsdp", split_axis=1, concat_axis=0, tiled=True),
        lax.all_to_all(pair_sums[1], "fsdp", split_axis=1, concat_axis=0, tiled=True),
        lax.all_to_all(down_sums, "fsdp", split_axis=1, concat_axis=0, tiled=True),
    )
    grad_down_out = jnp.transpose(down_back, (0, 2, 1))
    flat_tokens = token_mine.reshape(-1)
    moe_part = (
        jnp.zeros((row_count + 1, model_width), jnp.float32)
        .at[flat_tokens]
        .add(out_slots.reshape(-1, model_width))[:row_count]
    )
    output = (middle + moe_part).astype(jnp.bfloat16)
    grad_rows_mine = (
        jnp.zeros((row_count + 1, model_width), jnp.float32)
        .at[flat_tokens]
        .add(row_slots.reshape(-1, model_width))[:row_count]
    )
    grad_gates_mine = (
        jnp.zeros((row_count * TOP + 1,), jnp.float32)
        .at[slot_mine.reshape(-1)]
        .add(gate_slots.reshape(-1))[: row_count * TOP]
        .reshape(row_count, TOP)
    )
    grad_chosen = gate_values * (
        grad_gates_mine - jnp.sum(gate_values * grad_gates_mine, axis=-1, keepdims=True)
    )
    grad_logits = jnp.sum(grad_chosen[:, :, None] * picker, axis=1).astype(jnp.bfloat16)
    router_part = dot_left(normed_two, grad_logits)
    grad_normed_two = grad_rows_mine + dot_right(grad_logits, router_mat)
    grad_middle_norm, second_part = norm_back(middle, inverse_two, gain_two, grad_normed_two)
    grad_middle = cotangent.astype(jnp.float32) + grad_middle_norm
    grad_branch = gathered_copies(grad_middle.astype(jnp.bfloat16), "tp", 0)
    out_part = dot_left(attended, grad_branch)
    grad_attended = (
        dot_right(grad_branch, out_mat)
        .astype(jnp.bfloat16)
        .reshape(sequence_count, length_total, query_heads, HEAD_SIZE)
    )
    grad_rot_query, grad_rot_key, grad_values = attention_backward(
        queries, every_key, every_value, segments, grad_attended, log_totals
    )
    grad_query_lin = (
        rotate_back(grad_rot_query, cosine_lookup, sine_lookup)
        .reshape(group_rows, -1)
        .astype(jnp.bfloat16)
    )
    grad_key_lin = (
        rotate_back(grad_rot_key, cosine_lookup, sine_lookup)
        .reshape(group_rows, -1)
        .astype(jnp.bfloat16)
    )
    grad_value_lin = grad_values.reshape(group_rows, -1).astype(jnp.bfloat16)
    query_part = dot_left(normed_all, grad_query_lin)
    key_part = dot_left(normed_all, grad_key_lin)
    value_part = dot_left(normed_all, grad_value_lin)
    grad_normed = summed_on_arrival(
        (
            dot_right(grad_query_lin, query_mat)
            + dot_right(grad_key_lin, key_matrix)
            + dot_right(grad_value_lin, value_matrix)
        ).astype(jnp.bfloat16),
        "tp",
        0,
    )
    grad_inputs_norm, first_part = norm_back(inputs_wide, inverse_one, gain_one, grad_normed)
    grad_inputs = grad_middle + grad_inputs_norm
    first_sum, second_sum, router_sum = together((first_part, second_part, router_part), "tp")
    grad_query, grad_key, grad_value, grad_out, grad_router, grad_first, grad_second = (
        *tuple(
            (
                part.astype(jnp.float32)
                for part in in_one_piece(
                    (
                        query_part.astype(jnp.bfloat16),
                        key_part.astype(jnp.bfloat16),
                        value_part.astype(jnp.bfloat16),
                    ),
                    "fsdp",
                    0,
                    1,
                )
            )
        ),
        lax.psum_scatter(
            out_part.astype(jnp.bfloat16), "fsdp", scatter_dimension=1, tiled=True
        ).astype(jnp.float32),
        *tuple(
            (
                part.astype(jnp.float32)
                for part in sent_together_2(
                    (
                        router_sum.astype(jnp.bfloat16),
                        first_sum.astype(jnp.bfloat16),
                        second_sum.astype(jnp.bfloat16),
                    ),
                    "fsdp",
                    0,
                    1,
                )
            )
        ),
    )
    return (
        output,
        grad_inputs,
        grad_query,
        grad_key,
        grad_value,
        grad_out,
        grad_router,
        grad_first,
        grad_second,
        grad_gate_out,
        grad_up_out,
        grad_down_out,
    )


def solution(mesh):
    return jax.shard_map(
        per_device,
        mesh=mesh,
        in_specs=(
            P(("fsdp", "tp"), None),
            P("fsdp", None),
            P("fsdp", None),
            P("fsdp", "tp"),
            P("fsdp", "tp"),
            P("fsdp", "tp"),
            P("tp", "fsdp"),
            P("fsdp", None),
            P("fsdp"),
            P("fsdp"),
            P(None, "fsdp", "tp"),
            P(None, "fsdp", "tp"),
            P(None, "tp", "fsdp"),
            P(("fsdp", "tp"), None),
        ),
        out_specs=(
            P(("fsdp", "tp"), None),
            P(("fsdp", "tp"), None),
            P("fsdp", "tp"),
            P("fsdp", "tp"),
            P("fsdp", "tp"),
            P("tp", "fsdp"),
            P("fsdp", None),
            P("fsdp"),
            P("fsdp"),
            P(None, "fsdp", "tp"),
            P(None, "fsdp", "tp"),
            P(None, "tp", "fsdp"),
        ),
        check_vma=False,
    )
```

profile of v0, /device:TPU:8, one launch (start us, length us, event | category | flops | bytes accessed | tf_op | source)
XLA Modules:
  0.0 1131.6 jit_solution(13144364440288985582)
XLA Ops:
  13.9 68.9 %all-gather.4.cloned.1.call-done = bf16[1024,802]{1,0:T(8,128)(2,1)} async-done(((bf16[32,802]{1,0:T(8,128)(2,1)}), bf16[1024,802]{1,0:T(8,128)(2,1)}) %all-gather.4.cloned.1.call-update) | async-done | bytes 1642512 | tf_op jit(solution)/shard_map/all_gather | solution.py:22
  87.1 3.5 all-to-all-start
  95.0 18.5 %all-to-all-done = bf16[4,128,1024]{2,1,0:T(8,128)(2,1)S(1)} async-done(((bf16[4,128,1024]{2,1,0:T(8,128)(2,1)}), bf16[4,128,1024]{2,1,0:T(8,128)(2,1)S(1)}, u32[]{:S(2)}, u32[]{:S(2)}) %all-to-all-start) | async-done | bytes 1048608 | tf_op jit(solution)/shard_map/all_to_all | solution.py:34
  121.8 4.6 all-to-all-start.1
  128.7 9.0 reduce-window.16
  138.2 4.8 scatter_custom_fusion
  144.6 4.5 gather_fusion.2
  151.4 11.2 all-to-all-done.1
  166.7 6.9 gather_fusion.1
  174.0 4.9 gather_fusion
  178.9 4.2 reshape.861
  183.1 9.9 concatenate.90
  192.9 7.5 all-to-all-start.2
  208.5 61.8 %all-to-all-done.2 = bf16[32,33,2049]{2,1,0:T(8,128)(2,1)} async-done(((bf16[32,33,2049]{2,1,0:T(8,128)(2,1)}), bf16[32,33,2049]{2,1,0:T(8,128)(2,1)}, u32[]{:S(2)}, u32[]{:S(2)}) %all-to-all-start.2) | async-done | bytes 4327520 | tf_op jit(solution)/shard_map/all_to_all | solution.py:79
  270.3 11.3 %all-to-all-start.3 = ((bf16[32,32,1536]{2,1,0:T(8,128)(2,1)}), bf16[32,32,1536]{2,1,0:T(8,128)(2,1)}, u32[]{:S(2)}, u32[]{:S(2)}) async-start(bf16[32,32,1536]{2,1,0:T(8,128)(2,1)} %pad_maximum_fusion), calls=%async_computation.3 | async-start | bytes 6291456 | tf_op jit(solution)/shard_map/all_to_all | solution.py:70
  281.6 6.2 all_to_all.43
  289.0 33.5 %all-to-all-done.3 = bf16[32,32,1536]{2,1,0:T(8,128)(2,1)} async-done(((bf16[32,32,1536]{2,1,0:T(8,128)(2,1)}), bf16[32,32,1536]{2,1,0:T(8,128)(2,1)}, u32[]{:S(2)}, u32[]{:S(2)}) %all-to-all-start.3) | async-done | bytes 3145760 | tf_op jit(solution)/shard_map/all_to_all | solution.py:70
  322.5 3.3 fusion.32
  325.9 3.3 fusion.30
  329.2 5.1 multiply_reduce_fusion
  335.0 9.3 all-to-all-start.6
  344.4 5.0 fusion.60
  352.2 8.6 copy.227
  360.8 9.9 all-to-all-start.5
  370.7 4.6 fusion.51
  375.3 5.7 fusion.12
  382.4 8.8 scatter_custom_fusion.3
  391.4 50.1 %all-to-all-done.5 = f32[1,1056,1024]{2,0,1:T(1,128)} async-done(((f32[1,1056,1024]{2,0,1:T(1,128)}), f32[1,1056,1024]{2,0,1:T(1,128)}, u32[]{:S(2)}, u32[]{:S(2)}) %all-to-all-start.5) | async-done | bytes 4325408 | tf_op jit(solution)/shard_map/all_to_all | solution.py:440
  441.6 17.9 %scatter_custom_fusion.2 = f32[129,1024]{1,0:T(8,128)} fusion(s32[1056]{0:T(1024)S(1)} %get-tuple-element.251, f32[1,1056,1024]{2,0,1:T(1,128)} %all-to-all-done.5, f32[]{:T(128)} %constant.150.clone.1), kind=kCustom, calls=%fused_computation.8 | custom fusion | flops 1081344 | bytes 4853764 | tf_op jit(solution)/shard_map/scatter-add | solution.py:457
  462.4 9.3 all-to-all-start.7
  471.9 3.5 fusion.37
  475.5 3.2 fusion.40
  481.2 5.0 all-to-all-done.7
  488.2 4.6 fusion.7
  499.7 4.4 all-to-all-start.8
  504.5 25.7 %all-to-all-done.8 = bf16[4,128,1024]{2,1,0:T(8,128)(2,1)} async-done(((bf16[4,128,1024]{2,1,0:T(8,128)(2,1)}), bf16[4,128,1024]{2,1,0:T(8,128)(2,1)}, u32[]{:S(2)}, u32[]{:S(2)}) %all-to-all-start.8) | async-done | bytes 1048608 | tf_op jit(solution)/shard_map/all_to_all | solution.py:86
  533.1 4.4 all-to-all-start.9
  537.5 4.1 convolution_bitcast_fusion
  541.5 8.6 copy.226
  550.2 5.1 all-to-all-start.4
  567.0 49.5 %all-to-all-done.4 = f32[1,1056,1024]{2,0,1:T(1,128)} async-done(((f32[1,1056,1024]{2,0,1:T(1,128)}), f32[1,1056,1024]{2,0,1:T(1,128)}, u32[]{:S(2)}, u32[]{:S(2)}) %all-to-all-start.4) | async-done | bytes 4325408 | tf_op jit(solution)/shard_map/all_to_all | solution.py:439
  616.5 8.8 all-to-all-start.12
  625.3 17.2 %scatter_custom_fusion.1 = f32[129,1024]{1,0:T(8,128)S(1)} fusion(s32[1056]{0:T(1024)} %copy-done.57, f32[1,1056,1024]{2,0,1:T(1,128)} %all-to-all-done.4, f32[]{:T(128)} %constant.150.clone.1), kind=kCustom, calls=%fused_computation.11 | custom fusion | flops 1081344 | bytes 4854272 | tf_op jit(solution)/shard_map/scatter-add | solution.py:451
  644.9 9.8 all-to-all-start.10
  656.0 97.1 %reduce-scatter.10.cloned.1.call-done = bf16[256,32]{0,1:T(8,128)(2,1)} async-done(((bf16[256,1024]{0,1:T(8,128)(2,1)}), bf16[256,32]{0,1:T(8,128)(2,1)}) %reduce-scatter.10.cloned.1.call-update) | async-done | bytes 16400 | tf_op jit(solution)/shard_map/reduce_scatter | solution.py:525
  754.5 179.2 %reduce-scatter.18.cloned.1.call-done = bf16[32,34]{1,0:T(8,128)(2,1)} async-done(((bf16[1024,34]{1,0:T(8,128)(2,1)}), bf16[32,34]{1,0:T(8,128)(2,1)}) %reduce-scatter.18.cloned.1.call-update) | async-done | bytes 2192
  934.6 10.4 all-to-all-start.11
  947.6 168.3 %reduce-scatter.16.cloned.1.call-done = bf16[32,512]{1,0:T(8,128)(2,1)} async-done(((bf16[1024,512]{1,0:T(8,128)(2,1)}), bf16[32,512]{1,0:T(8,128)(2,1)}) %reduce-scatter.16.cloned.1.call-update) | async-done | bytes 32784
  (304 shorter events, 94.4 us)
Async XLA Ops:
  7.2 75.6 %all-gather.4.cloned.1.call-start = ((), (), s32[]{:S(2)}) async-start(), calls=%async_computation.18 | async-start | bytes 1892352 | tf_op jit(solution)/shard_map/all_gather | solution.py:22
  10.3 190.2 %all-gather.8.cloned.1.call-start = ((), (), s32[]{:S(2)}) async-start(), calls=%async_computation.20 | async-start | bytes 1310720 | tf_op jit(solution)/shard_map/all_gather | solution.py:365
  12.2 75.0 %copy-start.60 = (f32[128]{0:T(128)}, f32[128]{0:T(128)S(1)}, u32[]{:S(2)}) copy-start(f32[128]{0:T(128)S(1)} %add_rsqrt_fusion.1) | copy-start | bytes 1540
  84.8 6.2 copy-start.51
  84.8 6.4 copy-start.4
  87.1 26.4 %all-to-all-start = ((bf16[4,128,1024]{2,1,0:T(8,128)(2,1)}), bf16[4,128,1024]{2,1,0:T(8,128)(2,1)S(1)}, u32[]{:S(2)}, u32[]{:S(2)}) async-start(bf16[4,128,1024]{2,1,0:T(8,128)(2,1)} %broadcast_in_dim.138), calls=%async_computation | async-start | bytes 2097152 | tf_op jit(solution)/shard_map/all_to_all | solution.py:34
  91.0 24.7 %copy-start.20 = (f32[512,32]{0,1:T(8,128)}, f32[512,32]{0,1:T(8,128)S(1)}, u32[]{:S(2)}) copy-start(f32[512,32]{0,1:T(8,128)S(1)} %get-tuple-element.253) | copy-start | bytes 196612
  91.2 26.9 %copy-start.7 = (pred[512,512]{0,1:T(8,128)(4,1)}, pred[512,512]{0,1:T(8,128)(4,1)S(1)}, u32[]{:S(2)}) copy-start(pred[512,512]{0,1:T(8,128)(4,1)S(1)} %fusion.62) | copy-start | bytes 786436
  92.1 22.9 %copy-start.27 = (bf16[128,1024]{1,0:T(8,128)(2,1)S(1)}, bf16[128,1024]{1,0:T(8,128)(2,1)}, u32[]{:S(2)}) copy-start(bf16[128,1024]{1,0:T(8,128)(2,1)} %copy.211) | copy-start | bytes 786436
  121.8 40.9 %all-to-all-start.1 = ((f32[4,128,1024]{2,1,0:T(8,128)}), f32[4,128,1024]{2,1,0:T(8,128)}, u32[]{:S(2)}, u32[]{:S(2)}) async-start(f32[4,128,1024]{2,1,0:T(8,128)} %fusion.76), calls=%async_computation.1 | async-start | bytes 4194304 | tf_op jit(solution)/shard_map/all_to_all | solution.py:56
  126.4 17.5 %copy-start.13 = (bf16[128,1024]{1,0:T(8,128)(2,1)S(1)}, bf16[128,1024]{1,0:T(8,128)(2,1)}, u32[]{:S(2)}) copy-start(bf16[128,1024]{1,0:T(8,128)(2,1)} %param.27) | copy-start | bytes 786436
  126.4 77.3 %all-gather.6.cloned.1.call-start = ((), (), s32[]{:S(2)}) async-start(), calls=%async_computation.19 | async-start | bytes 2621440 | tf_op jit(solution)/shard_map/all_gather | solution.py:63
  151.4 13.1 %copy-start.6 = (bf16[128,1024]{1,0:T(8,128)(2,1)S(1)}, bf16[128,1024]{1,0:T(8,128)(2,1)}, u32[]{:S(2)}) copy-start(bf16[128,1024]{1,0:T(8,128)(2,1)} %param.14) | copy-start | bytes 786436
  151.4 13.3 %copy-start.42 = (f32[1024]{0:T(1024)S(1)}, f32[1024]{0:T(1024)}, u32[]{:S(2)}) copy-start(f32[1024]{0:T(1024)} %get-tuple-element.215) | copy-start | bytes 12292
  166.7 7.2 copy-start.41
  192.9 77.3 %all-to-all-start.2 = ((bf16[32,33,2049]{2,1,0:T(8,128)(2,1)}), bf16[32,33,2049]{2,1,0:T(8,128)(2,1)}, u32[]{:S(2)}, u32[]{:S(2)}) async-start(bf16[32,33,2049]{2,1,0:T(8,128)(2,1)} %concatenate.90), calls=%async_computation.2 | async-start | bytes 11141120 | tf_op jit(solution)/shard_map/all_to_all | solution.py:79
  270.3 52.3 %all-to-all-start.3 = ((bf16[32,32,1536]{2,1,0:T(8,128)(2,1)}), bf16[32,32,1536]{2,1,0:T(8,128)(2,1)}, u32[]{:S(2)}, u32[]{:S(2)}) async-start(bf16[32,32,1536]{2,1,0:T(8,128)(2,1)} %pad_maximum_fusion), calls=%async_computation.3 | async-start | bytes 6291456 | tf_op jit(solution)/shard_map/all_to_all | solution.py:70
  329.2 5.1 copy-start.18
  335.0 25.8 %all-to-all-start.6 = ((f32[1,32,33]{2,0,1:T(1,128)}), f32[1,32,33]{2,0,1:T(1,128)S(1)}, u32[]{:S(2)}, u32[]{:S(2)}) async-start(f32[1,32,33]{2,0,1:T(1,128)} %all_to_all.93), calls=%async_computation.6 | async-start | bytes 32768 | tf_op jit(solution)/shard_map/all_to_all | solution.py:441
  344.3 5.0 copy-start.17
  344.3 5.0 copy-start.19
  360.8 80.7 %all-to-all-start.5 = ((f32[1,1056,1024]{2,0,1:T(1,128)}), f32[1,1056,1024]{2,0,1:T(1,128)}, u32[]{:S(2)}, u32[]{:S(2)}) async-start(f32[1,1056,1024]{2,0,1:T(1,128)} %copy.227), calls=%async_computation.5 | async-start | bytes 8650752 | tf_op jit(solution)/shard_map/all_to_all | solution.py:440
  370.7 245.8 %reduce-scatter.14.cloned.1.call-start = ((), (), s32[]{:S(2)}) async-start(), calls=%async_computation.23 | async-start | bytes 2621440 | tf_op jit(solution)/shard_map/reduce_scatter | solution.py:434
  375.3 5.7 copy-start.44
  381.0 10.4 copy-start.54
  381.0 10.4 copy-start.56
  381.0 78.5 %copy-start.57 = (s32[1056]{0:T(1024)}, s32[1056]{0:T(1024)S(1)}, u32[]{:S(2)}) copy-start(s32[1056]{0:T(1024)S(1)} %get-tuple-element.251) | copy-start | bytes 12676
  441.6 18.0 %copy-start.59 = (f32[128]{0:T(128)S(1)}, f32[128]{0:T(128)}, u32[]{:S(2)}) copy-start(f32[128]{0:T(128)} %copy-done.58) | copy-start | bytes 1540
  441.6 19.5 %copy-start.14 = (bf16[128,1024]{1,0:T(8,128)(2,1)S(1)}, bf16[128,1024]{1,0:T(8,128)(2,1)}, u32[]{:S(2)}) copy-start(bf16[128,1024]{1,0:T(8,128)(2,1)} %param.27) | copy-start | bytes 786436
  462.4 23.8 %all-to-all-start.7 = ((bf16[4,128,1024]{2,1,0:T(8,128)(2,1)}), bf16[4,128,1024]{2,1,0:T(8,128)(2,1)}, u32[]{:S(2)}, u32[]{:S(2)}) async-start(bf16[4,128,1024]{2,1,0:T(8,128)(2,1)} %broadcast_in_dim.146), calls=%async_computation.7 | async-start | bytes 2097152 | tf_op jit(solution)/shard_map/all_to_all | solution.py:34
  471.7 170.9 %reduce-scatter.12.cloned.1.call-start = ((), (), s32[]{:S(2)}) async-start(), calls=%async_computation.22 | async-start | bytes 5242880 | tf_op jit(solution)/shard_map/reduce_scatter | solution.py:433
  481.2 6.9 copy-start.8
  481.2 6.9 copy-start.29
  481.2 6.9 copy-start.46
  499.7 32.0 %copy-start.48 = (f32[1024]{0:T(1024)S(1)}, f32[1024]{0:T(1024)}, u32[]{:S(2)}) copy-start(f32[1024]{0:T(1024)} %copy-done.47) | copy-start | bytes 12292
  499.7 32.0 %copy-start.61 = (f32[128]{0:T(128)S(1)}, f32[128]{0:T(128)}, u32[]{:S(2)}) copy-start(f32[128]{0:T(128)} %copy-done.60) | copy-start | bytes 1540
  499.7 30.6 %all-to-all-start.8 = ((bf16[4,128,1024]{2,1,0:T(8,128)(2,1)}), bf16[4,128,1024]{2,1,0:T(8,128)(2,1)}, u32[]{:S(2)}, u32[]{:S(2)}) async-start(bf16[4,128,1024]{2,1,0:T(8,128)(2,1)} %bitcast.340), calls=%async_computation.8 | async-start | bytes 2097152 | tf_op jit(solution)/shard_map/all_to_all | solution.py:86
  533.1 17.1 %all-to-all-start.9 = ((f32[4,1,34816]{2,1,0:T(1,128)}), f32[4,1,34816]{2,1,0:T(1,128)}, u32[]{:S(2)}, u32[]{:S(2)}) async-start(f32[4,1,34816]{2,1,0:T(1,128)} %broadcast_in_dim.149), calls=%async_computation.10 | async-start | bytes 1114112 | tf_op jit(solution)/shard_map/all_to_all | solution.py:34
  550.2 5.2 copy-start.26
  550.2 66.3 %all-to-all-start.4 = ((f32[1,1056,1024]{2,0,1:T(1,128)}), f32[1,1056,1024]{2,0,1:T(1,128)}, u32[]{:S(2)}, u32[]{:S(2)}) async-start(f32[1,1056,1024]{2,0,1:T(1,128)} %copy.226), calls=%async_computation.4 | async-start | bytes 8650752 | tf_op jit(solution)/shard_map/all_to_all | solution.py:439
  555.3 197.8 %reduce-scatter.10.cloned.1.call-start = ((), (), s32[]{:S(2)}) async-start(), calls=%async_computation.21 | async-start | bytes 540672 | tf_op jit(solution)/shard_map/reduce_scatter | solution.py:525
  558.0 375.7 %reduce-scatter.18.cloned.1.call-start = ((), (), s32[]{:S(2)}) async-start(), calls=%async_computation.25 | async-start | bytes 270336
  564.0 551.9 %reduce-scatter.16.cloned.1.call-start = ((), (), s32[]{:S(2)}) async-start(), calls=%async_computation.24 | async-start | bytes 1081344
  616.5 26.1 %all-to-all-start.12 = ((f32[1,1024,128]{2,0,1:T(1,128)}), f32[1,1024,128]{2,0,1:T(1,128)}, u32[]{:S(2)}, u32[]{:S(2)}) async-start(f32[1,1024,128]{2,0,1:T(1,128)} %bitcast.362), calls=%async_computation.15 | async-start | bytes 1048576 | tf_op jit(solution)/shard_map/all_to_all | solution.py:444
  642.6 12.2 %copy-start.15 = (bf16[128,1024]{1,0:T(8,128)(2,1)S(1)}, bf16[128,1024]{1,0:T(8,128)(2,1)}, u32[]{:S(2)}) copy-start(bf16[128,1024]{1,0:T(8,128)(2,1)} %param.27) | copy-start | bytes 786436
  644.9 289.7 %all-to-all-start.10 = ((f32[1,1024,128]{2,0,1:T(1,128)}), f32[1,1024,128]{2,0,1:T(1,128)}, u32[]{:S(2)}, u32[]{:S(2)}) async-start(f32[1,1024,128]{2,0,1:T(1,128)} %bitcast.349), calls=%async_computation.12 | async-start | bytes 1048576 | tf_op jit(solution)/shard_map/all_to_all | solution.py:442
  934.6 189.7 %copy-start.1 = (bf16[32,128,32]{1,2,0:T(8,128)(2,1)S(1)}, bf16[32,128,32]{1,2,0:T(8,128)(2,1)}, u32[]{:S(2)}) copy-start(bf16[32,128,32]{1,2,0:T(8,128)(2,1)} %param.26) | copy-start | bytes 786436
  934.6 185.2 %all-to-all-start.11 = ((f32[1,1024,128]{2,0,1:T(1,128)}), f32[1,1024,128]{2,0,1:T(1,128)S(1)}, u32[]{:S(2)}, u32[]{:S(2)}) async-start(f32[1,1024,128]{2,0,1:T(1,128)} %bitcast.348), calls=%async_computation.13 | async-start | bytes 1048576 | tf_op jit(solution)/shard_map/all_to_all | solution.py:443
  (35 other events, 72.5 us)
Sparse Core Ops, SparseCore 0:
  11.7 71.0 all-gather.3
  85.0 28.4 all-gather.7
  129.5 39.6 all-gather.5
  381.1 52.9 reduce-scatter.13
  481.4 55.8 reduce-scatter.11
  558.7 194.3 reduce-scatter.9
  755.6 178.0 reduce-scatter.17
  936.0 179.8 reduce-scatter.15
where the time goes:
time: 1150 us; the launch traced here: 1130 us
  waiting for transfers between devices  769 us (67%)
  local copies, waits for them, and re-layouts  102 us (9%)
  starting transfers between devices  98.8 us (9%)
  other arithmetic  83.2 us (7%)
  matrix products  62.8 us (5%)
  between operations  15.9 us (1%)
    unnamed x10, waiting for transfers between devices  348 us
    reduce_scatter x1, waiting for transfers between devices, per_device(): lax.psum_scatter(out_part.astype(jnp.bfloat16), 'fsdp', scatter_dimension...  97.1 us
    all_gather x1, waiting for transfers between devices, turned_gather(): out = lax.all_gather(both, axis, axis=0, tiled=True)  68.9 us
    all_to_all x1, waiting for transfers between devices, side_by_side_2(): lax.all_to_all(both, axis, split_axis=split_dim, concat_axis=concat_dim,...  61.8 us
    all_to_all x1, waiting for transfers between devices, per_device(): lax.all_to_all(grad_in_local, 'fsdp', split_axis=1, concat_axis=0, tiled=...  50.1 us
    all_to_all x1, waiting for transfers between devices, per_device(): lax.all_to_all(expert_out, 'fsdp', split_axis=1, concat_axis=0, tiled=True)  49.5 us
    all_to_all x1, waiting for transfers between devices, side_by_side(): lax.all_to_all(both, axis, split_axis=split_dim, concat_axis=concat_dim,...  33.5 us
    all_to_all x1, waiting for transfers between devices, summed_on_arrival(): parts = lax.all_to_all(in_blocks(shard, dim, peers), axis, 0, 0, tiled=True)  25.7 us
  transfers between devices with their start and end apart: 21, of which 12 were waited for; matrix products, arithmetic and copies ran while one was open for 19% of the time, Pallas kernels for 0%

commit v1 on v0

v1 whole, which is shorter than its diff:
```python
import math

import jax
import jax.numpy as jnp
from jax import lax
from jax.sharding import PartitionSpec as P

HEAD_SIZE = 64
EXPERTS = 32
TOP = 8


EPSILON = 1e-06
ROPE_BASE = 10000.0
MASKED = -1e30


def from_everyone(shard, axis):
    copies = jnp.broadcast_to(shard, (lax.axis_size(axis), *shard.shape))
    return lax.all_to_all(copies, axis, split_axis=0, concat_axis=0, tiled=True)


def swapped(blocks, axis):
    return lax.all_to_all(blocks, axis, split_axis=0, concat_axis=0, tiled=True)


def added_up(blocks, axis):
    return jnp.sum(swapped(blocks, axis).astype(jnp.float32), axis=0)


def dot_right(left_mat, right_mat):
    return lax.dot_general(
        left_mat, right_mat, (((1,), (1,)), ((), ())), preferred_element_type=jnp.float32
    )


def dot_left(left_mat, right_mat):
    return lax.dot_general(
        left_mat, right_mat, (((0,), (0,)), ((), ())), preferred_element_type=jnp.float32
    )


def rope_tables(seg_ids):
    length_total = seg_ids.shape[-1]
    places = jnp.arange(length_total, dtype=jnp.int32)
    starts_new = jnp.concatenate(
        [
            jnp.ones(seg_ids.shape[:-1] + (1,), dtype=jnp.bool_),
            seg_ids[..., 1:] != seg_ids[..., :-1],
        ],
        axis=-1,
    )
    doc_start = lax.cummax(jnp.where(starts_new, places, 0), axis=seg_ids.ndim - 1)
    position = (places - doc_start).astype(jnp.float32)
    halves = jnp.arange(HEAD_SIZE // 2, dtype=jnp.int32).astype(jnp.float32)
    rate_list = jnp.exp(halves * (-2.0 * math.log(ROPE_BASE) / HEAD_SIZE))
    angles = position[..., None] * rate_list
    return (jnp.cos(angles), jnp.sin(angles))


def rotary_apply(values, cosine_lookup, sine_lookup):
    half_dim = values.shape[-1] // 2
    front_half = values[..., :half_dim]
    back_half = values[..., half_dim:]
    cos_wide = cosine_lookup[..., None, :]
    sin_wide = sine_lookup[..., None, :]
    return jnp.concatenate(
        [
            front_half * cos_wide - back_half * sin_wide,
            back_half * cos_wide + front_half * sin_wide,
        ],
        axis=-1,
    )


def rotate_back(values, cosine_lookup, sine_lookup):
    half_dim = values.shape[-1] // 2
    front_half = values[..., :half_dim]
    back_half = values[..., half_dim:]
    cos_wide = cosine_lookup[..., None, :]
    sin_wide = sine_lookup[..., None, :]
    return jnp.concatenate(
        [
            front_half * cos_wide + back_half * sin_wide,
            back_half * cos_wide - front_half * sin_wide,
        ],
        axis=-1,
    )


def norm_back(values, inverse, gain_vec, grad_out):
    scaled = grad_out * gain_vec
    grad_gain = jnp.sum(grad_out * values * inverse, axis=0)
    grad_vals = inverse * scaled - values * inverse * inverse * inverse * jnp.mean(
        scaled * values, axis=-1, keepdims=True
    )
    return (grad_vals, grad_gain)


def head_scores(queries, keys, allowed):
    scores = jnp.einsum(
        "qkgd,tkd->kgqt", queries, keys, preferred_element_type=jnp.float32
    ) * HEAD_SIZE ** (-0.5)
    return jnp.where(allowed, scores, MASKED)


def slot_picker(my_routes, cap_dev):
    rows = my_routes.shape[0]
    named = (my_routes[:, :, None] == jnp.arange(EXPERTS, dtype=jnp.int32)).astype(jnp.float32)
    member = jnp.sum(named, axis=1)
    earlier = jnp.tril(jnp.ones((rows, rows), jnp.bfloat16), -1)
    slot = jnp.dot(earlier, member.astype(jnp.bfloat16), preferred_element_type=jnp.float32)
    slot = jnp.where(member > 0, slot, -1.0)
    picked = slot.T[:, None, :] == jnp.arange(cap_dev + 1, dtype=jnp.float32)[None, :, None]
    return named, picked.astype(jnp.bfloat16)


def per_device(
    inputs,
    segments,
    routes,
    query_weight,
    key_projection_weight,
    value_projection_weight,
    out_weight,
    router_weight,
    first_gain,
    second_gain,
    gate_weight,
    up_weight,
    down_weight,
    cotangent,
):
    row_count, model_width = inputs.shape
    length_total = segments.shape[1]
    my_offset = lax.axis_index("tp") * row_count
    tp_count = lax.axis_size("tp")
    fsdp_count = lax.axis_size("fsdp")
    width_shard = query_weight.shape[0]
    q_cols, k_cols, o_cols = query_weight.shape[1], key_projection_weight.shape[1], out_weight.shape[0]
    expert_count, _, hidden_shard = gate_weight.shape
    full_hidden = tp_count * hidden_shard
    cap_dev = row_count * TOP * 33 // (EXPERTS * 32)
    f32, bf16 = jnp.float32, jnp.bfloat16

    wide = q_cols + 2 * k_cols + o_cols
    packed = jnp.concatenate(
        [
            query_weight,
            key_projection_weight,
            value_projection_weight,
            out_weight.T,
            router_weight,
            first_gain[:, None],
            second_gain[:, None],
            jnp.zeros((width_shard, 128 - EXPERTS - 2), bf16),
        ],
        axis=1,
    )
    gathered = from_everyone(packed, "fsdp").reshape(model_width, -1)
    inputs_all = from_everyone(inputs, "tp").reshape(length_total, model_width)

    weight_blocks = jnp.concatenate(
        [gate_weight, up_weight, jnp.transpose(down_weight, (0, 2, 1))], axis=1
    )
    weights = from_everyone(swapped(weight_blocks, "fsdp"), "tp")
    weights = weights.reshape(tp_count, fsdp_count, 3, width_shard, hidden_shard)
    weights = jnp.transpose(weights, (2, 1, 3, 0, 4)).reshape(3, model_width, full_hidden)
    gate_mat, up_mat, down_mat = weights[0], weights[1], weights[2]

    my_routes = lax.dynamic_slice_in_dim(routes, my_offset, row_count, 0)
    named, picked = slot_picker(my_routes, cap_dev)
    cot_rows = jnp.einsum(
        "ect,td->ecd", picked[:, :cap_dev], cotangent, preferred_element_type=f32
    ).astype(bf16)
    cot_local = swapped(cot_rows, "fsdp").reshape(-1, model_width)

    qkv_mat = gathered[:, : q_cols + 2 * k_cols]
    out_mat_t = gathered[:, q_cols + 2 * k_cols : wide]
    router_mat = gathered[:, wide : wide + EXPERTS]
    gain_one = gathered[:, wide + EXPERTS].astype(f32)
    gain_two = gathered[:, wide + EXPERTS + 1].astype(f32)

    wide_all = inputs_all.astype(f32)
    inverse_all = lax.rsqrt(jnp.mean(wide_all * wide_all, axis=-1, keepdims=True) + EPSILON)
    normed_all = (wide_all * inverse_all * gain_one).astype(bf16)
    cosine, sine = rope_tables(segments[0])
    lin = jnp.dot(normed_all, qkv_mat, preferred_element_type=f32)
    query_heads, key_heads = q_cols // HEAD_SIZE, k_cols // HEAD_SIZE
    queries = rotary_apply(
        lin[:, :q_cols].reshape(length_total, query_heads, HEAD_SIZE), cosine, sine
    ).astype(bf16)
    keys = rotary_apply(
        lin[:, q_cols : q_cols + k_cols].reshape(length_total, key_heads, HEAD_SIZE), cosine, sine
    ).astype(bf16)
    values = lin[:, q_cols + k_cols :].astype(bf16).reshape(length_total, key_heads, HEAD_SIZE)
    queries = queries.reshape(length_total, key_heads, -1, HEAD_SIZE)
    place = jnp.arange(length_total, dtype=jnp.int32)
    allowed = (segments[0][:, None] == segments[0][None, :]) & (place[:, None] >= place[None, :])
    scores = head_scores(queries, keys, allowed)
    top_score = jnp.max(scores, axis=-1, keepdims=True)
    log_total = top_score + jnp.log(jnp.sum(jnp.exp(scores - top_score), axis=-1, keepdims=True))
    shares = jnp.exp(scores - log_total).astype(bf16)
    attended = (
        jnp.einsum("kgqt,tkd->qkgd", shares, values, preferred_element_type=f32)
        .reshape(length_total, q_cols)
        .astype(bf16)
    )
    branch = dot_right(attended, out_mat_t).astype(bf16)
    inputs_wide = inputs.astype(f32)
    middle = inputs_wide + added_up(branch.reshape(tp_count, row_count, model_width), "tp")
    inverse_two = lax.rsqrt(jnp.mean(middle * middle, axis=-1, keepdims=True) + EPSILON)
    normed_two = (middle * inverse_two * gain_two).astype(bf16)

    logits = jnp.dot(normed_two, router_mat, preferred_element_type=f32)
    chosen = jnp.sum(named * logits[:, None, :], axis=-1)
    gate_values = jax.nn.softmax(chosen, axis=-1)
    gates_low = gate_values.astype(bf16)
    gate_table = jnp.sum(named * gates_low.astype(f32)[:, :, None], axis=1)
    gates_mine = jnp.sum(picked[:, :cap_dev].astype(f32) * gate_table.T[:, None, :], axis=-1)

    rows_mine = jnp.einsum("ect,td->ecd", picked[:, :cap_dev], normed_two, preferred_element_type=f32).astype(bf16)
    gate_row = jnp.pad(gates_mine.astype(bf16)[:, None, :], ((0, 0), (0, 0), (0, model_width - cap_dev)))
    arrived = swapped(jnp.concatenate([rows_mine, gate_row], axis=1), "fsdp")
    rows_local = arrived[:, :cap_dev].reshape(-1, model_width)
    gate_sel = arrived[:, cap_dev, :cap_dev].astype(f32).reshape(-1, 1)

    grad_hidden = jnp.dot(cot_local, down_mat, preferred_element_type=f32)
    gate_act = jnp.dot(rows_local, gate_mat, preferred_element_type=f32)
    up_act = jnp.dot(rows_local, up_mat, preferred_element_type=f32)
    sigmoid_gate = jax.nn.sigmoid(gate_act)
    silu_gate = gate_act * sigmoid_gate
    grad_prod = grad_hidden * gate_sel
    grad_gate_pre = (
        grad_prod * up_act * sigmoid_gate * (1.0 + gate_act * (1.0 - sigmoid_gate))
    ).astype(bf16)
    grad_up_pre = (grad_prod * silu_gate).astype(bf16)
    grad_sel = jnp.sum(silu_gate * up_act * grad_hidden, axis=-1)
    grad_in = dot_right(grad_gate_pre, gate_mat) + dot_right(grad_up_pre, up_mat)
    sel_row = jnp.pad(
        grad_sel.reshape(fsdp_count, 1, cap_dev), ((0, 0), (0, 0), (0, model_width - cap_dev))
    ).astype(bf16)
    back = jnp.concatenate(
        [grad_in.astype(bf16).reshape(fsdp_count, cap_dev, model_width), sel_row], axis=1
    )
    back = swapped(back, "fsdp")
    hidden = (silu_gate * up_act * gate_sel).astype(bf16)
    expert_out = dot_right(hidden, down_mat).astype(bf16)
    out_back = swapped(expert_out.reshape(fsdp_count, cap_dev, model_width), "fsdp")

    def by_shard(left, right):
        both = dot_left(left, right).astype(bf16)
        return both.reshape(fsdp_count, width_shard, tp_count, hidden_shard)

    grads = jnp.stack(
        [
            by_shard(rows_local, grad_gate_pre),
            by_shard(rows_local, grad_up_pre),
            by_shard(cot_local, hidden),
        ],
        axis=1,
    )
    grads = jnp.transpose(grads, (3, 0, 1, 2, 4)).reshape(
        tp_count, fsdp_count, 3 * width_shard, hidden_shard
    )
    weight_grads = swapped(added_up(grads, "tp").astype(bf16), "fsdp").astype(f32)
    grad_gate_out = weight_grads[:, :width_shard]
    grad_up_out = weight_grads[:, width_shard : 2 * width_shard]
    grad_down_out = jnp.transpose(weight_grads[:, 2 * width_shard :], (0, 2, 1))

    picked_flat = picked[:, :cap_dev].reshape(-1, row_count)
    grad_rows = dot_left(picked_flat, back[:, :cap_dev].reshape(-1, model_width))
    sel_back = back[:, cap_dev, :cap_dev].astype(f32)
    gate_grad_table = jnp.sum(picked[:, :cap_dev].astype(f32) * sel_back[:, :, None], axis=1).T
    grad_gates = jnp.sum(named * gate_grad_table[:, None, :], axis=-1)
    grad_chosen = gate_values * (
        grad_gates - jnp.sum(gate_values * grad_gates, axis=-1, keepdims=True)
    )
    grad_logits = jnp.sum(grad_chosen[:, :, None] * named, axis=1).astype(bf16)
    router_part = dot_left(normed_two, grad_logits)
    grad_normed_two = grad_rows + dot_right(grad_logits, router_mat)
    grad_middle_norm, second_part = norm_back(middle, inverse_two, gain_two, grad_normed_two)
    grad_middle = cotangent.astype(f32) + grad_middle_norm
    output = (
        middle + dot_left(picked_flat, out_back.reshape(-1, model_width))
    ).astype(bf16)

    grad_branch = from_everyone(grad_middle.astype(bf16), "tp").reshape(length_total, model_width)
    out_part = dot_left(grad_branch, attended)
    grad_attended = (
        jnp.dot(grad_branch, out_mat_t, preferred_element_type=f32)
        .astype(bf16)
        .reshape(length_total, key_heads, -1, HEAD_SIZE)
    )
    whole = jnp.exp(head_scores(queries, keys, allowed) - log_total)
    grad_shares = jnp.einsum("qkgd,tkd->kgqt", grad_attended, values, preferred_element_type=f32)
    inner = jnp.sum(whole * grad_shares, axis=-1, keepdims=True)
    grad_scores = (whole * (grad_shares - inner)).astype(bf16)
    scale = HEAD_SIZE ** (-0.5)
    grad_rot_q = jnp.einsum("kgqt,tkd->qkgd", grad_scores, keys, preferred_element_type=f32) * scale
    grad_rot_k = jnp.einsum("kgqt,qkgd->tkd", grad_scores, queries, preferred_element_type=f32) * scale
    grad_values = jnp.einsum(
        "kgqt,qkgd->tkd", whole.astype(bf16), grad_attended, preferred_element_type=f32
    )
    grad_lin = jnp.concatenate(
        [
            rotate_back(
                grad_rot_q.reshape(length_total, query_heads, HEAD_SIZE), cosine, sine
            ).reshape(length_total, -1),
            rotate_back(grad_rot_k, cosine, sine).reshape(length_total, -1),
            grad_values.reshape(length_total, -1),
        ],
        axis=1,
    ).astype(bf16)
    qkv_part = dot_left(normed_all, grad_lin)
    grad_normed = added_up(
        dot_right(grad_lin, qkv_mat).astype(bf16).reshape(tp_count, row_count, model_width), "tp"
    )
    inverse_one = lax.dynamic_slice_in_dim(inverse_all, my_offset, row_count, 0)
    grad_inputs_norm, first_part = norm_back(inputs_wide, inverse_one, gain_one, grad_normed)
    grad_inputs = grad_middle + grad_inputs_norm

    token_parts = jnp.concatenate(
        [router_part, first_part[:, None], second_part[:, None]], axis=1
    )
    token_sums = jnp.sum(from_everyone(token_parts.T, "tp"), axis=0).T
    small = jnp.pad(token_sums, ((0, 0), (0, 128 - EXPERTS - 2)))
    sums_in = jnp.concatenate([qkv_part, out_part, small], axis=1).astype(bf16)
    sums = added_up(sums_in.reshape(fsdp_count, width_shard, -1), "fsdp")
    return (
        output,
        grad_inputs,
        sums[:, :q_cols],
        sums[:, q_cols : q_cols + k_cols],
        sums[:, q_cols + k_cols : q_cols + 2 * k_cols],
        sums[:, q_cols + 2 * k_cols : wide].T,
        sums[:, wide : wide + EXPERTS],
        sums[:, wide + EXPERTS],
        sums[:, wide + EXPERTS + 1],
        grad_gate_out,
        grad_up_out,
        grad_down_out,
    )


def solution(mesh):
    return jax.shard_map(
        per_device,
        mesh=mesh,
        in_specs=(
            P(("fsdp", "tp"), None),
            P("fsdp", None),
            P("fsdp", None),
            P("fsdp", "tp"),
            P("fsdp", "tp"),
            P("fsdp", "tp"),
            P("tp", "fsdp"),
            P("fsdp", None),
            P("fsdp"),
            P("fsdp"),
            P(None, "fsdp", "tp"),
            P(None, "fsdp", "tp"),
            P(None, "tp", "fsdp"),
            P(("fsdp", "tp"), None),
        ),
        out_specs=(
            P(("fsdp", "tp"), None),
            P(("fsdp", "tp"), None),
            P("fsdp", "tp"),
            P("fsdp", "tp"),
            P("fsdp", "tp"),
            P("tp", "fsdp"),
            P("fsdp", None),
            P("fsdp"),
            P("fsdp"),
            P(None, "fsdp", "tp"),
            P(None, "fsdp", "tp"),
            P(None, "tp", "fsdp"),
        ),
        check_vma=False,
    )
```

time: 1150 us -> 503 us (0.44)
  waiting for transfers between devices: 769 us -> 199 us
  blocking collectives: 0 us -> 58.5 us
  other arithmetic: 83.2 us -> 28.4 us
  local copies, waits for them, and re-layouts: 102 us -> 57.2 us
  starting transfers between devices: 98.8 us -> 76.6 us
  between operations: 15.9 us -> 2.43 us
    unnamed x10 -> x0, waiting for transfers between devices: 348 us -> none
    all_to_all x10 -> x8, waiting for transfers between devices: 232 us -> 123 us  [swapped(): return lax.all_to_all(blocks, axis, split_axis=0, concat_axis=0, tiled=True)]
    reduce_scatter x3 -> x0, waiting for transfers between devices: 97.2 us -> none  [the longest x1 97.1 us: per_device(): lax.psum_scatter(out_part.astype(jnp.bfloat16), 'fsdp', scatter_dimension...]
    all_gather x3 -> x0, waiting for transfers between devices: 68.9 us -> none  [the longest x1 68.9 us: turned_gather(): out = lax.all_gather(both, axis, axis=0, tiled=True)]
    all_to_all x0 -> x2, blocking collectives: none -> 58.5 us  [swapped(): return lax.all_to_all(blocks, axis, split_axis=0, concat_axis=0, tiled=True)]
    all_to_all x3 -> x5, waiting for transfers between devices: 23.5 us -> 75.7 us  [from_everyone(): return lax.all_to_all(copies, axis, split_axis=0, concat_axis=0, tiled=True)]
    scatter-add x3 -> x0, other arithmetic: 44 us -> none  [the longest x1 17.9 us: per_device(): grad_rows_mine = jnp.zeros((row_count + 1, model_width), jnp.float32).at[...]
    all_to_all x10 -> x8, starting transfers between devices: 81.1 us -> 50.2 us  [swapped(): return lax.all_to_all(blocks, axis, split_axis=0, concat_axis=0, tiled=True)]
  transfers between devices with their start and end apart: 21 -> 13, of which waited for: 12 -> 12; matrix products, arithmetic and copies ran while one was open for 19% -> 23% of each run, Pallas kernels for 0% -> 0%
where the time goes in v1:
time: 503 us; the launch traced here: 493 us
  waiting for transfers between devices  199 us (40%)
  starting transfers between devices  76.6 us (15%)
  matrix products  70.7 us (14%)
  blocking collectives  58.5 us (12%)
  local copies, waits for them, and re-layouts  57.2 us (11%)
  other arithmetic  28.4 us (6%)
    all_to_all x8, waiting for transfers between devices, swapped(): return lax.all_to_all(blocks, axis, split_axis=0, concat_axis=0, tiled=True)  123 us
    all_to_all x5, waiting for transfers between devices, from_everyone(): return lax.all_to_all(copies, axis, split_axis=0, concat_axis=0, tiled=True)  75.7 us
    all_to_all x2, blocking collectives, swapped(): return lax.all_to_all(blocks, axis, split_axis=0, concat_axis=0, tiled=True)  58.5 us
    all_to_all x8, starting transfers between devices, swapped(): return lax.all_to_all(blocks, axis, split_axis=0, concat_axis=0, tiled=True)  50.2 us
    all_to_all x5, starting transfers between devices, from_everyone(): return lax.all_to_all(copies, axis, split_axis=0, concat_axis=0, tiled=True)  26.5 us
    dot_general x8, matrix products, dot_left(): lax.dot_general(left_mat, right_mat, (((0,), (0,)), ((), ())), preferred_...  22 us
    dot_general x6, matrix products, dot_right(): lax.dot_general(left_mat, right_mat, (((1,), (1,)), ((), ())), preferred_...  16.3 us
  transfers between devices with their start and end apart: 13, of which 12 were waited for; matrix products, arithmetic and copies ran while one was open for 23% of the time, Pallas kernels for 0%

profile of v1, /device:TPU:8, one launch (start us, length us, event | category | flops | bytes accessed | tf_op | source)
XLA Modules:
  0.0 492.9 jit_solution(7551516305150465936)
XLA Ops:
  3.1 3.5 all-to-all-start
  6.9 14.1 %all-to-all-done = bf16[4,128,1024]{1,2,0:T(8,128)(2,1)S(1)} async-done(((bf16[4,128,1024]{1,2,0:T(8,128)(2,1)}), bf16[4,128,1024]{1,2,0:T(8,128)(2,1)S(1)}, u32[]{:S(2)}, u32[]{:S(2)}) %all-to-all-start) | async-done | bytes 1048608 | tf_op jit(solution)/shard_map/all_to_all | solution.py:20
  22.4 11.2 %all-to-all-start.1 = ((bf16[32,32,896]{2,1,0:T(8,128)(2,1)}), bf16[32,32,896]{2,1,0:T(8,128)(2,1)}, u32[]{:S(2)}, u32[]{:S(2)}) async-start(bf16[32,32,896]{2,1,0:T(8,128)(2,1)} %broadcast_in_dim.48), calls=%async_computation.1 | async-start | bytes 3670016 | tf_op jit(solution)/shard_map/all_to_all | solution.py:20
  37.4 22.7 %all-to-all-done.1 = bf16[32,32,896]{2,1,0:T(8,128)(2,1)} async-done(((bf16[32,32,896]{2,1,0:T(8,128)(2,1)}), bf16[32,32,896]{2,1,0:T(8,128)(2,1)}, u32[]{:S(2)}, u32[]{:S(2)}) %all-to-all-start.1) | async-done | bytes 1835040 | tf_op jit(solution)/shard_map/all_to_all | solution.py:20
  60.0 6.2 %all-to-all-start.4 = ((bf16[32,96,128]{2,1,0:T(8,128)(2,1)}), bf16[32,96,128]{2,1,0:T(8,128)(2,1)}, u32[]{:S(2)}, u32[]{:S(2)}) async-start(bf16[32,96,128]{2,1,0:T(8,128)(2,1)} %pad_maximum_fusion.2), calls=%async_computation.4 | async-start | bytes 1572864 | tf_op jit(solution)/shard_map/all_to_all | solution.py:24
  77.0 3.5 all-to-all-done.4
  80.5 16.9 %all_to_all.75 = bf16[4,128,1024]{2,1,0:T(8,128)(2,1)S(1)} all-to-all(bf16[4,128,1024]{2,1,0:T(8,128)(2,1)S(1)} %bitcast.202), channel_id=1, replica_groups=mesh['fsdp'=32,'tp'=4] {'tp'}, dimensions={0} | all-to-all | bytes 2097152 | tf_op jit(solution)/shard_map/all_to_all | solution.py:24
  97.4 3.4 broadcast_in_dim.55
  100.8 4.8 all-to-all-start.5
  109.4 2.4 convolution_convert_fusion.1
  111.8 30.8 %all-to-all-done.5 = bf16[4,32,96,128]{3,2,1,0:T(8,128)(2,1)} async-done(((bf16[4,32,96,128]{3,2,1,0:T(8,128)(2,1)}), bf16[4,32,96,128]{3,2,1,0:T(8,128)(2,1)}, u32[]{:S(2)}, u32[]{:S(2)}) %all-to-all-start.5) | async-done | bytes 3145760 | tf_op jit(solution)/shard_map/all_to_all | solution.py:20
  142.6 6.6 %all-to-all-start.7 = ((bf16[32,33,1024]{2,1,0:T(8,128)(2,1)}), bf16[32,33,1024]{2,1,0:T(8,128)(2,1)S(1)}, u32[]{:S(2)}, u32[]{:S(2)}) async-start(bf16[32,33,1024]{2,1,0:T(8,128)(2,1)} %convolution_convert_fusion.1), calls=%async_computation.7 | async-start | bytes 5242880 | tf_op jit(solution)/shard_map/all_to_all | solution.py:24
  153.9 29.9 %all-to-all-done.7 = bf16[32,33,1024]{2,1,0:T(8,128)(2,1)S(1)} async-done(((bf16[32,33,1024]{2,1,0:T(8,128)(2,1)}), bf16[32,33,1024]{2,1,0:T(8,128)(2,1)S(1)}, u32[]{:S(2)}, u32[]{:S(2)}) %all-to-all-start.7) | async-done | bytes 2162720 | tf_op jit(solution)/shard_map/all_to_all | solution.py:24
  185.4 8.4 %all-to-all-start.3 = ((bf16[32,34,1024]{2,1,0:T(8,128)(2,1)}), bf16[32,34,1024]{2,1,0:T(8,128)(2,1)S(1)}, u32[]{:S(2)}, u32[]{:S(2)}) async-start(bf16[32,34,1024]{2,1,0:T(8,128)(2,1)} %fusion.7), calls=%async_computation.3 | async-start | bytes 5242880 | tf_op jit(solution)/shard_map/all_to_all | solution.py:24
  193.8 2.4 fusion.99
  201.7 4.2 reshape.392
  205.9 4.5 fusion.23
  210.4 17.4 %all-to-all-done.3 = bf16[32,34,1024]{2,1,0:T(8,128)(2,1)S(1)} async-done(((bf16[32,34,1024]{2,1,0:T(8,128)(2,1)}), bf16[32,34,1024]{2,1,0:T(8,128)(2,1)S(1)}, u32[]{:S(2)}, u32[]{:S(2)}) %all-to-all-start.3) | async-done | bytes 2228256 | tf_op jit(solution)/shard_map/all_to_all | solution.py:24
  232.0 3.3 fusion.27
  235.6 3.9 multiply_convert_fusion.1
  240.3 2.6 fusion.29
  243.0 2.8 fusion.5
  245.7 2.7 reshape.393
  249.6 41.7 %all_to_all.76 = bf16[32,34,1024]{2,1,0:T(8,128)(2,1)S(1)} all-to-all(bf16[32,34,1024]{2,1,0:T(8,128)(2,1)S(1)} %fusion.8), channel_id=1, replica_groups=mesh['fsdp'=32,'tp'=4] {'fsdp'}, dimensions={0} | all-to-all | bytes 4456448 | tf_op jit(solution)/shard_map/all_to_all | solution.py:24
  296.6 3.5 all-to-all-start.9
  300.2 4.3 convolution_convert_fusion
  304.5 4.2 reshape.391
  308.6 4.4 convolution_convert_fusion.3
  314.6 5.2 %all-to-all-start.6 = ((bf16[32,33,1024]{2,1,0:T(8,128)(2,1)}), bf16[32,33,1024]{2,1,0:T(8,128)(2,1)}, u32[]{:S(2)}, u32[]{:S(2)}) async-start(bf16[32,33,1024]{2,1,0:T(8,128)(2,1)} %reshape.391), calls=%async_computation.6 | async-start | bytes 5242880 | tf_op jit(solution)/shard_map/all_to_all | solution.py:24
  322.4 6.3 %fusion.2 = (f32[2,2,512]{2,1,0:T(2,128)}, f32[2,512,512,2]{2,1,3,0:T(8,128)}) fusion(f32[2,512,512,2]{2,1,3,0:T(8,128)} %copy-done.2, f32[2,2,512]{2,1,0:T(2,128)S(1)} %copy-done.55, pred[512,512]{0,1:T(8,128)(4,1)S(1)} %fusion.33, bf16[512,2,64,1]{0,2,3,1:T(8,128)(2,1)S(1)} %bitcast.220, bf16[512,2,2,64]{0,3,2,1:T(8,128)(2,1)S(1)} %bitcast.227), kind=kOutput, calls=%fused_computation.6 | convolution fusion | flops 139458560 | bytes 9060352 | tf_op jit(solution)/shard_map/qkgd,tkd->kgqt/dot_general | solution.py:296
  330.7 4.7 fusion.4
  337.3 3.1 convolution_convert_fusion.8
  340.4 14.7 %all-to-all-done.6 = bf16[32,33,1024]{2,1,0:T(8,128)(2,1)} async-done(((bf16[32,33,1024]{2,1,0:T(8,128)(2,1)}), bf16[32,33,1024]{2,1,0:T(8,128)(2,1)}, u32[]{:S(2)}, u32[]{:S(2)}) %all-to-all-start.6) | async-done | bytes 2162720 | tf_op jit(solution)/shard_map/all_to_all | solution.py:24
  355.1 3.8 all-to-all-start.10
  358.9 4.1 convolution_convert_fusion.4
  368.1 4.4 convolution_convert_fusion.5
  377.5 4.8 all-to-all-start.13
  384.8 34.5 %all-to-all-done.13 = bf16[4,32,96,128]{3,2,1,0:T(8,128)(2,1)} async-done(((bf16[4,32,96,128]{3,2,1,0:T(8,128)(2,1)}), bf16[4,32,96,128]{3,2,1,0:T(8,128)(2,1)}, u32[]{:S(2)}, u32[]{:S(2)}) %all-to-all-start.13) | async-done | bytes 3145760 | tf_op jit(solution)/shard_map/all_to_all | solution.py:24
  420.2 3.5 all-to-all-start.11
  423.7 3.5 reduce_sum.232
  427.2 6.7 %all-to-all-done.11 = f32[4,34,1024]{2,1,0:T(8,128)S(1)} async-done(((f32[4,34,1024]{2,1,0:T(8,128)}), f32[4,34,1024]{2,1,0:T(8,128)S(1)}, u32[]{:S(2)}, u32[]{:S(2)}) %all-to-all-start.11) | async-done | bytes 557088 | tf_op jit(solution)/shard_map/all_to_all | solution.py:20
  433.9 9.0 %all-to-all-start.14 = ((bf16[32,96,128]{2,1,0:T(8,128)(2,1)}), bf16[32,96,128]{2,1,0:T(8,128)(2,1)S(1)}, u32[]{:S(2)}, u32[]{:S(2)}) async-start(bf16[32,96,128]{2,1,0:T(8,128)(2,1)} %reduce_sum.232), calls=%async_computation.14 | async-start | bytes 1572864 | tf_op jit(solution)/shard_map/all_to_all | solution.py:24
  448.0 3.0 convolution_convert_fusion.7
  451.3 2.6 pad_maximum_fusion.1
  454.0 3.7 all-to-all-done.14
  457.7 6.1 %all-to-all-start.12 = ((bf16[32,32,896]{2,1,0:T(8,128)(2,1)}), bf16[32,32,896]{2,1,0:T(8,128)(2,1)S(1)}, u32[]{:S(2)}, u32[]{:S(2)}) async-start(bf16[32,32,896]{2,1,0:T(8,128)(2,1)} %pad_maximum_fusion.1), calls=%async_computation.12 | async-start | bytes 3670016 | tf_op jit(solution)/shard_map/all_to_all | solution.py:24
  463.8 3.0 fusion.19
  470.0 19.6 %all-to-all-done.12 = bf16[32,32,896]{2,1,0:T(8,128)(2,1)S(1)} async-done(((bf16[32,32,896]{2,1,0:T(8,128)(2,1)}), bf16[32,32,896]{2,1,0:T(8,128)(2,1)S(1)}, u32[]{:S(2)}, u32[]{:S(2)}) %all-to-all-start.12) | async-done | bytes 1835040 | tf_op jit(solution)/shard_map/all_to_all | solution.py:24
  (283 shorter events, 77.9 us)
Async XLA Ops:
  0.6 105.0 %copy-start = (s32[512,8]{0,1:T(8,128)S(1)}, s32[512,8]{0,1:T(8,128)}, u32[]{:S(2)}) copy-start(s32[512,8]{0,1:T(8,128)} %param.16) | copy-start | bytes 49156
  0.7 5.9 %copy-start.82 = (bf16[32]{0:T(256)(128)(2,1)S(1)}, bf16[32]{0:T(256)(128)(2,1)}, u32[]{:S(2)}) copy-start(bf16[32]{0:T(256)(128)(2,1)} %param.22) | copy-start | bytes 196
  0.7 6.0 %copy-start.83 = (bf16[32]{0:T(256)(128)(2,1)S(1)}, bf16[32]{0:T(256)(128)(2,1)}, u32[]{:S(2)}) copy-start(bf16[32]{0:T(256)(128)(2,1)} %param.23) | copy-start | bytes 196
  0.7 6.1 %copy-start.72 = (bf16[32,32]{1,0:T(8,128)(2,1)S(1)}, bf16[32,32]{1,0:T(8,128)(2,1)}, u32[]{:S(2)}) copy-start(bf16[32,32]{1,0:T(8,128)(2,1)} %param.21) | copy-start | bytes 6148
  0.7 6.1 %copy-start.65 = (bf16[256,32]{0,1:T(8,128)(2,1)S(1)}, bf16[256,32]{0,1:T(8,128)(2,1)}, u32[]{:S(2)}) copy-start(bf16[256,32]{0,1:T(8,128)(2,1)} %param.20) | copy-start | bytes 49156
  0.7 6.1 %copy-start.71 = (bf16[32,128]{1,0:T(8,128)(2,1)S(1)}, bf16[32,128]{1,0:T(8,128)(2,1)}, u32[]{:S(2)}) copy-start(bf16[32,128]{1,0:T(8,128)(2,1)} %param.19) | copy-start | bytes 24580
  0.7 6.1 %copy-start.70 = (bf16[32,128]{1,0:T(8,128)(2,1)S(1)}, bf16[32,128]{1,0:T(8,128)(2,1)}, u32[]{:S(2)}) copy-start(bf16[32,128]{1,0:T(8,128)(2,1)} %param.18) | copy-start | bytes 24580
  0.7 6.1 %copy-start.64 = (bf16[32,256]{1,0:T(8,128)(2,1)S(1)}, bf16[32,256]{1,0:T(8,128)(2,1)}, u32[]{:S(2)}) copy-start(bf16[32,256]{1,0:T(8,128)(2,1)} %param.17) | copy-start | bytes 49156
  3.1 18.0 %all-to-all-start = ((bf16[4,128,1024]{1,2,0:T(8,128)(2,1)}), bf16[4,128,1024]{1,2,0:T(8,128)(2,1)S(1)}, u32[]{:S(2)}, u32[]{:S(2)}) async-start(bf16[4,128,1024]{1,2,0:T(8,128)(2,1)} %broadcast_in_dim.44), calls=%async_computation | async-start | bytes 2097152 | tf_op jit(solution)/shard_map/all_to_all | solution.py:20
  22.4 11.2 %copy-start.61 = (s32[1,512]{1,0:T(1,128)S(1)}, s32[1,512]{1,0:T(1,128)}, u32[]{:S(2)}) copy-start(s32[1,512]{1,0:T(1,128)} %param.15) | copy-start | bytes 6148
  22.4 11.9 %copy-start.35 = (bf16[32,128,32]{1,2,0:T(8,128)(2,1)S(1)}, bf16[32,128,32]{1,2,0:T(8,128)(2,1)}, u32[]{:S(2)}) copy-start(bf16[32,128,32]{1,2,0:T(8,128)(2,1)} %param.26) | copy-start | bytes 786436
  22.4 11.9 %copy-start.36 = (bf16[32,32,128]{2,1,0:T(8,128)(2,1)S(1)}, bf16[32,32,128]{2,1,0:T(8,128)(2,1)}, u32[]{:S(2)}) copy-start(bf16[32,32,128]{2,1,0:T(8,128)(2,1)} %param.25) | copy-start | bytes 786436
  22.4 12.0 %copy-start.37 = (bf16[32,32,128]{2,1,0:T(8,128)(2,1)S(1)}, bf16[32,32,128]{2,1,0:T(8,128)(2,1)}, u32[]{:S(2)}) copy-start(bf16[32,32,128]{2,1,0:T(8,128)(2,1)} %param.24) | copy-start | bytes 786436
  22.4 37.6 %all-to-all-start.1 = ((bf16[32,32,896]{2,1,0:T(8,128)(2,1)}), bf16[32,32,896]{2,1,0:T(8,128)(2,1)}, u32[]{:S(2)}, u32[]{:S(2)}) async-start(bf16[32,32,896]{2,1,0:T(8,128)(2,1)} %broadcast_in_dim.48), calls=%async_computation.1 | async-start | bytes 3670016 | tf_op jit(solution)/shard_map/all_to_all | solution.py:20
  60.0 20.5 %all-to-all-start.4 = ((bf16[32,96,128]{2,1,0:T(8,128)(2,1)}), bf16[32,96,128]{2,1,0:T(8,128)(2,1)}, u32[]{:S(2)}, u32[]{:S(2)}) async-start(bf16[32,96,128]{2,1,0:T(8,128)(2,1)} %pad_maximum_fusion.2), calls=%async_computation.4 | async-start | bytes 1572864 | tf_op jit(solution)/shard_map/all_to_all | solution.py:24
  75.4 25.4 %copy-start.26 = (bf16[2,64,2,512]{3,1,2,0:T(8,128)(2,1)}, bf16[2,64,2,512]{3,1,2,0:T(8,128)(2,1)S(1)}, u32[]{:S(2)}) copy-start(bf16[2,64,2,512]{3,1,2,0:T(8,128)(2,1)S(1)} %convolution_convert_fusion.11) | copy-start | bytes 786436
  100.8 5.1 %copy-start.10 = (bf16[128,1024]{1,0:T(8,128)(2,1)S(1)}, bf16[128,1024]{1,0:T(8,128)(2,1)}, u32[]{:S(2)}) copy-start(bf16[128,1024]{1,0:T(8,128)(2,1)} %param.14) | copy-start | bytes 786436
  100.8 41.8 %all-to-all-start.5 = ((bf16[4,32,96,128]{3,2,1,0:T(8,128)(2,1)}), bf16[4,32,96,128]{3,2,1,0:T(8,128)(2,1)}, u32[]{:S(2)}, u32[]{:S(2)}) async-start(bf16[4,32,96,128]{3,2,1,0:T(8,128)(2,1)} %broadcast_in_dim.55), calls=%async_computation.5 | async-start | bytes 6291456 | tf_op jit(solution)/shard_map/all_to_all | solution.py:20
  105.6 3.8 copy-start.50
  105.6 3.7 copy-start.19
  142.6 41.3 %all-to-all-start.7 = ((bf16[32,33,1024]{2,1,0:T(8,128)(2,1)}), bf16[32,33,1024]{2,1,0:T(8,128)(2,1)S(1)}, u32[]{:S(2)}, u32[]{:S(2)}) async-start(bf16[32,33,1024]{2,1,0:T(8,128)(2,1)} %convolution_convert_fusion.1), calls=%async_computation.7 | async-start | bytes 5242880 | tf_op jit(solution)/shard_map/all_to_all | solution.py:24
  185.4 42.4 %all-to-all-start.3 = ((bf16[32,34,1024]{2,1,0:T(8,128)(2,1)}), bf16[32,34,1024]{2,1,0:T(8,128)(2,1)S(1)}, u32[]{:S(2)}, u32[]{:S(2)}) async-start(bf16[32,34,1024]{2,1,0:T(8,128)(2,1)} %fusion.7), calls=%async_computation.3 | async-start | bytes 5242880 | tf_op jit(solution)/shard_map/all_to_all | solution.py:24
  249.6 42.0 %copy-start.51 = (s32[128,8]{0,1:T(8,128)S(1)}, s32[128,8]{0,1:T(8,128)}, u32[]{:S(2)}) copy-start(s32[128,8]{0,1:T(8,128)} %copy-done.50) | copy-start | bytes 12292
  249.6 42.0 %copy-start.43 = (f32[128,8]{0,1:T(8,128)S(1)}, f32[128,8]{0,1:T(8,128)}, u32[]{:S(2)}) copy-start(f32[128,8]{0,1:T(8,128)} %copy-done.42) | copy-start | bytes 12292
  249.6 42.0 %copy-start.67 = (f32[128]{0:T(128)S(1)}, f32[128]{0:T(128)}, u32[]{:S(2)}) copy-start(f32[128]{0:T(128)} %copy-done.66) | copy-start | bytes 1540
  249.6 42.0 %copy-start.69 = (f32[128]{0:T(128)S(1)}, f32[128]{0:T(128)}, u32[]{:S(2)}) copy-start(f32[128]{0:T(128)} %copy-done.68) | copy-start | bytes 1540
  296.6 18.0 %all-to-all-start.9 = ((bf16[4,128,1024]{1,2,0:T(8,128)(2,1)}), bf16[4,128,1024]{1,2,0:T(8,128)(2,1)S(1)}, u32[]{:S(2)}, u32[]{:S(2)}) async-start(bf16[4,128,1024]{1,2,0:T(8,128)(2,1)} %broadcast_in_dim.56), calls=%async_computation.9 | async-start | bytes 2097152 | tf_op jit(solution)/shard_map/all_to_all | solution.py:20
  314.6 40.5 %all-to-all-start.6 = ((bf16[32,33,1024]{2,1,0:T(8,128)(2,1)}), bf16[32,33,1024]{2,1,0:T(8,128)(2,1)}, u32[]{:S(2)}, u32[]{:S(2)}) async-start(bf16[32,33,1024]{2,1,0:T(8,128)(2,1)} %reshape.391), calls=%async_computation.6 | async-start | bytes 5242880 | tf_op jit(solution)/shard_map/all_to_all | solution.py:24
  320.4 8.2 %copy-start.14 = (bf16[4,128,1024]{2,1,0:T(8,128)(2,1)}, bf16[4,128,1024]{2,1,0:T(8,128)(2,1)S(1)}, u32[]{:S(2)}) copy-start(bf16[4,128,1024]{2,1,0:T(8,128)(2,1)S(1)} %copy.195) | copy-start | bytes 3145732
  322.3 6.3 %copy-start.3 = (f32[2,512,512,2]{2,1,3,0:T(8,128)S(1)}, f32[2,512,512,2]{2,1,3,0:T(8,128)}, u32[]{:S(2)}) copy-start(f32[2,512,512,2]{2,1,3,0:T(8,128)} %copy-done.2) | copy-start | bytes 12582916
  322.4 6.3 %copy-start.56 = (f32[2,2,512]{2,1,0:T(2,128)S(1)}, f32[2,2,512]{2,1,0:T(2,128)}, u32[]{:S(2)}) copy-start(f32[2,2,512]{2,1,0:T(2,128)} %copy-done.54) | copy-start | bytes 24580
  330.7 4.7 copy-start.31
  330.7 4.7 copy-start.33
  337.3 17.7 %copy-start.34 = (bf16[512,256]{1,0:T(8,128)(2,1)}, bf16[512,256]{1,0:T(8,128)(2,1)S(1)}, u32[]{:S(2)}) copy-start(bf16[512,256]{1,0:T(8,128)(2,1)S(1)} %copy.199) | copy-start | bytes 786436
  337.3 21.5 %copy-start.25 = (bf16[1056,512]{1,0:T(8,128)(2,1)S(1)}, bf16[1056,512]{1,0:T(8,128)(2,1)}, u32[]{:S(2)}) copy-start(bf16[1056,512]{1,0:T(8,128)(2,1)} %copy-done.24) | copy-start | bytes 3244036
  355.1 22.4 %all-to-all-start.10 = ((bf16[4,128,1024]{2,1,0:T(8,128)(2,1)}), bf16[4,128,1024]{2,1,0:T(8,128)(2,1)S(1)}, u32[]{:S(2)}, u32[]{:S(2)}) async-start(bf16[4,128,1024]{2,1,0:T(8,128)(2,1)} %bitcast.213), calls=%async_computation.10 | async-start | bytes 2097152 | tf_op jit(solution)/shard_map/all_to_all | solution.py:24
  377.5 5.4 %copy-start.18 = (bf16[128,1024]{1,0:T(8,128)(2,1)S(1)}, bf16[128,1024]{1,0:T(8,128)(2,1)}, u32[]{:S(2)}) copy-start(bf16[128,1024]{1,0:T(8,128)(2,1)} %copy-done.17) | copy-start | bytes 786436
  377.5 5.4 %copy-start.53 = (bf16[128,32]{0,1:T(8,128)(2,1)S(1)}, bf16[128,32]{0,1:T(8,128)(2,1)}, u32[]{:S(2)}) copy-start(bf16[128,32]{0,1:T(8,128)(2,1)} %copy-done.52) | copy-start | bytes 24580
  377.5 6.6 %copy-start.11 = (bf16[128,1024]{1,0:T(8,128)(2,1)S(1)}, bf16[128,1024]{1,0:T(8,128)(2,1)}, u32[]{:S(2)}) copy-start(bf16[128,1024]{1,0:T(8,128)(2,1)} %param.14) | copy-start | bytes 786436
  377.5 6.6 %copy-start.59 = (f32[1024]{0:T(1024)S(1)}, f32[1024]{0:T(1024)}, u32[]{:S(2)}) copy-start(f32[1024]{0:T(1024)} %copy-done.58) | copy-start | bytes 12292
  377.5 41.8 %all-to-all-start.13 = ((bf16[4,32,96,128]{3,2,1,0:T(8,128)(2,1)}), bf16[4,32,96,128]{3,2,1,0:T(8,128)(2,1)}, u32[]{:S(2)}, u32[]{:S(2)}) async-start(bf16[4,32,96,128]{3,2,1,0:T(8,128)(2,1)} %bitcast.197), calls=%async_computation.13 | async-start | bytes 6291456 | tf_op jit(solution)/shard_map/all_to_all | solution.py:24
  382.9 37.3 %copy-start.79 = (f32[128]{0:T(128)}, f32[128]{0:T(128)S(1)}, u32[]{:S(2)}) copy-start(f32[128]{0:T(128)S(1)} %dynamic-slice_bitcast_fusion) | copy-start | bytes 1540
  420.2 13.7 %all-to-all-start.11 = ((f32[4,34,1024]{2,1,0:T(8,128)}), f32[4,34,1024]{2,1,0:T(8,128)S(1)}, u32[]{:S(2)}, u32[]{:S(2)}) async-start(f32[4,34,1024]{2,1,0:T(8,128)} %broadcast_in_dim.107), calls=%async_computation.11 | async-start | bytes 1310720 | tf_op jit(solution)/shard_map/all_to_all | solution.py:20
  423.7 19.2 %copy-start.13 = (bf16[512,1024]{1,0:T(8,128)(2,1)S(1)}, bf16[512,1024]{1,0:T(8,128)(2,1)}, u32[]{:S(2)}) copy-start(bf16[512,1024]{1,0:T(8,128)(2,1)} %copy-done.12) | copy-start | bytes 3145732
  433.9 23.8 %all-to-all-start.14 = ((bf16[32,96,128]{2,1,0:T(8,128)(2,1)}), bf16[32,96,128]{2,1,0:T(8,128)(2,1)S(1)}, u32[]{:S(2)}, u32[]{:S(2)}) async-start(bf16[32,96,128]{2,1,0:T(8,128)(2,1)} %reduce_sum.232), calls=%async_computation.14 | async-start | bytes 1572864 | tf_op jit(solution)/shard_map/all_to_all | solution.py:24
  444.3 3.7 copy-start.46
  457.7 32.0 %all-to-all-start.12 = ((bf16[32,32,896]{2,1,0:T(8,128)(2,1)}), bf16[32,32,896]{2,1,0:T(8,128)(2,1)S(1)}, u32[]{:S(2)}, u32[]{:S(2)}) async-start(bf16[32,32,896]{2,1,0:T(8,128)(2,1)} %pad_maximum_fusion.1), calls=%async_computation.12 | async-start | bytes 3670016 | tf_op jit(solution)/shard_map/all_to_all | solution.py:24
  468.3 24.2 %copy-start.1 = (s32[512,8]{0,1:T(8,128)S(1)}, s32[512,8]{0,1:T(8,128)}, u32[]{:S(2)}) copy-start(s32[512,8]{0,1:T(8,128)} %param.16) | copy-start | bytes 49156
  (50 other events, 88.8 us)

commit v2 on v1

--- a/solution.py
+++ b/solution.py
@@ -3,6 +3,8 @@
 import jax
 import jax.numpy as jnp
 from jax import lax
+from jax.experimental import pallas as pl
+from jax.experimental.pallas import tpu as pltpu
 from jax.sharding import PartitionSpec as P
 
 HEAD_SIZE = 64
@@ -95,6 +97,339 @@
         scaled * values, axis=-1, keepdims=True
     )
     return (grad_vals, grad_gain)
+
+
+MESH = pl.DeviceIdType.MESH
+FSDP, TP, SPARE = 32, 4, 33
+F32, BF16 = jnp.float32, jnp.bfloat16
+
+
+def peer(me, k):
+    z, x, y = me // 8, (me // 4) % 2, me % 4
+    return ((z + k // 8) % 4 * 2 + (x + (k // 4) % 2) % 2) * 4 + (y + k % 4) % 4
+
+
+def giver(me, k):
+    z, x, y = me // 8, (me // 4) % 2, me % 4
+    return ((z + 4 - k // 8) % 4 * 2 + (x + (k // 4) % 2) % 2) * 4 + (y + 4 - k % 4) % 4
+
+
+def loop(low, high, step):
+    def body(k, carry):
+        step(k)
+        return carry
+
+    lax.fori_loop(low, high, body, 0)
+
+
+def greet(me, tp):
+    barrier = pltpu.get_barrier_semaphore()
+    loop(
+        1,
+        FSDP,
+        lambda k: pl.semaphore_signal(
+            barrier, inc=1, device_id={"fsdp": peer(me, k)}, device_id_type=MESH
+        ),
+    )
+    for k in range(1, TP):
+        pl.semaphore_signal(
+            barrier, inc=1, device_id={"tp": lax.rem(tp + k, TP)}, device_id_type=MESH
+        )
+    pl.semaphore_wait(barrier, FSDP - 1 + TP - 1)
+
+
+def to_fsdp(src, dst, send, recv, where):
+    return pltpu.make_async_remote_copy(
+        src_ref=src,
+        dst_ref=dst,
+        send_sem=send,
+        recv_sem=recv,
+        device_id={"fsdp": where},
+        device_id_type=MESH,
+    )
+
+
+def to_tp(src, dst, send, recv, where):
+    return pltpu.make_async_remote_copy(
+        src_ref=src,
+        dst_ref=dst,
+        send_sem=send,
+        recv_sem=recv,
+        device_id={"tp": where},
+        device_id_type=MESH,
+    )
+
+
+def nn(a, b):
+    return jnp.dot(a, b, preferred_element_type=F32)
+
+
+def nt(a, b):
+    return lax.dot_general(a, b, (((1,), (1,)), ((), ())), preferred_element_type=F32)
+
+
+def tn(a, b):
+    return lax.dot_general(a, b, (((0,), (0,)), ((), ())), preferred_element_type=F32)
+
+
+def lanes(shape):
+    return lax.broadcasted_iota(jnp.int32, shape, len(shape) - 1)
+
+
+def rows_of(shape):
+    return lax.broadcasted_iota(jnp.int32, shape, 0)
+
+
+def half_swap(v):
+    width = v.shape[-1]
+    front = lanes(v.shape) % HEAD_SIZE < HEAD_SIZE // 2
+    ahead = pltpu.roll(v, width - HEAD_SIZE // 2, 1)
+    behind = pltpu.roll(v, HEAD_SIZE // 2, 1)
+    return jnp.where(front, -ahead, behind)
+
+
+def wide_table(table, width):
+    return jnp.concatenate([table] * (width // 128), axis=1)
+
+
+def pick(slot_ref, experts, count):
+    parts = []
+    for e in experts:
+        row = slot_ref[pl.ds(e, 1), :]
+        parts.append(jnp.broadcast_to(row, (count, row.shape[1])))
+    both = jnp.concatenate(parts, axis=0)
+    want = (rows_of(both.shape) % count).astype(F32)
+    return (both == want).astype(BF16)
+
+
+def forward_kernel(
+    packed_ref, inputs_ref, seg_ref, routes_ref, blocks_ref, cot_ref,
+    middle_ref, normed_two_ref, gates_ref, slot_ref, weights_ref, cot_main_ref, cot_spare_ref,
+    packed_all_ref, heads_ref, normed_all_ref, attended_ref, cos_ref, sin_ref,
+    inputs_all, blocks_in, send_main, send_spare, branch_out, branch_in,
+    packed_send, packed_recv, blocks_send, blocks_recv, main_send, main_recv, spare_send, spare_recv,
+    inputs_send, inputs_recv, weights_send, weights_recv, branch_send, branch_recv, own_sem,
+):
+    me, tp = lax.axis_index("fsdp"), lax.axis_index("tp")
+    rows, width = inputs_ref.shape
+    total = seg_ref.shape[1]
+    greet(me, tp)
+
+    def packed_copy(k):
+        return to_fsdp(
+            packed_ref, packed_all_ref.at[me], packed_send.at[k], packed_recv.at[k], peer(me, k)
+        )
+
+    def inputs_copy(k):
+        return to_tp(
+            inputs_ref, inputs_all.at[tp], inputs_send.at[k], inputs_recv.at[k], lax.rem(tp + k, TP)
+        )
+
+    def blocks_copy(k):
+        p = peer(me, k)
+        return to_fsdp(blocks_ref.at[p], blocks_in.at[me], blocks_send.at[k], blocks_recv.at[k], p)
+
+    def main_copy(k):
+        return to_fsdp(
+            send_main.at[k], cot_main_ref.at[k], main_send.at[k], main_recv.at[k], peer(me, k)
+        )
+
+    def spare_copy(k):
+        return to_fsdp(
+            send_spare.at[k], cot_spare_ref.at[k], spare_send.at[k], spare_recv.at[k], peer(me, k)
+        )
+
+    def branch_copy(k):
+        q = lax.rem(tp + k, TP)
+        return to_tp(
+            branch_out.at[q], branch_in.at[k], branch_send.at[k], branch_recv.at[k], q
+        )
+
+    for k in (2, 1, 3):
+        inputs_copy(k).start()
+    loop(1, FSDP, lambda k: packed_copy(k).start())
+    loop(1, FSDP, lambda k: blocks_copy(k).start())
+    keep = [
+        pltpu.make_async_copy(packed_ref, packed_all_ref.at[me], own_sem.at[0]),
+        pltpu.make_async_copy(inputs_ref, inputs_all.at[tp], own_sem.at[1]),
+        pltpu.make_async_copy(blocks_ref.at[me], blocks_in.at[me], own_sem.at[2]),
+    ]
+    for copy in keep:
+        copy.start()
+
+    at = lanes((rows, 128))
+    member = jnp.zeros((rows, 128), F32)
+    for k in range(TOP):
+        member = member + (routes_ref[:, k : k + 1] == at).astype(F32)
+    earlier = (rows_of((rows, rows)) > lanes((rows, rows))).astype(BF16)
+    slot = nn(earlier, member.astype(BF16))
+    slot = jnp.where(member > 0, slot, -1.0)
+    slot_ref[...] = jnp.transpose(slot)[:EXPERTS]
+
+    def some_rows(i):
+        hot = pick(slot_ref, [peer(me, 4 * i + j) for j in range(4)], 40)
+        out = nn(hot, cot_ref[...])
+        for j in range(4):
+            send_main[4 * i + j] = out[40 * j : 40 * j + 32].astype(BF16)
+            send_spare[4 * i + j] = out[40 * j + 32 : 40 * j + 33]
+
+        def go(k):
+            main_copy(k).start()
+            spare_copy(k).start()
+
+        loop(jnp.maximum(4 * i, 1), 4 * i + 4, go)
+
+    loop(0, FSDP // 4, some_rows)
+    cot_main_ref[0] = send_main[0]
+    cot_spare_ref[0] = send_spare[0]
+
+    seg_row = jnp.broadcast_to(seg_ref[...].astype(F32), (128, total))
+    seg_col = jnp.transpose(seg_row)[:, :1]
+    same = (seg_col == seg_row[:1]) & (rows_of((total, total)) >= lanes((total, total)))
+    allowed = same.astype(F32)
+    place = jnp.sum(allowed, axis=1, keepdims=True) - 1.0
+    halves = (lanes((1, 128)) % (HEAD_SIZE // 2)).astype(F32)
+    rate = jnp.exp(halves * (-2.0 * math.log(ROPE_BASE) / HEAD_SIZE))
+    angle = place * rate
+    cos_ref[...] = jnp.cos(angle)
+    sin_ref[...] = jnp.sin(angle)
+
+    for k in range(1, TP):
+        inputs_copy(k).wait_recv()
+    keep[1].wait()
+    wide = inputs_all[...].reshape(total, width).astype(F32)
+    inverse = lax.rsqrt(jnp.mean(wide * wide, axis=-1, keepdims=True) + EPSILON)
+
+    loop(1, FSDP, lambda k: packed_copy(k).wait_recv())
+    keep[0].wait()
+    tail = jnp.transpose(packed_all_ref[:, :, 768:896].reshape(width, 128).astype(F32))
+    normed = (wide * inverse * tail[EXPERTS : EXPERTS + 1]).astype(BF16)
+    normed_all_ref[...] = normed
+    lin = nn(normed, packed_all_ref[:, :, 0:512].reshape(width, 512))
+    turn = lin[:, :384]
+    turned = turn * wide_table(cos_ref[...], 384) + half_swap(turn) * wide_table(sin_ref[...], 384)
+    heads_ref[:, :384] = turned.astype(BF16)
+    heads_ref[:, 384:] = lin[:, 384:].astype(BF16)
+    outs = []
+    for h in range(4):
+        g = h // 2
+        q = heads_ref[:, 64 * h : 64 * h + 64]
+        key = heads_ref[:, 256 + 64 * g : 320 + 64 * g]
+        value = heads_ref[:, 384 + 64 * g : 448 + 64 * g]
+        scores = jnp.where(allowed > 0, nt(q, key) * HEAD_SIZE ** (-0.5), MASKED)
+        top = jnp.max(scores, axis=1, keepdims=True)
+        grown = jnp.exp(scores - top)
+        shares = (grown * (1.0 / jnp.sum(grown, axis=1, keepdims=True))).astype(BF16)
+        outs.append(nn(shares, value))
+    attended = jnp.concatenate(outs, axis=1).astype(BF16)
+    attended_ref[...] = attended
+    branch = nt(attended, packed_all_ref[:, :, 512:768].reshape(width, 256))
+    branch_out[...] = branch.astype(BF16).reshape(TP, rows, width)
+    for k in (2, 1, 3):
+        branch_copy(k).start()
+
+    loop(1, FSDP, lambda k: blocks_copy(k).wait_recv())
+    keep[2].wait()
+    sibling = tp + 1 - 2 * lax.rem(tp, 2)
+    across = lax.rem(tp + 2, TP)
+    first = to_tp(blocks_in, weights_ref.at[tp], weights_send.at[0], weights_recv.at[0], across)
+    second = to_tp(blocks_in, weights_ref.at[tp], weights_send.at[1], weights_recv.at[1], sibling)
+    third = to_tp(
+        weights_ref.at[across], weights_ref.at[across], weights_send.at[2], weights_recv.at[2], sibling
+    )
+    first.start()
+    second.start()
+    mine = pltpu.make_async_copy(blocks_in, weights_ref.at[tp], own_sem.at[3])
+    mine.start()
+
+    for k in range(1, TP):
+        branch_copy(k).wait_recv()
+    middle = inputs_ref[...].astype(F32) + branch_out[tp].astype(F32)
+    for k in range(1, TP):
+        middle = middle + branch_in[k].astype(F32)
+    middle_ref[...] = middle
+    inverse_two = lax.rsqrt(jnp.mean(middle * middle, axis=-1, keepdims=True) + EPSILON)
+    normed_two = (middle * inverse_two * tail[EXPERTS + 1 : EXPERTS + 2]).astype(BF16)
+    normed_two_ref[...] = normed_two
+    logits = nn(normed_two, packed_all_ref[:, :, 768:896].reshape(width, 128))
+    logits = jnp.where(member > 0, logits, MASKED)
+    grown = jnp.exp(logits - jnp.max(logits, axis=1, keepdims=True)) * member
+    gates_ref[...] = grown / jnp.sum(grown, axis=1, keepdims=True)
+
+    first.wait_recv()
+    third.start()
+
+    def got(k):
+        main_copy(k).wait_recv()
+        spare_copy(k).wait_recv()
+
+    loop(1, FSDP, got)
+    second.wait_recv()
+    third.wait_recv()
+    mine.wait()
+
+    def gone(k):
+        packed_copy(k).wait_send()
+        blocks_copy(k).wait_send()
+        main_copy(k).wait_send()
+        spare_copy(k).wait_send()
+
+    loop(1, FSDP, gone)
+    for k in range(1, TP):
+        inputs_copy(k).wait_send()
+        branch_copy(k).wait_send()
+    for copy in (first, second, third):
+        copy.wait_send()
+
+
+def shape(dims, kind):
+    return jax.ShapeDtypeStruct(dims, kind)
+
+
+def dma(count):
+    return pltpu.SemaphoreType.DMA((count,))
+
+
+def forward(packed, inputs, seg, routes, blocks, cot):
+    rows, width = inputs.shape
+    total = seg.shape[1]
+    vmem = pl.BlockSpec(memory_space=pltpu.VMEM)
+    out = (
+        shape((rows, width), F32),
+        shape((rows, width), BF16),
+        shape((rows, 128), F32),
+        shape((EXPERTS, rows), F32),
+        shape((TP, *blocks.shape), BF16),
+        shape((FSDP, 32, width), BF16),
+        shape((FSDP, 1, width), F32),
+        shape((FSDP, *packed.shape), BF16),
+        shape((total, 512), BF16),
+        shape((total, width), BF16),
+        shape((total, 256), BF16),
+        shape((total, 128), F32),
+        shape((total, 128), F32),
+    )
+    return pl.pallas_call(
+        forward_kernel,
+        out_shape=out,
+        in_specs=[vmem] * 6,
+        out_specs=[vmem] * len(out),
+        scratch_shapes=[
+            pltpu.VMEM((TP, rows, width), BF16),
+            pltpu.VMEM(blocks.shape, BF16),
+            pltpu.VMEM((FSDP, 32, width), BF16),
+            pltpu.VMEM((FSDP, 1, width), F32),
+            pltpu.VMEM((TP, rows, width), BF16),
+            pltpu.VMEM((TP, rows, width), BF16),
+            *[dma(FSDP)] * 8,
+            *[dma(TP)] * 6,
+            dma(4),
+        ],
+        compiler_params=pltpu.CompilerParams(
+            collective_id=1, has_side_effects=True, vmem_limit_bytes=56 * 2**20
+        ),
+        name="attention_forward",
+    )(packed, inputs, seg, routes, blocks, cot)
 
 
 def head_scores(queries, keys, allowed):
@@ -157,68 +492,48 @@
         ],
         axis=1,
     )
-    gathered = from_everyone(packed, "fsdp").reshape(model_width, -1)
-    inputs_all = from_everyone(inputs, "tp").reshape(length_total, model_width)
-
     weight_blocks = jnp.concatenate(
         [gate_weight, up_weight, jnp.transpose(down_weight, (0, 2, 1))], axis=1
     )
-    weights = from_everyone(swapped(weight_blocks, "fsdp"), "tp")
+    my_routes = lax.dynamic_slice_in_dim(routes, my_offset, row_count, 0)
+    (
+        middle, normed_two, gates, slot, weights, cot_main, cot_spare,
+        packed_all, heads, normed_all, attended, cos_wide, sin_wide,
+    ) = forward(packed, inputs, segments, my_routes, weight_blocks, cotangent)
     weights = weights.reshape(tp_count, fsdp_count, 3, width_shard, hidden_shard)
     weights = jnp.transpose(weights, (2, 1, 3, 0, 4)).reshape(3, model_width, full_hidden)
     gate_mat, up_mat, down_mat = weights[0], weights[1], weights[2]
-
-    my_routes = lax.dynamic_slice_in_dim(routes, my_offset, row_count, 0)
-    named, picked = slot_picker(my_routes, cap_dev)
-    cot_rows = jnp.einsum(
-        "ect,td->ecd", picked[:, :cap_dev], cotangent, preferred_element_type=f32
-    ).astype(bf16)
-    cot_local = swapped(cot_rows, "fsdp").reshape(-1, model_width)
-
+    me = lax.axis_index("fsdp")
+    offs = jnp.arange(FSDP, dtype=jnp.int32)
+    peers = peer(me, offs)
+    givers = giver(me, offs)
+    back_of = jnp.zeros((FSDP,), jnp.int32).at[givers].set(offs)
+    cot_main, cot_spare = cot_main[back_of], cot_spare[back_of]
+    cot_local = jnp.concatenate([cot_main, cot_spare.astype(bf16)], axis=1).reshape(-1, model_width)
+    gathered = packed_all.reshape(model_width, -1)
     qkv_mat = gathered[:, : q_cols + 2 * k_cols]
     out_mat_t = gathered[:, q_cols + 2 * k_cols : wide]
     router_mat = gathered[:, wide : wide + EXPERTS]
     gain_one = gathered[:, wide + EXPERTS].astype(f32)
     gain_two = gathered[:, wide + EXPERTS + 1].astype(f32)
-
-    wide_all = inputs_all.astype(f32)
-    inverse_all = lax.rsqrt(jnp.mean(wide_all * wide_all, axis=-1, keepdims=True) + EPSILON)
-    normed_all = (wide_all * inverse_all * gain_one).astype(bf16)
-    cosine, sine = rope_tables(segments[0])
-    lin = jnp.dot(normed_all, qkv_mat, preferred_element_type=f32)
     query_heads, key_heads = q_cols // HEAD_SIZE, k_cols // HEAD_SIZE
-    queries = rotary_apply(
-        lin[:, :q_cols].reshape(length_total, query_heads, HEAD_SIZE), cosine, sine
-    ).astype(bf16)
-    keys = rotary_apply(
-        lin[:, q_cols : q_cols + k_cols].reshape(length_total, key_heads, HEAD_SIZE), cosine, sine
-    ).astype(bf16)
-    values = lin[:, q_cols + k_cols :].astype(bf16).reshape(length_total, key_heads, HEAD_SIZE)
-    queries = queries.reshape(length_total, key_heads, -1, HEAD_SIZE)
+    queries = heads[:, :q_cols].reshape(length_total, key_heads, -1, HEAD_SIZE)
+    keys = heads[:, q_cols : q_cols + k_cols].reshape(length_total, key_heads, HEAD_SIZE)
+    values = heads[:, q_cols + k_cols :].reshape(length_total, key_heads, HEAD_SIZE)
+    cosine, sine = cos_wide[:, :32], sin_wide[:, :32]
     place = jnp.arange(length_total, dtype=jnp.int32)
     allowed = (segments[0][:, None] == segments[0][None, :]) & (place[:, None] >= place[None, :])
     scores = head_scores(queries, keys, allowed)
     top_score = jnp.max(scores, axis=-1, keepdims=True)
     log_total = top_score + jnp.log(jnp.sum(jnp.exp(scores - top_score), axis=-1, keepdims=True))
-    shares = jnp.exp(scores - log_total).astype(bf16)
-    attended = (
-        jnp.einsum("kgqt,tkd->qkgd", shares, values, preferred_element_type=f32)
-        .reshape(length_total, q_cols)
-        .astype(bf16)
-    )
-    branch = dot_right(attended, out_mat_t).astype(bf16)
     inputs_wide = inputs.astype(f32)
-    middle = inputs_wide + added_up(branch.reshape(tp_count, row_count, model_width), "tp")
+    inverse_one = lax.rsqrt(jnp.mean(inputs_wide * inputs_wide, axis=-1, keepdims=True) + EPSILON)
     inverse_two = lax.rsqrt(jnp.mean(middle * middle, axis=-1, keepdims=True) + EPSILON)
-    normed_two = (middle * inverse_two * gain_two).astype(bf16)
-
-    logits = jnp.dot(normed_two, router_mat, preferred_element_type=f32)
-    chosen = jnp.sum(named * logits[:, None, :], axis=-1)
-    gate_values = jax.nn.softmax(chosen, axis=-1)
-    gates_low = gate_values.astype(bf16)
-    gate_table = jnp.sum(named * gates_low.astype(f32)[:, :, None], axis=1)
+    named = (my_routes[:, :, None] == jnp.arange(EXPERTS, dtype=jnp.int32)).astype(f32)
+    gate_values = jnp.sum(named * gates[:, None, :EXPERTS], axis=-1)
+    gate_table = gates[:, :EXPERTS].astype(bf16).astype(f32)
+    picked = (slot[:, None, :] == jnp.arange(cap_dev + 1, dtype=f32)[None, :, None]).astype(bf16)
     gates_mine = jnp.sum(picked[:, :cap_dev].astype(f32) * gate_table.T[:, None, :], axis=-1)
-
     rows_mine = jnp.einsum("ect,td->ecd", picked[:, :cap_dev], normed_two, preferred_element_type=f32).astype(bf16)
     gate_row = jnp.pad(gates_mine.astype(bf16)[:, None, :], ((0, 0), (0, 0), (0, model_width - cap_dev)))
     arrived = swapped(jnp.concatenate([rows_mine, gate_row], axis=1), "fsdp")
@@ -316,7 +631,6 @@
     grad_normed = added_up(
         dot_right(grad_lin, qkv_mat).astype(bf16).reshape(tp_count, row_count, model_width), "tp"
     )
-    inverse_one = lax.dynamic_slice_in_dim(inverse_all, my_offset, row_count, 0)
     grad_inputs_norm, first_part = norm_back(inputs_wide, inverse_one, gain_one, grad_normed)
     grad_inputs = grad_middle + grad_inputs_norm
 

time: 503 us -> 460 us (0.915)
  Pallas kernels: 0 us -> 110 us
  waiting for transfers between devices: 199 us -> 111 us
  blocking collectives: 58.5 us -> 0 us
  local copies, waits for them, and re-layouts: 57.2 us -> 78.5 us
  starting transfers between devices: 76.6 us -> 58.9 us
  matrix products: 70.7 us -> 54.8 us
  other arithmetic: 28.4 us -> 35.5 us
    pallas_call x0 -> x1, Pallas kernels: none -> 110 us  [forward(): pl.pallas_call(forward_kernel, out_shape=out, in_specs=[vmem] * 6, out_sp...]
    all_to_all x5 -> x2, waiting for transfers between devices: 75.7 us -> 6.84 us  [from_everyone(): return lax.all_to_all(copies, axis, split_axis=0, concat_axis=0, tiled=True)]
    all_to_all x2 -> x0, blocking collectives: 58.5 us -> none  [swapped(): return lax.all_to_all(blocks, axis, split_axis=0, concat_axis=0, tiled=True)]
    all_to_all x8 -> x7, waiting for transfers between devices: 123 us -> 105 us  [swapped(): return lax.all_to_all(blocks, axis, split_axis=0, concat_axis=0, tiled=True)]
    all_to_all x5 -> x2, starting transfers between devices: 26.5 us -> 8.11 us  [from_everyone(): return lax.all_to_all(copies, axis, split_axis=0, concat_axis=0, tiled=True)]
    slice x4 -> x8, local copies, waits for them, and re-layouts: 0.15 us -> 8.04 us  [the longest x2 3.32 us: per_device(): heads[:, q_cols + k_cols:].reshape(length_total, key_heads, HEAD_SIZE)]
    dot_general x5 -> x0, matrix products: 7.44 us -> none  [the longest x1 2.43 us: per_device(): jnp.einsum('ect,td->ecd', picked[:, :cap_dev], cotangent, preferred_eleme...]
    another operation x6, local copies, waits for them, and re-layouts: 6.61 us -> 12.8 us  [per_device(): jnp.stack([by_shard(rows_local, grad_gate_pre), by_shard(rows_local, grad...]
  transfers between devices with their start and end apart: 13 -> 9, of which waited for: 12 -> 7; matrix products, arithmetic and copies ran while one was open for 23% -> 26% of each run, Pallas kernels for 0% -> 0%
where the time goes in v2:
time: 460 us; the launch traced here: 451 us
  waiting for transfers between devices  111 us (24%)
  Pallas kernels  110 us (24%)
  local copies, waits for them, and re-layouts  78.5 us (17%)
  starting transfers between devices  58.9 us (13%)
  matrix products  54.8 us (12%)
  other arithmetic  35.5 us (8%)
    pallas_call x1, Pallas kernels, forward(): pl.pallas_call(forward_kernel, out_shape=out, in_specs=[vmem] * 6, out_sp...  110 us
    all_to_all x7, waiting for transfers between devices, swapped(): return lax.all_to_all(blocks, axis, split_axis=0, concat_axis=0, tiled=True)  105 us
    all_to_all x7, starting transfers between devices, swapped(): return lax.all_to_all(blocks, axis, split_axis=0, concat_axis=0, tiled=True)  50.8 us
    dot_general x8, matrix products, dot_left(): lax.dot_general(left_mat, right_mat, (((0,), (0,)), ((), ())), preferred_...  21.7 us
    dot_general x5, matrix products, dot_right(): lax.dot_general(left_mat, right_mat, (((1,), (1,)), ((), ())), preferred_...  13.3 us
    another operation x6, local copies, waits for them, and re-layouts, per_device(): jnp.stack([by_shard(rows_local, grad_gate_pre), by_shard(rows_local, grad...  12.8 us
    unnamed x115, local copies, waits for them, and re-layouts  12.7 us
  transfers between devices with their start and end apart: 9, of which 7 were waited for; matrix products, arithmetic and copies ran while one was open for 26% of the time, Pallas kernels for 0%

profile of v2, /device:TPU:8, one launch (start us, length us, event | category | flops | bytes accessed | tf_op | source)
XLA Modules:
  0.0 451.3 jit_solution(2729911596133077225)
XLA Ops:
  2.9 2.1 pad_maximum_fusion.3.blocks_ref
  6.4 110.3 %attention_forward.1 = (f32[128,1024]{1,0:T(8,128)}, bf16[128,1024]{1,0:T(8,128)(2,1)}, f32[128,128]{1,0:T(8,128)}, f32[32,128]{1,0:T(8,128)}, bf16[4,32,96,128]...) custom-call(bf16[32,896]{1,0:T(8,128)(2,1)} %concatenate.39.packed_r, ...), custom_call_target="tpu_custom_call" | custom-call | tf_op jit(solution)/shard_map/attention_forward/pallas_call | solution.py:412
  122.4 7.5 %all-to-all-start = ((bf16[32,34,1024]{2,1,0:T(8,128)(2,1)}), bf16[32,34,1024]{2,1,0:T(8,128)(2,1)}, u32[]{:S(2)}, u32[]{:S(2)}) async-start(bf16[32,34,1024]{2,1,0:T(8,128)(2,1)} %fusion.7), calls=%async_computation | async-start | bytes 5242880 | tf_op jit(solution)/shard_map/all_to_all | solution.py:26
  130.0 6.0 %copy.253 = bf16[4,32,3,32,128]{4,0,3,1,2:T(4,128)(2,1)S(1)} copy(bf16[4,32,3,32,128]{4,3,2,1,0:T(8,128)(2,1)} %bitcast.186) | data formatting | bytes 6291456 | tf_op jit(solution)/shard_map/reshape | solution.py:503
  137.4 3.6 gather_fusion
  141.1 3.5 pad_maximum_fusion.1
  144.6 4.2 reshape.445
  148.9 3.2 fusion.95
  153.0 2.6 fusion.29
  155.7 10.8 %all-to-all-done = bf16[32,34,1024]{2,1,0:T(8,128)(2,1)} async-done(((bf16[32,34,1024]{2,1,0:T(8,128)(2,1)}), bf16[32,34,1024]{2,1,0:T(8,128)(2,1)}, u32[]{:S(2)}, u32[]{:S(2)}) %all-to-all-start) | async-done | bytes 2228256 | tf_op jit(solution)/shard_map/all_to_all | solution.py:26
  167.5 2.9 reshape.442
  173.1 4.0 multiply_convert_fusion.1
  177.3 3.0 fusion.35
  180.2 2.7 fusion.5
  182.9 2.7 reshape.446
  187.6 8.7 %all-to-all-start.2 = ((bf16[32,34,1024]{2,1,0:T(8,128)(2,1)}), bf16[32,34,1024]{2,1,0:T(8,128)(2,1)S(1)}, u32[]{:S(2)}, u32[]{:S(2)}) async-start(bf16[32,34,1024]{2,1,0:T(8,128)(2,1)} %fusion.8), calls=%async_computation.2 | async-start | bytes 5242880 | tf_op jit(solution)/shard_map/all_to_all | solution.py:26
  200.6 2.3 slice_convert_fusion
  210.3 21.0 %all-to-all-done.2 = bf16[32,34,1024]{2,1,0:T(8,128)(2,1)S(1)} async-done(((bf16[32,34,1024]{2,1,0:T(8,128)(2,1)}), bf16[32,34,1024]{2,1,0:T(8,128)(2,1)S(1)}, u32[]{:S(2)}, u32[]{:S(2)}) %all-to-all-start.2) | async-done | bytes 2228256 | tf_op jit(solution)/shard_map/all_to_all | solution.py:26
  236.5 3.9 all-to-all-start.3
  244.9 4.0 convolution_convert_fusion
  248.9 4.2 reshape.444
  253.0 4.4 convolution_convert_fusion.2
  258.5 7.9 %all-to-all-start.1 = ((bf16[32,33,1024]{2,1,0:T(8,128)(2,1)}), bf16[32,33,1024]{2,1,0:T(8,128)(2,1)S(1)}, u32[]{:S(2)}, u32[]{:S(2)}) async-start(bf16[32,33,1024]{2,1,0:T(8,128)(2,1)} %reshape.444), calls=%async_computation.1 | async-start | bytes 5242880 | tf_op jit(solution)/shard_map/all_to_all | solution.py:26
  266.4 2.3 copy.192
  270.6 3.8 fusion.2
  280.9 21.3 %all-to-all-done.1 = bf16[32,33,1024]{2,1,0:T(8,128)(2,1)S(1)} async-done(((bf16[32,33,1024]{2,1,0:T(8,128)(2,1)}), bf16[32,33,1024]{2,1,0:T(8,128)(2,1)S(1)}, u32[]{:S(2)}, u32[]{:S(2)}) %all-to-all-start.1) | async-done | bytes 2162720 | tf_op jit(solution)/shard_map/all_to_all | solution.py:26
  302.2 4.3 all-to-all-start.4
  306.5 4.4 convolution_convert_fusion.3
  310.9 2.2 stack_reshape.11
  313.1 2.4 copy.206
  315.5 2.1 stack_reshape.10
  317.6 2.3 copy.205
  319.9 4.4 convolution_convert_fusion.4
  324.4 2.2 stack_reshape.9
  328.4 2.0 pad_maximum_fusion
  330.4 4.8 %all-to-all-start.7 = ((bf16[4,32,96,128]{3,2,1,0:T(8,128)(2,1)}), bf16[4,32,96,128]{3,2,1,0:T(8,128)(2,1)}, u32[]{:S(2)}, u32[]{:S(2)}) async-start(bf16[4,32,96,128]{3,2,1,0:T(8,128)(2,1)} %bitcast.179), calls=%async_computation.7 | async-start | bytes 6291456 | tf_op jit(solution)/shard_map/all_to_all | solution.py:26
  341.4 30.8 %all-to-all-done.7 = bf16[4,32,96,128]{3,2,1,0:T(8,128)(2,1)} async-done(((bf16[4,32,96,128]{3,2,1,0:T(8,128)(2,1)}), bf16[4,32,96,128]{3,2,1,0:T(8,128)(2,1)}, u32[]{:S(2)}, u32[]{:S(2)}) %all-to-all-start.7) | async-done | bytes 3145760 | tf_op jit(solution)/shard_map/all_to_all | solution.py:26
  374.1 4.2 all-to-all-start.5
  378.3 3.5 reduce_sum.192
  381.7 6.8 %all-to-all-done.5 = f32[4,34,1024]{2,1,0:T(8,128)} async-done(((f32[4,34,1024]{2,1,0:T(8,128)}), f32[4,34,1024]{2,1,0:T(8,128)}, u32[]{:S(2)}, u32[]{:S(2)}) %all-to-all-start.5) | async-done | bytes 557088 | tf_op jit(solution)/shard_map/all_to_all | solution.py:22
  388.6 8.7 %all-to-all-start.8 = ((bf16[32,96,128]{2,1,0:T(8,128)(2,1)}), bf16[32,96,128]{2,1,0:T(8,128)(2,1)}, u32[]{:S(2)}, u32[]{:S(2)}) async-start(bf16[32,96,128]{2,1,0:T(8,128)(2,1)} %reduce_sum.192), calls=%async_computation.8 | async-start | bytes 1572864 | tf_op jit(solution)/shard_map/all_to_all | solution.py:26
  397.3 2.3 copy.201
  399.6 2.5 convolution_convert_fusion.7
  402.1 3.1 convolution_convert_fusion.5
  408.2 2.8 pad_maximum_fusion.2
  411.9 8.9 %all-to-all-start.6 = ((bf16[32,32,896]{2,1,0:T(8,128)(2,1)}), bf16[32,32,896]{2,1,0:T(8,128)(2,1)}, u32[]{:S(2)}, u32[]{:S(2)}) async-start(bf16[32,32,896]{2,1,0:T(8,128)(2,1)} %pad_maximum_fusion.2), calls=%async_computation.6 | async-start | bytes 3670016 | tf_op jit(solution)/shard_map/all_to_all | solution.py:26
  423.6 2.3 fusion.96
  427.1 19.7 %all-to-all-done.6 = bf16[32,32,896]{2,1,0:T(8,128)(2,1)} async-done(((bf16[32,32,896]{2,1,0:T(8,128)(2,1)}), bf16[32,32,896]{2,1,0:T(8,128)(2,1)}, u32[]{:S(2)}, u32[]{:S(2)}) %all-to-all-start.6) | async-done | bytes 1835040 | tf_op jit(solution)/shard_map/all_to_all | solution.py:26
  (196 shorter events, 69.8 us)
Async XLA Ops:
  2.2 114.6 %copy-start.38 = (s32[128,8]{0,1:T(8,128)}, s32[128,8]{0,1:T(8,128)S(1)}, u32[]{:S(2)}) copy-start(s32[128,8]{0,1:T(8,128)S(1)} %constant_dynamic-slice_fusion) | copy-start | bytes 12292
  122.4 44.0 %all-to-all-start = ((bf16[32,34,1024]{2,1,0:T(8,128)(2,1)}), bf16[32,34,1024]{2,1,0:T(8,128)(2,1)}, u32[]{:S(2)}, u32[]{:S(2)}) async-start(bf16[32,34,1024]{2,1,0:T(8,128)(2,1)} %fusion.7), calls=%async_computation | async-start | bytes 5242880 | tf_op jit(solution)/shard_map/all_to_all | solution.py:26
  130.0 6.0 %copy-start.29 = (f32[32,1,1024]{2,1,0:T(1,128)S(1)}, f32[32,1,1024]{2,1,0:T(1,128)}, u32[]{:S(2)}) copy-start(f32[32,1,1024]{2,1,0:T(1,128)} %get-tuple-element.31) | copy-start | bytes 393220
  148.9 4.2 copy-start.17
  167.5 2.9 copy-start.10
  170.4 2.0 copy-start.22
  170.4 2.7 copy-start.54
  177.3 3.0 copy-start.18
  187.6 8.7 %copy-start.28 = (f32[128,128]{1,0:T(8,128)S(1)}, f32[128,128]{1,0:T(8,128)}, u32[]{:S(2)}) copy-start(f32[128,128]{1,0:T(8,128)} %get-tuple-element.28) | copy-start | bytes 196612
  187.6 43.8 %all-to-all-start.2 = ((bf16[32,34,1024]{2,1,0:T(8,128)(2,1)}), bf16[32,34,1024]{2,1,0:T(8,128)(2,1)S(1)}, u32[]{:S(2)}, u32[]{:S(2)}) async-start(bf16[32,34,1024]{2,1,0:T(8,128)(2,1)} %fusion.8), calls=%async_computation.2 | async-start | bytes 5242880 | tf_op jit(solution)/shard_map/all_to_all | solution.py:26
  196.3 8.4 %copy-start.4 = (f32[128,1024]{1,0:T(8,128)S(1)}, f32[128,1024]{1,0:T(8,128)}, u32[]{:S(2)}) copy-start(f32[128,1024]{1,0:T(8,128)} %get-tuple-element.25) | copy-start | bytes 1572868
  197.0 8.3 %copy-start.44 = (s32[1,512]{1,0:T(1,128)S(1)}, s32[1,512]{1,0:T(1,128)}, u32[]{:S(2)}) copy-start(s32[1,512]{1,0:T(1,128)} %seg_ref.1) | copy-start | bytes 6148
  200.6 6.8 %copy-start.23 = (bf16[512,128]{0,1:T(8,128)(2,1)}, bf16[512,128]{0,1:T(8,128)(2,1)S(1)}, u32[]{:S(2)}) copy-start(bf16[512,128]{0,1:T(8,128)(2,1)S(1)} %copy.188) | copy-start | bytes 393220
  209.4 22.0 %copy-start.26 = (f32[32,128]{1,0:T(8,128)S(1)}, f32[32,128]{1,0:T(8,128)}, u32[]{:S(2)}) copy-start(f32[32,128]{1,0:T(8,128)} %get-tuple-element.26) | copy-start | bytes 49156
  209.4 22.3 %copy-start.37 = (f32[128,32]{0,1:T(8,128)S(1)}, f32[128,32]{0,1:T(8,128)}, u32[]{:S(2)}) copy-start(f32[128,32]{0,1:T(8,128)} %copy.186) | copy-start | bytes 49156
  209.4 22.3 %copy-start.39 = (s32[128,8]{0,1:T(8,128)S(1)}, s32[128,8]{0,1:T(8,128)}, u32[]{:S(2)}) copy-start(s32[128,8]{0,1:T(8,128)} %copy-done.38) | copy-start | bytes 12292
  210.3 22.1 %copy-start.35 = (f32[1024,1]{0,1:T(1,128)S(1)}, f32[1024,1]{0,1:T(1,128)}, u32[]{:S(2)}) copy-start(f32[1024,1]{0,1:T(1,128)} %copy.223) | copy-start | bytes 12292
  210.3 22.1 %copy-start.46 = (f32[128]{0:T(128)S(1)}, f32[128]{0:T(128)}, u32[]{:S(2)}) copy-start(f32[128]{0:T(128)} %add_rsqrt_fusion.1) | copy-start | bytes 1540
  231.8 2.6 copy-start.32
  231.8 3.2 copy-start.14
  234.4 2.2 copy-start.7
  235.2 5.2 %copy-start.43 = (f32[2,2,512]{2,1,0:T(2,128)S(1)}, f32[2,2,512]{2,1,0:T(2,128)}, u32[]{:S(2)}) copy-start(f32[2,2,512]{2,1,0:T(2,128)} %copy-done.42) | copy-start | bytes 24580
  235.4 9.4 %copy-start.21 = (bf16[1,32,32,4,128]{4,3,2,1,0:T(4,128)(2,1)S(1)}, bf16[1,32,32,4,128]{4,3,2,1,0:T(4,128)(2,1)}, u32[]{:S(2)}) copy-start(bf16[1,32,32,4,128]{4,3,2,1,0:T(4,128)(2,1)} %copy-done.20) | copy-start | bytes 3145732
  236.5 20.9 %all-to-all-start.3 = ((bf16[4,128,1024]{1,2,0:T(8,128)(2,1)}), bf16[4,128,1024]{1,2,0:T(8,128)(2,1)S(1)}, u32[]{:S(2)}, u32[]{:S(2)}) async-start(bf16[4,128,1024]{1,2,0:T(8,128)(2,1)} %broadcast_in_dim.32), calls=%async_computation.3 | async-start | bytes 2097152 | tf_op jit(solution)/shard_map/all_to_all | solution.py:22
  258.5 43.7 %all-to-all-start.1 = ((bf16[32,33,1024]{2,1,0:T(8,128)(2,1)}), bf16[32,33,1024]{2,1,0:T(8,128)(2,1)S(1)}, u32[]{:S(2)}, u32[]{:S(2)}) async-start(bf16[32,33,1024]{2,1,0:T(8,128)(2,1)} %reshape.444), calls=%async_computation.1 | async-start | bytes 5242880 | tf_op jit(solution)/shard_map/all_to_all | solution.py:26
  270.5 3.9 copy-start.3
  270.6 3.9 copy-start.34
  302.2 28.2 %all-to-all-start.4 = ((bf16[4,128,1024]{2,1,0:T(8,128)(2,1)}), bf16[4,128,1024]{2,1,0:T(8,128)(2,1)}, u32[]{:S(2)}, u32[]{:S(2)}) async-start(bf16[4,128,1024]{2,1,0:T(8,128)(2,1)} %bitcast.192), calls=%async_computation.4 | async-start | bytes 2097152 | tf_op jit(solution)/shard_map/all_to_all | solution.py:26
  330.4 6.0 %copy-start.11 = (bf16[128,1024]{1,0:T(8,128)(2,1)S(1)}, bf16[128,1024]{1,0:T(8,128)(2,1)}, u32[]{:S(2)}) copy-start(bf16[128,1024]{1,0:T(8,128)(2,1)} %inputs_ref.1) | copy-start | bytes 786436
  330.4 6.2 %copy-start.33 = (bf16[128,32]{0,1:T(8,128)(2,1)S(1)}, bf16[128,32]{0,1:T(8,128)(2,1)}, u32[]{:S(2)}) copy-start(bf16[128,32]{0,1:T(8,128)(2,1)} %copy-done.32) | copy-start | bytes 24580
  330.4 41.8 %all-to-all-start.7 = ((bf16[4,32,96,128]{3,2,1,0:T(8,128)(2,1)}), bf16[4,32,96,128]{3,2,1,0:T(8,128)(2,1)}, u32[]{:S(2)}, u32[]{:S(2)}) async-start(bf16[4,32,96,128]{3,2,1,0:T(8,128)(2,1)} %bitcast.179), calls=%async_computation.7 | async-start | bytes 6291456 | tf_op jit(solution)/shard_map/all_to_all | solution.py:26
  335.2 5.5 %copy-start.45 = (f32[1024]{0:T(1024)S(1)}, f32[1024]{0:T(1024)}, u32[]{:S(2)}) copy-start(f32[1024]{0:T(1024)} %get-tuple-element.38) | copy-start | bytes 12292
  336.5 37.6 %copy-start.40 = (f32[1024,1]{0,1:T(1,128)}, f32[1024,1]{0,1:T(1,128)S(1)}, u32[]{:S(2)}) copy-start(f32[1024,1]{0,1:T(1,128)S(1)} %copy.224) | copy-start | bytes 12292
  336.6 4.1 copy-start.50
  374.1 14.5 %all-to-all-start.5 = ((f32[4,34,1024]{2,1,0:T(8,128)}), f32[4,34,1024]{2,1,0:T(8,128)}, u32[]{:S(2)}, u32[]{:S(2)}) async-start(f32[4,34,1024]{2,1,0:T(8,128)} %broadcast_in_dim.35), calls=%async_computation.5 | async-start | bytes 1310720 | tf_op jit(solution)/shard_map/all_to_all | solution.py:22
  388.6 23.4 %all-to-all-start.8 = ((bf16[32,96,128]{2,1,0:T(8,128)(2,1)}), bf16[32,96,128]{2,1,0:T(8,128)(2,1)}, u32[]{:S(2)}, u32[]{:S(2)}) async-start(bf16[32,96,128]{2,1,0:T(8,128)(2,1)} %reduce_sum.192), calls=%async_computation.8 | async-start | bytes 1572864 | tf_op jit(solution)/shard_map/all_to_all | solution.py:26
  397.3 4.8 %copy-start.31 = (bf16[512,2,64]{0,2,1:T(8,128)(2,1)S(1)}, bf16[512,2,64]{0,2,1:T(8,128)(2,1)}, u32[]{:S(2)}) copy-start(bf16[512,2,64]{0,2,1:T(8,128)(2,1)} %copy-done.30) | copy-start | bytes 393220
  411.9 34.9 %all-to-all-start.6 = ((bf16[32,32,896]{2,1,0:T(8,128)(2,1)}), bf16[32,32,896]{2,1,0:T(8,128)(2,1)}, u32[]{:S(2)}, u32[]{:S(2)}) async-start(bf16[32,32,896]{2,1,0:T(8,128)(2,1)} %pad_maximum_fusion.2), calls=%async_computation.6 | async-start | bytes 3670016 | tf_op jit(solution)/shard_map/all_to_all | solution.py:26
  423.4 2.4 copy-start.52
  423.5 2.4 copy-start.6
  423.5 2.4 copy-start.8
  423.5 2.4 copy-start.15
  423.5 2.4 copy-start.36
  423.5 2.4 copy-start.41
  423.5 2.4 copy-start.47
  423.5 2.4 copy-start.49
  423.5 2.4 copy-start.51
  425.9 25.2 %copy-start.1 = (s32[512,8]{0,1:T(8,128)S(1)}, s32[512,8]{0,1:T(8,128)}, u32[]{:S(2)}) copy-start(s32[512,8]{0,1:T(8,128)} %param.16) | copy-start | bytes 49156
  (16 other events, 21.6 us)

commit v3 on v2

--- a/solution.py
+++ b/solution.py
@@ -15,88 +15,6 @@
 EPSILON = 1e-06
 ROPE_BASE = 10000.0
 MASKED = -1e30
-
-
-def from_everyone(shard, axis):
-    copies = jnp.broadcast_to(shard, (lax.axis_size(axis), *shard.shape))
-    return lax.all_to_all(copies, axis, split_axis=0, concat_axis=0, tiled=True)
-
-
-def swapped(blocks, axis):
-    return lax.all_to_all(blocks, axis, split_axis=0, concat_axis=0, tiled=True)
-
-
-def added_up(blocks, axis):
-    return jnp.sum(swapped(blocks, axis).astype(jnp.float32), axis=0)
-
-
-def dot_right(left_mat, right_mat):
-    return lax.dot_general(
-        left_mat, right_mat, (((1,), (1,)), ((), ())), preferred_element_type=jnp.float32
-    )
-
-
-def dot_left(left_mat, right_mat):
-    return lax.dot_general(
-        left_mat, right_mat, (((0,), (0,)), ((), ())), preferred_element_type=jnp.float32
-    )
-
-
-def rope_tables(seg_ids):
-    length_total = seg_ids.shape[-1]
-    places = jnp.arange(length_total, dtype=jnp.int32)
-    starts_new = jnp.concatenate(
-        [
-            jnp.ones(seg_ids.shape[:-1] + (1,), dtype=jnp.bool_),
-            seg_ids[..., 1:] != seg_ids[..., :-1],
-        ],
-        axis=-1,
-    )
-    doc_start = lax.cummax(jnp.where(starts_new, places, 0), axis=seg_ids.ndim - 1)
-    position = (places - doc_start).astype(jnp.float32)
-    halves = jnp.arange(HEAD_SIZE // 2, dtype=jnp.int32).astype(jnp.float32)
-    rate_list = jnp.exp(halves * (-2.0 * math.log(ROPE_BASE) / HEAD_SIZE))
-    angles = position[..., None] * rate_list
-    return (jnp.cos(angles), jnp.sin(angles))
-
-
-def rotary_apply(values, cosine_lookup, sine_lookup):
-    half_dim = values.shape[-1] // 2
-    front_half = values[..., :half_dim]
-    back_half = values[..., half_dim:]
-    cos_wide = cosine_lookup[..., None, :]
-    sin_wide = sine_lookup[..., None, :]
-    return jnp.concatenate(
-        [
-            front_half * cos_wide - back_half * sin_wide,
-            back_half * cos_wide + front_half * sin_wide,
-        ],
-        axis=-1,
-    )
-
-
-def rotate_back(values, cosine_lookup, sine_lookup):
-    half_dim = values.shape[-1] // 2
-    front_half = values[..., :half_dim]
-    back_half = values[..., half_dim:]
-    cos_wide = cosine_lookup[..., None, :]
-    sin_wide = sine_lookup[..., None, :]
-    return jnp.concatenate(
-        [
-            front_half * cos_wide + back_half * sin_wide,
-            back_half * cos_wide - front_half * sin_wide,
-        ],
-        axis=-1,
-    )
-
-
-def norm_back(values, inverse, gain_vec, grad_out):
-    scaled = grad_out * gain_vec
-    grad_gain = jnp.sum(grad_out * values * inverse, axis=0)
-    grad_vals = inverse * scaled - values * inverse * inverse * inverse * jnp.mean(
-        scaled * values, axis=-1, keepdims=True
-    )
-    return (grad_vals, grad_gain)
 
 
 MESH = pl.DeviceIdType.MESH
@@ -432,22 +350,500 @@
     )(packed, inputs, seg, routes, blocks, cot)
 
 
-def head_scores(queries, keys, allowed):
-    scores = jnp.einsum(
-        "qkgd,tkd->kgqt", queries, keys, preferred_element_type=jnp.float32
-    ) * HEAD_SIZE ** (-0.5)
-    return jnp.where(allowed, scores, MASKED)
-
-
-def slot_picker(my_routes, cap_dev):
-    rows = my_routes.shape[0]
-    named = (my_routes[:, :, None] == jnp.arange(EXPERTS, dtype=jnp.int32)).astype(jnp.float32)
-    member = jnp.sum(named, axis=1)
-    earlier = jnp.tril(jnp.ones((rows, rows), jnp.bfloat16), -1)
-    slot = jnp.dot(earlier, member.astype(jnp.bfloat16), preferred_element_type=jnp.float32)
-    slot = jnp.where(member > 0, slot, -1.0)
-    picked = slot.T[:, None, :] == jnp.arange(cap_dev + 1, dtype=jnp.float32)[None, :, None]
-    return named, picked.astype(jnp.bfloat16)
+def greet_fsdp(me):
+    barrier = pltpu.get_barrier_semaphore()
+    loop(
+        1,
+        FSDP,
+        lambda k: pl.semaphore_signal(
+            barrier, inc=1, device_id={"fsdp": peer(me, k)}, device_id_type=MESH
+        ),
+    )
+    pl.semaphore_wait(barrier, FSDP - 1)
+
+
+def to_column(table, count):
+    n = table.shape[0]
+    spread = jnp.broadcast_to(table[:, None, :], (n, count, 128)).reshape(n * count, 128)
+    mine = lanes(spread.shape) == rows_of(spread.shape) % count
+    return jnp.sum(jnp.where(mine, spread, 0.0), axis=1, keepdims=True)
+
+
+def to_table(column, count):
+    n = column.shape[0] // count
+    spread = jnp.broadcast_to(column, (n * count, 128))
+    mine = lanes(spread.shape) == rows_of(spread.shape) % count
+    return jnp.sum(jnp.where(mine, spread, 0.0).reshape(n, count, 128), axis=1)
+
+
+def expert_kernel(
+    normed_two_ref, gates_ref, slot_ref, weights_ref, cot_main_ref, cot_spare_ref,
+    middle_ref, cot_ref, tail_ref,
+    out_main_ref, out_spare_ref, grads_ref, grad_middle_ref, router_part_ref, second_ref,
+    hot_main_ref, hot_spare_ref,
+    gate_mat, up_mat, down_mat, gate_t, row_send, spare_send, row_in, spare_in,
+    back_send, back_spare_send, back_in, back_spare_in,
+    hidden_ref, dgate_ref, dup_ref, ghidden_ref, sel_ref, gg_ref,
+    row_s, row_r, spare_s, spare_r, back_s, back_r, bspare_s, bspare_r,
+):
+    me = lax.axis_index("fsdp")
+    rows, width = normed_two_ref.shape
+    main = FSDP * 32
+    greet_fsdp(me)
+
+    def row_copy(k):
+        return to_fsdp(row_send.at[k], row_in.at[k], row_s.at[k], row_r.at[k], peer(me, k))
+
+    def spare_copy(k):
+        return to_fsdp(spare_send.at[k], spare_in.at[k], spare_s.at[k], spare_r.at[k], peer(me, k))
+
+    def back_copy(k):
+        return to_fsdp(back_send.at[k], back_in.at[k], back_s.at[k], back_r.at[k], giver(me, k))
+
+    def bspare_copy(k):
+        return to_fsdp(
+            back_spare_send.at[k], back_spare_in.at[k], bspare_s.at[k], bspare_r.at[k], giver(me, k)
+        )
+
+    gates_low = gates_ref[...].astype(BF16).astype(F32)
+    gate_t[...] = jnp.transpose(gates_low)[:EXPERTS]
+
+    def some_rows(i):
+        experts = [peer(me, 4 * i + j) for j in range(4)]
+        hot = pick(slot_ref, experts, 40)
+        out = nn(hot, normed_two_ref[...])
+        for j in range(4):
+            k = 4 * i + j
+            mine = hot[40 * j : 40 * j + 40].astype(F32)
+            column = jnp.sum(mine * gate_t[pl.ds(experts[j], 1), :], axis=1, keepdims=True)
+            row_send[k] = out[40 * j : 40 * j + 32].astype(BF16)
+            spare_send[k, :, :1024] = out[40 * j + 32 : 40 * j + 33]
+            spare_send[k, :, 1024:] = to_table(column, 40)
+            hot_main_ref[k] = hot[40 * j : 40 * j + 32]
+            hot_spare_ref[pl.ds(k, 1), :] = mine[32:33]
+
+        def go(k):
+            row_copy(k).start()
+            spare_copy(k).start()
+
+        loop(jnp.maximum(4 * i, 1), 4 * i + 4, go)
+
+    loop(0, FSDP // 4, some_rows)
+    row_in[0] = row_send[0]
+    spare_in[0] = spare_send[0]
+
+    for j in range(TP):
+        cols = slice(128 * j, 128 * j + 128)
+        gate_mat[:, cols] = weights_ref[j, :, 0:32, :].reshape(width, 128)
+        up_mat[:, cols] = weights_ref[j, :, 32:64, :].reshape(width, 128)
+        down_mat[:, cols] = weights_ref[j, :, 64:96, :].reshape(width, 128)
+
+    def hidden_grads(i):
+        cot_rows = cot_main_ref[pl.ds(8 * i, 8)].reshape(256, width)
+        ghidden_ref[pl.ds(256 * i, 256), :] = nn(cot_rows, down_mat[...])
+
+    loop(0, 4, hidden_grads)
+    cot_spare = cot_spare_ref[...].reshape(FSDP, width).astype(BF16)
+    ghidden_ref[pl.ds(main, FSDP), :] = nn(cot_spare, down_mat[...])
+
+    def expert_rows(x, gate, where):
+        gate_act = nn(x, gate_mat[...])
+        up_act = nn(x, up_mat[...])
+        grad_hidden = ghidden_ref[where, :]
+        sigmoid_gate = 1.0 / (1.0 + jnp.exp(-gate_act))
+        silu_gate = gate_act * sigmoid_gate
+        both = silu_gate * up_act
+        hidden_ref[where, :] = (both * gate).astype(BF16)
+        grad_prod = grad_hidden * gate
+        dgate = (
+            grad_prod * up_act * sigmoid_gate * (1.0 + gate_act * (1.0 - sigmoid_gate))
+        ).astype(BF16)
+        dup = (grad_prod * silu_gate).astype(BF16)
+        dgate_ref[where, :] = dgate
+        dup_ref[where, :] = dup
+        grad_in = nt(dgate, gate_mat[...]) + nt(dup, up_mat[...])
+        return grad_in, jnp.sum(both * grad_hidden, axis=1, keepdims=True)
+
+    def some_experts(i):
+        def got(k):
+            row_copy(k).wait_recv()
+            spare_copy(k).wait_recv()
+
+        loop(jnp.maximum(8 * i, 1), 8 * i + 8, got)
+        x = row_in[pl.ds(8 * i, 8)].reshape(256, width)
+        gate = to_column(spare_in[pl.ds(8 * i, 8), :, 1024:].reshape(8, 128), 32)
+        grad_in, sel = expert_rows(x, gate, pl.ds(256 * i, 256))
+        back_send[pl.ds(8 * i, 8)] = grad_in.astype(BF16).reshape(8, 32, width)
+        sel_ref[pl.ds(8 * i, 8), :] = to_table(sel, 32)
+        loop(jnp.maximum(8 * i, 1), 8 * i + 8, lambda k: back_copy(k).start())
+
+    loop(0, 4, some_experts)
+    spare = spare_in[...].reshape(FSDP, 1152)
+    spare_gate = spare[:, 1056:1057]
+    spare_rows = spare[:, :1024].astype(BF16)
+    grad_in, sel = expert_rows(spare_rows, spare_gate, pl.ds(main, FSDP))
+    sel_all = jnp.where(lanes((FSDP, 128)) == 32, sel, sel_ref[...])
+    for k in range(FSDP):
+        back_spare_send[k, :, :1024] = grad_in[k : k + 1]
+        back_spare_send[k, :, 1024:] = sel_all[k : k + 1]
+    loop(1, FSDP, lambda k: bspare_copy(k).start())
+    back_in[0] = back_send[0]
+    back_spare_in[0] = back_spare_send[0]
+
+    def outputs(i):
+        out = nt(hidden_ref[pl.ds(256 * i, 256), :], down_mat[...])
+        out_main_ref[pl.ds(8 * i, 8)] = out.astype(BF16).reshape(8, 32, width)
+
+    loop(0, 4, outputs)
+    out = nt(hidden_ref[pl.ds(main, FSDP), :], down_mat[...])
+    for k in range(FSDP):
+        out_spare_ref[k] = out[k : k + 1]
+
+    def weight_grads(i):
+        at = pl.ds(pl.multiple_of(256 * i, 256), 256)
+        x = row_in[:, :, at].reshape(main, 256)
+        x_spare = spare_in[:, :, at].reshape(FSDP, 256).astype(BF16)
+        c = cot_main_ref[:, :, at].reshape(main, 256)
+        c_spare = cot_spare_ref[:, :, at].reshape(FSDP, 256).astype(BF16)
+        for m, (a, a_spare, b) in enumerate(
+            ((x, x_spare, dgate_ref), (x, x_spare, dup_ref), (c, c_spare, hidden_ref))
+        ):
+            part = tn(a, b[pl.ds(0, main), :]) + tn(a_spare, b[pl.ds(main, FSDP), :])
+            part = part.astype(BF16)
+            for j in range(TP):
+                grads_ref[j, pl.ds(8 * i, 8), 32 * m : 32 * m + 32, :] = part[
+                    :, 128 * j : 128 * j + 128
+                ].reshape(8, 32, 128)
+
+    loop(0, 4, weight_grads)
+
+    def back_got(k):
+        back_copy(k).wait_recv()
+        bspare_copy(k).wait_recv()
+
+    loop(1, FSDP, back_got)
+    hot = hot_main_ref[...].reshape(main, rows)
+    hot_spare = hot_spare_ref[...]
+    back_spare = back_spare_in[...].reshape(FSDP, 1152)
+    grad_rows = tn(hot, back_in[...].reshape(main, width)) + tn(
+        hot_spare.astype(BF16), back_spare[:, :1024].astype(BF16)
+    )
+    sel = back_spare[:, 1024:]
+    by_slot = jnp.sum(
+        (hot.astype(F32) * to_column(sel, 32)).reshape(FSDP, 32, rows), axis=1
+    ) + hot_spare * sel[:, 32:33]
+    gg_ref[...] = jnp.zeros_like(gg_ref)
+    for k in range(FSDP):
+        gg_ref[pl.ds(peer(me, k), 1), :] = by_slot[k : k + 1]
+    grad_gates = jnp.transpose(gg_ref[...])
+    gates = gates_ref[...]
+    grad_chosen = gates * (grad_gates - jnp.sum(gates * grad_gates, axis=1, keepdims=True))
+    grad_logits = grad_chosen.astype(BF16)
+    tail = tail_ref[...].reshape(width, 128)
+    gain_two = jnp.transpose(tail.astype(F32))[EXPERTS + 1 : EXPERTS + 2]
+    router_part_ref[...] = tn(normed_two_ref[...], grad_logits)
+    dy = grad_rows + nt(grad_logits, tail)
+    middle = middle_ref[...]
+    inverse = lax.rsqrt(jnp.mean(middle * middle, axis=-1, keepdims=True) + EPSILON)
+    scaled = dy * gain_two
+    second_ref[...] = jnp.sum(dy * middle * inverse, axis=0, keepdims=True)
+    grad_middle_ref[...] = (
+        cot_ref[...].astype(F32)
+        + inverse * scaled
+        - middle
+        * inverse
+        * inverse
+        * inverse
+        * jnp.mean(scaled * middle, axis=-1, keepdims=True)
+    )
+
+    def gone(k):
+        row_copy(k).wait_send()
+        spare_copy(k).wait_send()
+        back_copy(k).wait_send()
+        bspare_copy(k).wait_send()
+
+    loop(1, FSDP, gone)
+
+
+def experts(normed_two, gates, slot, weights, cot_main, cot_spare, middle, cot, tail):
+    rows, width = normed_two.shape
+    hidden = 128 * TP
+    slots = FSDP * SPARE
+    vmem = pl.BlockSpec(memory_space=pltpu.VMEM)
+    out = (
+        shape((FSDP, 32, width), BF16),
+        shape((FSDP, 1, width), F32),
+        shape(weights.shape, BF16),
+        shape((rows, width), F32),
+        shape((width, 128), F32),
+        shape((1, width), F32),
+        shape((FSDP, 32, rows), BF16),
+        shape((FSDP, rows), F32),
+    )
+    return pl.pallas_call(
+        expert_kernel,
+        out_shape=out,
+        in_specs=[vmem] * 9,
+        out_specs=[vmem] * len(out),
+        scratch_shapes=[
+            *[pltpu.VMEM((width, hidden), BF16)] * 3,
+            pltpu.VMEM((EXPERTS, rows), F32),
+            *[pltpu.VMEM((FSDP, 32, width), BF16), pltpu.VMEM((FSDP, 1, width + 128), F32)] * 4,
+            *[pltpu.VMEM((slots, hidden), BF16)] * 3,
+            pltpu.VMEM((slots, hidden), F32),
+            pltpu.VMEM((FSDP, 128), F32),
+            pltpu.VMEM((128, 128), F32),
+            *[dma(FSDP)] * 8,
+        ],
+        compiler_params=pltpu.CompilerParams(
+            collective_id=2, has_side_effects=True, vmem_limit_bytes=56 * 2**20
+        ),
+        name="experts",
+    )(normed_two, gates, slot, weights, cot_main, cot_spare, middle, cot, tail)
+
+
+def backward_kernel(
+    grad_middle_ref, packed_all_ref, heads_ref, normed_all_ref, attended_ref, cos_ref, sin_ref,
+    seg_ref, out_main_ref, out_spare_ref, grads_ref, middle_ref, hot_main_ref, hot_spare_ref,
+    inputs_ref, router_part_ref, second_ref,
+    output_ref, grad_inputs_ref, sums_ref, weight_grads_ref,
+    branch_own, branch_all, out_in, out_spare_in, pair_in, across_send, across_in, dw_send, dw_in,
+    normed_send, normed_in, sums_send, sums_in, small_own, small_in,
+    branch_s, branch_r, out_s, out_r, spare_s, spare_r, pair_s, pair_r, across_s, across_r,
+    dw_s, dw_r, normed_s, normed_r, sums_s, sums_r, small_s, small_r,
+):
+    me, tp = lax.axis_index("fsdp"), lax.axis_index("tp")
+    rows, width = inputs_ref.shape
+    total = seg_ref.shape[1]
+    core = lax.rem(tp, 2)
+    sibling = tp + 1 - 2 * core
+    across = lax.rem(tp + 2, TP)
+    greet(me, tp)
+
+    def branch_copy(k):
+        return to_tp(
+            branch_own, branch_all.at[tp], branch_s.at[k], branch_r.at[k], lax.rem(tp + k, TP)
+        )
+
+    def out_copy(k):
+        return to_fsdp(out_main_ref.at[k], out_in.at[k], out_s.at[k], out_r.at[k], giver(me, k))
+
+    def spare_copy(k):
+        return to_fsdp(
+            out_spare_ref.at[k], out_spare_in.at[k], spare_s.at[k], spare_r.at[k], giver(me, k)
+        )
+
+    def pair_copy(x):
+        return to_tp(
+            grads_ref.at[2 * x + 1 - core], pair_in.at[x], pair_s.at[x], pair_r.at[x], sibling
+        )
+
+    across_copy = to_tp(across_send, across_in, across_s.at[0], across_r.at[0], across)
+
+    def dw_copy(k):
+        p = peer(me, k)
+        return to_fsdp(dw_send.at[p], dw_in.at[me], dw_s.at[k], dw_r.at[k], p)
+
+    def normed_copy(k):
+        q = lax.rem(tp + k, TP)
+        return to_tp(normed_send.at[q], normed_in.at[k], normed_s.at[k], normed_r.at[k], q)
+
+    def sums_copy(k):
+        p = peer(me, k)
+        return to_fsdp(sums_send.at[p], sums_in.at[k], sums_s.at[k], sums_r.at[k], p)
+
+    def small_copy(k):
+        return to_tp(small_own, small_in.at[k], small_s.at[k], small_r.at[k], lax.rem(tp + k, TP))
+
+    grad_middle = grad_middle_ref[...]
+    branch_own[...] = grad_middle.astype(BF16)
+    for k in (2, 1, 3):
+        branch_copy(k).start()
+    for x in range(2):
+        pair_copy(x).start()
+
+    def out_go(k):
+        out_copy(k).start()
+        spare_copy(k).start()
+
+    loop(1, FSDP, out_go)
+    branch_all[tp] = branch_own[...]
+    out_in[0] = out_main_ref[0]
+    out_spare_in[0] = out_spare_ref[0]
+
+    for x in range(2):
+        pair_copy(x).wait_recv()
+    far = 1 - tp // 2
+    across_send[...] = (
+        grads_ref[2 * far + core].astype(F32) + pair_in[far].astype(F32)
+    ).astype(BF16)
+    across_copy.start()
+
+    seg_row = jnp.broadcast_to(seg_ref[...].astype(F32), (128, total))
+    seg_col = jnp.transpose(seg_row)[:, :1]
+    allowed = (
+        (seg_col == seg_row[:1]) & (rows_of((total, total)) >= lanes((total, total)))
+    ).astype(F32)
+
+    for k in range(1, TP):
+        branch_copy(k).wait_recv()
+    branch = branch_all[...].reshape(total, width)
+    out_part = tn(branch, attended_ref[...])
+    grad_attended = nn(branch, packed_all_ref[:, :, 512:768].reshape(width, 256)).astype(BF16)
+    scale = HEAD_SIZE ** (-0.5)
+    dq, dk, dv = [], [], []
+    for g in range(2):
+        key = heads_ref[:, 256 + 64 * g : 320 + 64 * g]
+        value = heads_ref[:, 384 + 64 * g : 448 + 64 * g]
+        dk_sum, dv_sum = None, None
+        for h in (2 * g, 2 * g + 1):
+            q = heads_ref[:, 64 * h : 64 * h + 64]
+            da = grad_attended[:, 64 * h : 64 * h + 64]
+            scores = jnp.where(allowed > 0, nt(q, key) * scale, MASKED)
+            top = jnp.max(scores, axis=1, keepdims=True)
+            grown = jnp.exp(scores - top)
+            whole = grown * (1.0 / jnp.sum(grown, axis=1, keepdims=True))
+            grad_shares = nt(da, value)
+            inner = jnp.sum(whole * grad_shares, axis=1, keepdims=True)
+            grad_scores = (whole * (grad_shares - inner)).astype(BF16)
+            dq.append(nn(grad_scores, key) * scale)
+            dk_one = tn(grad_scores, q) * scale
+            dv_one = tn(whole.astype(BF16), da)
+            dk_sum = dk_one if dk_sum is None else dk_sum + dk_one
+            dv_sum = dv_one if dv_sum is None else dv_sum + dv_one
+        dk.append(dk_sum)
+        dv.append(dv_sum)
+    turned = jnp.concatenate(dq + dk, axis=1)
+    turn = turned * wide_table(cos_ref[...], 384) - half_swap(turned) * wide_table(
+        sin_ref[...], 384
+    )
+    grad_lin = jnp.concatenate([turn] + dv, axis=1).astype(BF16)
+    grad_normed = nt(grad_lin, packed_all_ref[:, :, 0:512].reshape(width, 512))
+    normed_send[...] = grad_normed.astype(BF16).reshape(TP, rows, width)
+    for k in (2, 1, 3):
+        normed_copy(k).start()
+    gain_one = jnp.transpose(packed_all_ref[:, :, 768:896].reshape(width, 128).astype(F32))[
+        EXPERTS : EXPERTS + 1
+    ]
+    first = jnp.sum(grad_normed * normed_all_ref[...].astype(F32), axis=0, keepdims=True) / gain_one
+
+    qkv_part = tn(normed_all_ref[...], grad_lin)
+    sums_send[:, :, 0:512] = qkv_part.astype(BF16).reshape(FSDP, 32, 512)
+    sums_send[:, :, 512:768] = out_part.astype(BF16).reshape(FSDP, 32, 256)
+    at = rows_of((128, width))
+    gains = jnp.where(at == EXPERTS, first, 0.0) + jnp.where(at == EXPERTS + 1, second_ref[...], 0.0)
+    small = router_part_ref[...] + jnp.transpose(gains)
+    sums_send[:, :, 768:896] = small.astype(BF16).reshape(FSDP, 32, 128)
+    loop(1, FSDP, lambda k: sums_copy(k).start())
+    sums_in[0] = sums_send[me]
+
+    across_copy.wait_recv()
+    near = tp // 2
+    dw_send[...] = (
+        grads_ref[tp].astype(F32) + pair_in[near].astype(F32) + across_in[...].astype(F32)
+    ).astype(BF16)
+    loop(1, FSDP, lambda k: dw_copy(k).start())
+    dw_in[me] = dw_send[me]
+
+    for k in range(1, TP):
+        normed_copy(k).wait_recv()
+    dy = normed_send[tp].astype(F32)
+    for k in range(1, TP):
+        dy = dy + normed_in[k].astype(F32)
+    wide = inputs_ref[...].astype(F32)
+    inverse = lax.rsqrt(jnp.mean(wide * wide, axis=-1, keepdims=True) + EPSILON)
+    scaled = dy * gain_one
+    grad_inputs_ref[...] = (
+        grad_middle
+        + inverse * scaled
+        - wide
+        * inverse
+        * inverse
+        * inverse
+        * jnp.mean(scaled * wide, axis=-1, keepdims=True)
+    )
+
+    def out_got(k):
+        out_copy(k).wait_recv()
+        spare_copy(k).wait_recv()
+
+    loop(1, FSDP, out_got)
+    hot = hot_main_ref[...].reshape(FSDP * 32, rows)
+    output_ref[...] = (
+        middle_ref[...]
+        + tn(hot, out_in[...].reshape(FSDP * 32, width))
+        + tn(hot_spare_ref[...].astype(BF16), out_spare_in[...].reshape(FSDP, width).astype(BF16))
+    ).astype(BF16)
+
+    loop(1, FSDP, lambda k: sums_copy(k).wait_recv())
+    sums = jnp.sum(sums_in[...].astype(F32), axis=0)
+    sums_ref[:, :768] = sums[:, :768]
+    small_own[...] = sums[:, 768:]
+    for k in (2, 1, 3):
+        small_copy(k).start()
+    loop(1, FSDP, lambda k: dw_copy(k).wait_recv())
+    weight_grads_ref[...] = dw_in[...].astype(F32)
+    for k in range(1, TP):
+        small_copy(k).wait_recv()
+    sums_ref[:, 768:] = small_own[...] + small_in[1] + small_in[2] + small_in[3]
+
+    def gone(k):
+        out_copy(k).wait_send()
+        spare_copy(k).wait_send()
+        sums_copy(k).wait_send()
+        dw_copy(k).wait_send()
+
+    loop(1, FSDP, gone)
+    for k in range(1, TP):
+        branch_copy(k).wait_send()
+        normed_copy(k).wait_send()
+        small_copy(k).wait_send()
+    for x in range(2):
+        pair_copy(x).wait_send()
+    across_copy.wait_send()
+
+
+def backward(*operands):
+    grads, inputs, packed_all = operands[10], operands[14], operands[1]
+    rows, width = inputs.shape
+    vmem = pl.BlockSpec(memory_space=pltpu.VMEM)
+    out = (
+        shape((rows, width), BF16),
+        shape((rows, width), F32),
+        shape(packed_all.shape[1:], F32),
+        shape(grads.shape[1:], F32),
+    )
+    return pl.pallas_call(
+        backward_kernel,
+        out_shape=out,
+        in_specs=[vmem] * len(operands),
+        out_specs=[vmem] * len(out),
+        scratch_shapes=[
+            pltpu.VMEM((rows, width), BF16),
+            pltpu.VMEM((TP, rows, width), BF16),
+            pltpu.VMEM((FSDP, 32, width), BF16),
+            pltpu.VMEM((FSDP, 1, width), F32),
+            pltpu.VMEM((2, *grads.shape[1:]), BF16),
+            *[pltpu.VMEM(grads.shape[1:], BF16)] * 4,
+            *[pltpu.VMEM((TP, rows, width), BF16)] * 2,
+            *[pltpu.VMEM(packed_all.shape, BF16)] * 2,
+            pltpu.VMEM((32, 128), F32),
+            pltpu.VMEM((TP, 32, 128), F32),
+            *[dma(TP)] * 2,
+            *[dma(FSDP)] * 4,
+            *[dma(2)] * 2,
+            *[dma(1)] * 2,
+            *[dma(FSDP)] * 2,
+            *[dma(TP)] * 2,
+            *[dma(FSDP)] * 2,
+            *[dma(TP)] * 2,
+        ],
+        compiler_params=pltpu.CompilerParams(
+            collective_id=3, has_side_effects=True, vmem_limit_bytes=56 * 2**20
+        ),
+        name="attention_backward",
+    )(*operands)
 
 
 def per_device(
@@ -466,17 +862,10 @@
     down_weight,
     cotangent,
 ):
-    row_count, model_width = inputs.shape
-    length_total = segments.shape[1]
+    row_count = inputs.shape[0]
     my_offset = lax.axis_index("tp") * row_count
-    tp_count = lax.axis_size("tp")
-    fsdp_count = lax.axis_size("fsdp")
     width_shard = query_weight.shape[0]
     q_cols, k_cols, o_cols = query_weight.shape[1], key_projection_weight.shape[1], out_weight.shape[0]
-    expert_count, _, hidden_shard = gate_weight.shape
-    full_hidden = tp_count * hidden_shard
-    cap_dev = row_count * TOP * 33 // (EXPERTS * 32)
-    f32, bf16 = jnp.float32, jnp.bfloat16
 
     wide = q_cols + 2 * k_cols + o_cols
     packed = jnp.concatenate(
@@ -488,159 +877,26 @@
             router_weight,
             first_gain[:, None],
             second_gain[:, None],
-            jnp.zeros((width_shard, 128 - EXPERTS - 2), bf16),
+            jnp.zeros((width_shard, 128 - EXPERTS - 2), BF16),
         ],
         axis=1,
     )
-    weight_blocks = jnp.concatenate(
+    blocks = jnp.concatenate(
         [gate_weight, up_weight, jnp.transpose(down_weight, (0, 2, 1))], axis=1
     )
     my_routes = lax.dynamic_slice_in_dim(routes, my_offset, row_count, 0)
     (
         middle, normed_two, gates, slot, weights, cot_main, cot_spare,
-        packed_all, heads, normed_all, attended, cos_wide, sin_wide,
-    ) = forward(packed, inputs, segments, my_routes, weight_blocks, cotangent)
-    weights = weights.reshape(tp_count, fsdp_count, 3, width_shard, hidden_shard)
-    weights = jnp.transpose(weights, (2, 1, 3, 0, 4)).reshape(3, model_width, full_hidden)
-    gate_mat, up_mat, down_mat = weights[0], weights[1], weights[2]
-    me = lax.axis_index("fsdp")
-    offs = jnp.arange(FSDP, dtype=jnp.int32)
-    peers = peer(me, offs)
-    givers = giver(me, offs)
-    back_of = jnp.zeros((FSDP,), jnp.int32).at[givers].set(offs)
-    cot_main, cot_spare = cot_main[back_of], cot_spare[back_of]
-    cot_local = jnp.concatenate([cot_main, cot_spare.astype(bf16)], axis=1).reshape(-1, model_width)
-    gathered = packed_all.reshape(model_width, -1)
-    qkv_mat = gathered[:, : q_cols + 2 * k_cols]
-    out_mat_t = gathered[:, q_cols + 2 * k_cols : wide]
-    router_mat = gathered[:, wide : wide + EXPERTS]
-    gain_one = gathered[:, wide + EXPERTS].astype(f32)
-    gain_two = gathered[:, wide + EXPERTS + 1].astype(f32)
-    query_heads, key_heads = q_cols // HEAD_SIZE, k_cols // HEAD_SIZE
-    queries = heads[:, :q_cols].reshape(length_total, key_heads, -1, HEAD_SIZE)
-    keys = heads[:, q_cols : q_cols + k_cols].reshape(length_total, key_heads, HEAD_SIZE)
-    values = heads[:, q_cols + k_cols :].reshape(length_total, key_heads, HEAD_SIZE)
-    cosine, sine = cos_wide[:, :32], sin_wide[:, :32]
-    place = jnp.arange(length_total, dtype=jnp.int32)
-    allowed = (segments[0][:, None] == segments[0][None, :]) & (place[:, None] >= place[None, :])
-    scores = head_scores(queries, keys, allowed)
-    top_score = jnp.max(scores, axis=-1, keepdims=True)
-    log_total = top_score + jnp.log(jnp.sum(jnp.exp(scores - top_score), axis=-1, keepdims=True))
-    inputs_wide = inputs.astype(f32)
-    inverse_one = lax.rsqrt(jnp.mean(inputs_wide * inputs_wide, axis=-1, keepdims=True) + EPSILON)
-    inverse_two = lax.rsqrt(jnp.mean(middle * middle, axis=-1, keepdims=True) + EPSILON)
-    named = (my_routes[:, :, None] == jnp.arange(EXPERTS, dtype=jnp.int32)).astype(f32)
-    gate_values = jnp.sum(named * gates[:, None, :EXPERTS], axis=-1)
-    gate_table = gates[:, :EXPERTS].astype(bf16).astype(f32)
-    picked = (slot[:, None, :] == jnp.arange(cap_dev + 1, dtype=f32)[None, :, None]).astype(bf16)
-    gates_mine = jnp.sum(picked[:, :cap_dev].astype(f32) * gate_table.T[:, None, :], axis=-1)
-    rows_mine = jnp.einsum("ect,td->ecd", picked[:, :cap_dev], normed_two, preferred_element_type=f32).astype(bf16)
-    gate_row = jnp.pad(gates_mine.astype(bf16)[:, None, :], ((0, 0), (0, 0), (0, model_width - cap_dev)))
-    arrived = swapped(jnp.concatenate([rows_mine, gate_row], axis=1), "fsdp")
-    rows_local = arrived[:, :cap_dev].reshape(-1, model_width)
-    gate_sel = arrived[:, cap_dev, :cap_dev].astype(f32).reshape(-1, 1)
-
-    grad_hidden = jnp.dot(cot_local, down_mat, preferred_element_type=f32)
-    gate_act = jnp.dot(rows_local, gate_mat, preferred_element_type=f32)
-    up_act = jnp.dot(rows_local, up_mat, preferred_element_type=f32)
-    sigmoid_gate = jax.nn.sigmoid(gate_act)
-    silu_gate = gate_act * sigmoid_gate
-    grad_prod = grad_hidden * gate_sel
-    grad_gate_pre = (
-        grad_prod * up_act * sigmoid_gate * (1.0 + gate_act * (1.0 - sigmoid_gate))
-    ).astype(bf16)
-    grad_up_pre = (grad_prod * silu_gate).astype(bf16)
-    grad_sel = jnp.sum(silu_gate * up_act * grad_hidden, axis=-1)
-    grad_in = dot_right(grad_gate_pre, gate_mat) + dot_right(grad_up_pre, up_mat)
-    sel_row = jnp.pad(
-        grad_sel.reshape(fsdp_count, 1, cap_dev), ((0, 0), (0, 0), (0, model_width - cap_dev))
-    ).astype(bf16)
-    back = jnp.concatenate(
-        [grad_in.astype(bf16).reshape(fsdp_count, cap_dev, model_width), sel_row], axis=1
-    )
-    back = swapped(back, "fsdp")
-    hidden = (silu_gate * up_act * gate_sel).astype(bf16)
-    expert_out = dot_right(hidden, down_mat).astype(bf16)
-    out_back = swapped(expert_out.reshape(fsdp_count, cap_dev, model_width), "fsdp")
-
-    def by_shard(left, right):
-        both = dot_left(left, right).astype(bf16)
-        return both.reshape(fsdp_count, width_shard, tp_count, hidden_shard)
-
-    grads = jnp.stack(
-        [
-            by_shard(rows_local, grad_gate_pre),
-            by_shard(rows_local, grad_up_pre),
-            by_shard(cot_local, hidden),
-        ],
-        axis=1,
-    )
-    grads = jnp.transpose(grads, (3, 0, 1, 2, 4)).reshape(
-        tp_count, fsdp_count, 3 * width_shard, hidden_shard
-    )
-    weight_grads = swapped(added_up(grads, "tp").astype(bf16), "fsdp").astype(f32)
-    grad_gate_out = weight_grads[:, :width_shard]
-    grad_up_out = weight_grads[:, width_shard : 2 * width_shard]
-    grad_down_out = jnp.transpose(weight_grads[:, 2 * width_shard :], (0, 2, 1))
-
-    picked_flat = picked[:, :cap_dev].reshape(-1, row_count)
-    grad_rows = dot_left(picked_flat, back[:, :cap_dev].reshape(-1, model_width))
-    sel_back = back[:, cap_dev, :cap_dev].astype(f32)
-    gate_grad_table = jnp.sum(picked[:, :cap_dev].astype(f32) * sel_back[:, :, None], axis=1).T
-    grad_gates = jnp.sum(named * gate_grad_table[:, None, :], axis=-1)
-    grad_chosen = gate_values * (
-        grad_gates - jnp.sum(gate_values * grad_gates, axis=-1, keepdims=True)
-    )
-    grad_logits = jnp.sum(grad_chosen[:, :, None] * named, axis=1).astype(bf16)
-    router_part = dot_left(normed_two, grad_logits)
-    grad_normed_two = grad_rows + dot_right(grad_logits, router_mat)
-    grad_middle_norm, second_part = norm_back(middle, inverse_two, gain_two, grad_normed_two)
-    grad_middle = cotangent.astype(f32) + grad_middle_norm
-    output = (
-        middle + dot_left(picked_flat, out_back.reshape(-1, model_width))
-    ).astype(bf16)
-
-    grad_branch = from_everyone(grad_middle.astype(bf16), "tp").reshape(length_total, model_width)
-    out_part = dot_left(grad_branch, attended)
-    grad_attended = (
-        jnp.dot(grad_branch, out_mat_t, preferred_element_type=f32)
-        .astype(bf16)
-        .reshape(length_total, key_heads, -1, HEAD_SIZE)
-    )
-    whole = jnp.exp(head_scores(queries, keys, allowed) - log_total)
-    grad_shares = jnp.einsum("qkgd,tkd->kgqt", grad_attended, values, preferred_element_type=f32)
-    inner = jnp.sum(whole * grad_shares, axis=-1, keepdims=True)
-    grad_scores = (whole * (grad_shares - inner)).astype(bf16)
-    scale = HEAD_SIZE ** (-0.5)
-    grad_rot_q = jnp.einsum("kgqt,tkd->qkgd", grad_scores, keys, preferred_element_type=f32) * scale
-    grad_rot_k = jnp.einsum("kgqt,qkgd->tkd", grad_scores, queries, preferred_element_type=f32) * scale
-    grad_values = jnp.einsum(
-        "kgqt,qkgd->tkd", whole.astype(bf16), grad_attended, preferred_element_type=f32
-    )
-    grad_lin = jnp.concatenate(
-        [
-            rotate_back(
-                grad_rot_q.reshape(length_total, query_heads, HEAD_SIZE), cosine, sine
-            ).reshape(length_total, -1),
-            rotate_back(grad_rot_k, cosine, sine).reshape(length_total, -1),
-            grad_values.reshape(length_total, -1),
-        ],
-        axis=1,
-    ).astype(bf16)
-    qkv_part = dot_left(normed_all, grad_lin)
-    grad_normed = added_up(
-        dot_right(grad_lin, qkv_mat).astype(bf16).reshape(tp_count, row_count, model_width), "tp"
-    )
-    grad_inputs_norm, first_part = norm_back(inputs_wide, inverse_one, gain_one, grad_normed)
-    grad_inputs = grad_middle + grad_inputs_norm
-
-    token_parts = jnp.concatenate(
-        [router_part, first_part[:, None], second_part[:, None]], axis=1
-    )
-    token_sums = jnp.sum(from_everyone(token_parts.T, "tp"), axis=0).T
-    small = jnp.pad(token_sums, ((0, 0), (0, 128 - EXPERTS - 2)))
-    sums_in = jnp.concatenate([qkv_part, out_part, small], axis=1).astype(bf16)
-    sums = added_up(sums_in.reshape(fsdp_count, width_shard, -1), "fsdp")
+        packed_all, heads, normed_all, attended, cosine, sine,
+    ) = forward(packed, inputs, segments, my_routes, blocks, cotangent)
+    tail = packed_all[:, :, wide:]
+    (
+        out_main, out_spare, grads, grad_middle, router_part, second_part, hot_main, hot_spare
+    ) = experts(normed_two, gates, slot, weights, cot_main, cot_spare, middle, cotangent, tail)
+    output, grad_inputs, sums, weight_grads = backward(
+        grad_middle, packed_all, heads, normed_all, attended, cosine, sine, segments,
+        out_main, out_spare, grads, middle, hot_main, hot_spare, inputs, router_part, second_part,
+    )
     return (
         output,
         grad_inputs,
@@ -651,9 +907,9 @@
         sums[:, wide : wide + EXPERTS],
         sums[:, wide + EXPERTS],
         sums[:, wide + EXPERTS + 1],
-        grad_gate_out,
-        grad_up_out,
-        grad_down_out,
+        weight_grads[:, :width_shard],
+        weight_grads[:, width_shard : 2 * width_shard],
+        jnp.transpose(weight_grads[:, 2 * width_shard :], (0, 2, 1)),
     )
 
 

time: 460 us -> 322 us (0.70); the launches traced: 451 us -> 320 us
  Pallas kernels: 110 us -> 301 us
  waiting for transfers between devices: 111 us -> 0 us
  local copies, waits for them, and re-layouts: 78.5 us -> 15.8 us
  starting transfers between devices: 58.9 us -> 0 us
  matrix products: 54.8 us -> 0 us
  other arithmetic: 35.5 us -> 2.03 us
    pallas_call x0 -> x2, Pallas kernels: none -> 191 us  [the longest x1 111 us: backward(): pl.pallas_call(backward_kernel, out_shape=out, in_specs=[vmem] * len(oper...]
    all_to_all x9 -> x0, waiting for transfers between devices: 111 us -> none  [the longest x7 105 us: swapped(): return lax.all_to_all(blocks, axis, split_axis=0, concat_axis=0, tiled=True)]
    all_to_all x9 -> x0, starting transfers between devices: 58.9 us -> none  [the longest x7 50.8 us: swapped(): return lax.all_to_all(blocks, axis, split_axis=0, concat_axis=0, tiled=True)]
    dot_general x23 -> x0, matrix products: 54.8 us -> none  [the longest x8 21.7 us: dot_left(): lax.dot_general(left_mat, right_mat, (((0,), (0,)), ((), ())), preferred_...]
    reshape x6 -> x0, local copies, waits for them, and re-layouts: 20.1 us -> none  [the longest x1 5.97 us: per_device(): weights.reshape(tp_count, fsdp_count, 3, width_shard, hidden_shard)]
    another operation x6 -> x0, local copies, waits for them, and re-layouts: 12.8 us -> none  [per_device(): jnp.stack([by_shard(rows_local, grad_gate_pre), by_shard(rows_local, grad...]
    slice x10 -> x1, local copies, waits for them, and re-layouts: 13.6 us -> 1.67 us  [per_device(): tail = packed_all[:, :, wide:]]
    reduce_sum x13 -> x0, other arithmetic: 11 us -> none  [the longest x3 6.71 us: added_up(): return jnp.sum(swapped(blocks, axis).astype(jnp.float32), axis=0)]
  transfers between devices with their start and end apart: 9 -> 0, of which waited for: 7 -> 0; matrix products, arithmetic and copies ran while one was open for 26% -> 0% of each run, Pallas kernels for 0% -> 0%
where the time goes in v3:
time: 322 us; the launch traced here: 320 us
  Pallas kernels  301 us (93%)
  local copies, waits for them, and re-layouts  15.8 us (5%)
    pallas_call x1, Pallas kernels, backward(): pl.pallas_call(backward_kernel, out_shape=out, in_specs=[vmem] * len(oper...  111 us
    pallas_call x1, Pallas kernels, forward(): pl.pallas_call(forward_kernel, out_shape=out, in_specs=[vmem] * 6, out_sp...  110 us
    pallas_call x1, Pallas kernels, experts(): pl.pallas_call(expert_kernel, out_shape=out, in_specs=[vmem] * 9, out_spe...  80.2 us

profile of v3, /device:TPU:8, one launch (start us, length us, event | category | flops | bytes accessed | tf_op | source)
XLA Modules:
  0.0 319.9 jit_solution(9364813289770290760)
XLA Ops:
  0.6 0.0 copy-start
  0.7 0.7 copy-done
  1.4 0.7 copy.29
  2.1 0.8 copy.30
  2.9 1.5 concatenate.6.packed_ref
  4.3 0.7 copy.32.routes_ref
  5.1 2.0 pad_maximum_fusion.blocks_ref
  7.1 110.3 %attention_forward.1 = (f32[128,1024]{1,0:T(8,128)}, bf16[128,1024]{1,0:T(8,128)(2,1)}, f32[128,128]{1,0:T(8,128)}, f32[32,128]{1,0:T(8,128)}, bf16[4,32,96,128]...) custom-call(bf16[32,896]{1,0:T(8,128)(2,1)} %concatenate.6.packed_re, ...), custom_call_target="tpu_custom_call" | custom-call | tf_op jit(solution)/shard_map/attention_forward/pallas_call | solution.py:330
  117.5 1.7 slice.33.tail_ref
  119.1 80.2 %experts.1 = (bf16[32,32,1024]{2,1,0:T(8,128)(2,1)}, f32[32,1,1024]{2,1,0:T(1,128)}, bf16[4,32,96,128]{3,2,1,0:T(8,128)(2,1)}, f32[128,1024]{1,0:T(8,128)}, f32[...) custom-call(bf16[128,1024]{1,0:T(8,128)(2,1)} %get-tuple-element.37.normed_two_ref, ...), custom_call_target="tpu_custom_call" | custom-call | tf_op jit(solution)/shard_map/experts/pallas_call | solution.py:584
  199.4 110.9 %attention_backward.1 = (bf16[128,1024]{1,0:T(8,128)(2,1)}, f32[128,1024]{1,0:T(8,128)}, f32[32,896]{1,0:T(8,128)}, f32[32,96,128]{2,1,0:T(8,128)}) custom-call(f32[128,1024]{1,0:T(8,128)} %get-tuple-element.45.grad_middle_ref, bf16[32,32,896]{2,1,0:T(8,128)(2,1)} %get-tuple-element.44.packed_all_ref, bf16[512,512]{1,0:T(8,128)(2,1)} %get-tuple-element.46.heads_ref, ...), custom_call_target="tpu_custom_call" | custom-call | tf_op jit(solution)/shard_map/attention_backward/pallas_call | solution.py:817
  310.2 1.5 slice_reduce_fusion
  311.7 1.3 slice.38
  313.1 1.3 fusion
  314.4 1.4 slice_bitcast_fusion.1
  315.8 0.0 copy-start.2
  315.8 0.0 copy-start.1
  315.8 2.6 slice_bitcast_fusion
  318.4 0.0 copy-done.2
  318.4 0.7 copy.35
  319.1 0.0 copy-done.1
  319.1 0.8 copy.36
  (2 shorter events, 0.0 us)
Async XLA Ops:
  0.6 0.7 copy-start
  315.8 2.6 copy-start.2
  315.8 3.3 %copy-start.1 = (f32[128,1024]{1,0:T(8,128)S(1)}, f32[128,1024]{1,0:T(8,128)}, u32[]{:S(2)}) copy-start(f32[128,1024]{1,0:T(8,128)} %get-tuple-element.84) | copy-start | bytes 1572868

commit v4 on v3

--- a/solution.py
+++ b/solution.py
@@ -32,6 +32,10 @@
     return ((z + 4 - k // 8) % 4 * 2 + (x + (k // 4) % 2) % 2) * 4 + (y + 4 - k % 4) % 4
 
 
+def side(tp, k):
+    return lax.rem(tp + 2 * ((k // 4) % 2), TP)
+
+
 def loop(low, high, step):
     def body(k, carry):
         step(k)
@@ -42,18 +46,22 @@
 
 def greet(me, tp):
     barrier = pltpu.get_barrier_semaphore()
-    loop(
-        1,
-        FSDP,
-        lambda k: pl.semaphore_signal(
-            barrier, inc=1, device_id={"fsdp": peer(me, k)}, device_id_type=MESH
-        ),
-    )
+
+    def signal(k):
+        for q in (tp, lax.rem(tp + 2, TP)):
+            pl.semaphore_signal(
+                barrier,
+                inc=1,
+                device_id={"fsdp": peer(me, k), "tp": q},
+                device_id_type=MESH,
+            )
+
+    loop(1, FSDP, signal)
     for k in range(1, TP):
         pl.semaphore_signal(
             barrier, inc=1, device_id={"tp": lax.rem(tp + k, TP)}, device_id_type=MESH
         )
-    pl.semaphore_wait(barrier, FSDP - 1 + TP - 1)
+    pl.semaphore_wait(barrier, 2 * (FSDP - 1) + TP - 1)
 
 
 def to_fsdp(src, dst, send, recv, where):
@@ -74,6 +82,17 @@
         send_sem=send,
         recv_sem=recv,
         device_id={"tp": where},
+        device_id_type=MESH,
+    )
+
+
+def to_side(src, dst, send, recv, where, q):
+    return pltpu.make_async_remote_copy(
+        src_ref=src,
+        dst_ref=dst,
+        send_sem=send,
+        recv_sem=recv,
+        device_id={"fsdp": where, "tp": q},
         device_id_type=MESH,
     )
 
@@ -138,33 +157,56 @@
             packed_ref, packed_all_ref.at[me], packed_send.at[k], packed_recv.at[k], peer(me, k)
         )
 
+    core = lax.rem(tp, 2)
+    sibling = tp + 1 - 2 * core
+    across = lax.rem(tp + 2, TP)
+
     def inputs_copy(k):
-        return to_tp(
-            inputs_ref, inputs_all.at[tp], inputs_send.at[k], inputs_recv.at[k], lax.rem(tp + k, TP)
-        )
+        block, where = ((tp, across), (tp, sibling), (across, sibling))[k]
+        src = inputs_ref if k < 2 else inputs_all.at[block]
+        return to_tp(src, inputs_all.at[block], inputs_send.at[k], inputs_recv.at[k], where)
 
     def blocks_copy(k):
         p = peer(me, k)
-        return to_fsdp(blocks_ref.at[p], blocks_in.at[me], blocks_send.at[k], blocks_recv.at[k], p)
+        return to_side(
+            blocks_ref.at[p], blocks_in.at[me], blocks_send.at[k], blocks_recv.at[k], p, side(tp, k)
+        )
 
     def main_copy(k):
-        return to_fsdp(
-            send_main.at[k], cot_main_ref.at[k], main_send.at[k], main_recv.at[k], peer(me, k)
+        return to_side(
+            send_main.at[k],
+            cot_main_ref.at[k],
+            main_send.at[k],
+            main_recv.at[k],
+            peer(me, k),
+            side(tp, k),
         )
 
     def spare_copy(k):
-        return to_fsdp(
-            send_spare.at[k], cot_spare_ref.at[k], spare_send.at[k], spare_recv.at[k], peer(me, k)
-        )
-
-    def branch_copy(k):
-        q = lax.rem(tp + k, TP)
+        return to_side(
+            send_spare.at[k],
+            cot_spare_ref.at[k],
+            spare_send.at[k],
+            spare_recv.at[k],
+            peer(me, k),
+            side(tp, k),
+        )
+
+    def branch_copy(x):
         return to_tp(
-            branch_out.at[q], branch_in.at[k], branch_send.at[k], branch_recv.at[k], q
-        )
-
-    for k in (2, 1, 3):
-        inputs_copy(k).start()
+            branch_out.at[2 * x + 1 - core],
+            branch_in.at[x],
+            branch_send.at[x],
+            branch_recv.at[x],
+            sibling,
+        )
+
+    branch_across = to_tp(
+        branch_in.at[2], branch_in.at[3], branch_send.at[2], branch_recv.at[2], across
+    )
+
+    inputs_copy(0).start()
+    inputs_copy(1).start()
     loop(1, FSDP, lambda k: packed_copy(k).start())
     loop(1, FSDP, lambda k: blocks_copy(k).start())
     keep = [
@@ -212,8 +254,10 @@
     cos_ref[...] = jnp.cos(angle)
     sin_ref[...] = jnp.sin(angle)
 
-    for k in range(1, TP):
-        inputs_copy(k).wait_recv()
+    inputs_copy(0).wait_recv()
+    inputs_copy(2).start()
+    inputs_copy(1).wait_recv()
+    inputs_copy(2).wait_recv()
     keep[1].wait()
     wide = inputs_all[...].reshape(total, width).astype(F32)
     inverse = lax.rsqrt(jnp.mean(wide * wide, axis=-1, keepdims=True) + EPSILON)
@@ -243,13 +287,19 @@
     attended_ref[...] = attended
     branch = nt(attended, packed_all_ref[:, :, 512:768].reshape(width, 256))
     branch_out[...] = branch.astype(BF16).reshape(TP, rows, width)
-    for k in (2, 1, 3):
-        branch_copy(k).start()
+    for x in range(2):
+        branch_copy(x).start()
+    for x in range(2):
+        branch_copy(x).wait_recv()
+    near = tp // 2
+    far = 1 - near
+    branch_in[2] = (
+        branch_out[across].astype(F32) + branch_in[far].astype(F32)
+    ).astype(BF16)
+    branch_across.start()
 
     loop(1, FSDP, lambda k: blocks_copy(k).wait_recv())
     keep[2].wait()
-    sibling = tp + 1 - 2 * lax.rem(tp, 2)
-    across = lax.rem(tp + 2, TP)
     first = to_tp(blocks_in, weights_ref.at[tp], weights_send.at[0], weights_recv.at[0], across)
     second = to_tp(blocks_in, weights_ref.at[tp], weights_send.at[1], weights_recv.at[1], sibling)
     third = to_tp(
@@ -260,11 +310,9 @@
     mine = pltpu.make_async_copy(blocks_in, weights_ref.at[tp], own_sem.at[3])
     mine.start()
 
-    for k in range(1, TP):
-        branch_copy(k).wait_recv()
+    branch_across.wait_recv()
     middle = inputs_ref[...].astype(F32) + branch_out[tp].astype(F32)
-    for k in range(1, TP):
-        middle = middle + branch_in[k].astype(F32)
+    middle = middle + branch_in[near].astype(F32) + branch_in[3].astype(F32)
     middle_ref[...] = middle
     inverse_two = lax.rsqrt(jnp.mean(middle * middle, axis=-1, keepdims=True) + EPSILON)
     normed_two = (middle * inverse_two * tail[EXPERTS + 1 : EXPERTS + 2]).astype(BF16)
@@ -293,10 +341,11 @@
         spare_copy(k).wait_send()
 
     loop(1, FSDP, gone)
-    for k in range(1, TP):
+    for k in range(3):
         inputs_copy(k).wait_send()
-        branch_copy(k).wait_send()
-    for copy in (first, second, third):
+    for x in range(2):
+        branch_copy(x).wait_send()
+    for copy in (branch_across, first, second, third):
         copy.wait_send()
 
 
@@ -350,13 +399,16 @@
     )(packed, inputs, seg, routes, blocks, cot)
 
 
-def greet_fsdp(me):
+def greet_fsdp(me, tp):
     barrier = pltpu.get_barrier_semaphore()
     loop(
         1,
         FSDP,
         lambda k: pl.semaphore_signal(
-            barrier, inc=1, device_id={"fsdp": peer(me, k)}, device_id_type=MESH
+            barrier,
+            inc=1,
+            device_id={"fsdp": peer(me, k), "tp": side(tp, k)},
+            device_id_type=MESH,
         ),
     )
     pl.semaphore_wait(barrier, FSDP - 1)
@@ -386,23 +438,35 @@
     hidden_ref, dgate_ref, dup_ref, ghidden_ref, sel_ref, gg_ref,
     row_s, row_r, spare_s, spare_r, back_s, back_r, bspare_s, bspare_r,
 ):
-    me = lax.axis_index("fsdp")
+    me, tp = lax.axis_index("fsdp"), lax.axis_index("tp")
+    half = (me // 4) % 2
     rows, width = normed_two_ref.shape
     main = FSDP * 32
-    greet_fsdp(me)
+    greet_fsdp(me, tp)
 
     def row_copy(k):
-        return to_fsdp(row_send.at[k], row_in.at[k], row_s.at[k], row_r.at[k], peer(me, k))
+        return to_side(
+            row_send.at[k], row_in.at[k], row_s.at[k], row_r.at[k], peer(me, k), side(tp, k)
+        )
 
     def spare_copy(k):
-        return to_fsdp(spare_send.at[k], spare_in.at[k], spare_s.at[k], spare_r.at[k], peer(me, k))
+        return to_side(
+            spare_send.at[k], spare_in.at[k], spare_s.at[k], spare_r.at[k], peer(me, k), side(tp, k)
+        )
 
     def back_copy(k):
-        return to_fsdp(back_send.at[k], back_in.at[k], back_s.at[k], back_r.at[k], giver(me, k))
+        return to_side(
+            back_send.at[k], back_in.at[k], back_s.at[k], back_r.at[k], giver(me, k), side(tp, k)
+        )
 
     def bspare_copy(k):
-        return to_fsdp(
-            back_spare_send.at[k], back_spare_in.at[k], bspare_s.at[k], bspare_r.at[k], giver(me, k)
+        return to_side(
+            back_spare_send.at[k],
+            back_spare_in.at[k],
+            bspare_s.at[k],
+            bspare_r.at[k],
+            giver(me, k),
+            side(tp, k),
         )
 
     gates_low = gates_ref[...].astype(BF16).astype(F32)
@@ -432,11 +496,17 @@
     row_in[0] = row_send[0]
     spare_in[0] = spare_send[0]
 
-    for j in range(TP):
-        cols = slice(128 * j, 128 * j + 128)
-        gate_mat[:, cols] = weights_ref[j, :, 0:32, :].reshape(width, 128)
-        up_mat[:, cols] = weights_ref[j, :, 32:64, :].reshape(width, 128)
-        down_mat[:, cols] = weights_ref[j, :, 64:96, :].reshape(width, 128)
+    def side_by_side(i):
+        at = pl.ds(pl.multiple_of(128 * i, 128), 128)
+        swap = 2 * lax.rem(half + i, 2)
+        for j in range(TP):
+            cols = slice(128 * j, 128 * j + 128)
+            block = weights_ref[lax.rem(j + swap, TP), pl.ds(4 * i, 4)]
+            gate_mat[at, cols] = block[:, 0:32].reshape(128, 128)
+            up_mat[at, cols] = block[:, 32:64].reshape(128, 128)
+            down_mat[at, cols] = block[:, 64:96].reshape(128, 128)
+
+    loop(0, 8, side_by_side)
 
     def hidden_grads(i):
         cot_rows = cot_main_ref[pl.ds(8 * i, 8)].reshape(256, width)
@@ -511,9 +581,13 @@
             part = tn(a, b[pl.ds(0, main), :]) + tn(a_spare, b[pl.ds(main, FSDP), :])
             part = part.astype(BF16)
             for j in range(TP):
-                grads_ref[j, pl.ds(8 * i, 8), 32 * m : 32 * m + 32, :] = part[
-                    :, 128 * j : 128 * j + 128
-                ].reshape(8, 32, 128)
+                for h in range(2):
+                    grads_ref[
+                        lax.rem(j + 2 * lax.rem(half + h, 2), TP),
+                        pl.ds(8 * i + 4 * h, 4),
+                        32 * m : 32 * m + 32,
+                        :,
+                    ] = part[128 * h : 128 * h + 128, 128 * j : 128 * j + 128].reshape(4, 32, 128)
 
     loop(0, 4, weight_grads)
 
@@ -622,16 +696,23 @@
     greet(me, tp)
 
     def branch_copy(k):
-        return to_tp(
-            branch_own, branch_all.at[tp], branch_s.at[k], branch_r.at[k], lax.rem(tp + k, TP)
-        )
+        block, where = ((tp, across), (tp, sibling), (across, sibling))[k]
+        src = branch_own if k < 2 else branch_all.at[block]
+        return to_tp(src, branch_all.at[block], branch_s.at[k], branch_r.at[k], where)
 
     def out_copy(k):
-        return to_fsdp(out_main_ref.at[k], out_in.at[k], out_s.at[k], out_r.at[k], giver(me, k))
+        return to_side(
+            out_main_ref.at[k], out_in.at[k], out_s.at[k], out_r.at[k], giver(me, k), side(tp, k)
+        )
 
     def spare_copy(k):
-        return to_fsdp(
-            out_spare_ref.at[k], out_spare_in.at[k], spare_s.at[k], spare_r.at[k], giver(me, k)
+        return to_side(
+            out_spare_ref.at[k],
+            out_spare_in.at[k],
+            spare_s.at[k],
+            spare_r.at[k],
+            giver(me, k),
+            side(tp, k),
         )
 
     def pair_copy(x):
@@ -643,11 +724,20 @@
 
     def dw_copy(k):
         p = peer(me, k)
-        return to_fsdp(dw_send.at[p], dw_in.at[me], dw_s.at[k], dw_r.at[k], p)
-
-    def normed_copy(k):
-        q = lax.rem(tp + k, TP)
-        return to_tp(normed_send.at[q], normed_in.at[k], normed_s.at[k], normed_r.at[k], q)
+        return to_side(dw_send.at[p], dw_in.at[me], dw_s.at[k], dw_r.at[k], p, side(tp, k))
+
+    def normed_copy(x):
+        return to_tp(
+            normed_send.at[2 * x + 1 - core],
+            normed_in.at[x],
+            normed_s.at[x],
+            normed_r.at[x],
+            sibling,
+        )
+
+    normed_across = to_tp(
+        normed_in.at[2], normed_in.at[3], normed_s.at[2], normed_r.at[2], across
+    )
 
     def sums_copy(k):
         p = peer(me, k)
@@ -658,8 +748,8 @@
 
     grad_middle = grad_middle_ref[...]
     branch_own[...] = grad_middle.astype(BF16)
-    for k in (2, 1, 3):
-        branch_copy(k).start()
+    branch_copy(0).start()
+    branch_copy(1).start()
     for x in range(2):
         pair_copy(x).start()
 
@@ -669,12 +759,15 @@
 
     loop(1, FSDP, out_go)
     branch_all[tp] = branch_own[...]
+    branch_copy(0).wait_recv()
+    branch_copy(2).start()
     out_in[0] = out_main_ref[0]
     out_spare_in[0] = out_spare_ref[0]
 
     for x in range(2):
         pair_copy(x).wait_recv()
-    far = 1 - tp // 2
+    near = tp // 2
+    far = 1 - near
     across_send[...] = (
         grads_ref[2 * far + core].astype(F32) + pair_in[far].astype(F32)
     ).astype(BF16)
@@ -686,8 +779,8 @@
         (seg_col == seg_row[:1]) & (rows_of((total, total)) >= lanes((total, total)))
     ).astype(F32)
 
-    for k in range(1, TP):
-        branch_copy(k).wait_recv()
+    branch_copy(1).wait_recv()
+    branch_copy(2).wait_recv()
     branch = branch_all[...].reshape(total, width)
     out_part = tn(branch, attended_ref[...])
     grad_attended = nn(branch, packed_all_ref[:, :, 512:768].reshape(width, 256)).astype(BF16)
@@ -721,8 +814,8 @@
     grad_lin = jnp.concatenate([turn] + dv, axis=1).astype(BF16)
     grad_normed = nt(grad_lin, packed_all_ref[:, :, 0:512].reshape(width, 512))
     normed_send[...] = grad_normed.astype(BF16).reshape(TP, rows, width)
-    for k in (2, 1, 3):
-        normed_copy(k).start()
+    for x in range(2):
+        normed_copy(x).start()
     gain_one = jnp.transpose(packed_all_ref[:, :, 768:896].reshape(width, 128).astype(F32))[
         EXPERTS : EXPERTS + 1
     ]
@@ -738,19 +831,22 @@
     loop(1, FSDP, lambda k: sums_copy(k).start())
     sums_in[0] = sums_send[me]
 
+    for x in range(2):
+        normed_copy(x).wait_recv()
+    normed_in[2] = (
+        normed_send[across].astype(F32) + normed_in[far].astype(F32)
+    ).astype(BF16)
+    normed_across.start()
+
     across_copy.wait_recv()
-    near = tp // 2
     dw_send[...] = (
         grads_ref[tp].astype(F32) + pair_in[near].astype(F32) + across_in[...].astype(F32)
     ).astype(BF16)
     loop(1, FSDP, lambda k: dw_copy(k).start())
     dw_in[me] = dw_send[me]
 
-    for k in range(1, TP):
-        normed_copy(k).wait_recv()
-    dy = normed_send[tp].astype(F32)
-    for k in range(1, TP):
-        dy = dy + normed_in[k].astype(F32)
+    normed_across.wait_recv()
+    dy = normed_send[tp].astype(F32) + normed_in[near].astype(F32) + normed_in[3].astype(F32)
     wide = inputs_ref[...].astype(F32)
     inverse = lax.rsqrt(jnp.mean(wide * wide, axis=-1, keepdims=True) + EPSILON)
     scaled = dy * gain_one
@@ -795,12 +891,13 @@
         dw_copy(k).wait_send()
 
     loop(1, FSDP, gone)
-    for k in range(1, TP):
+    for k in range(3):
         branch_copy(k).wait_send()
-        normed_copy(k).wait_send()
-        small_copy(k).wait_send()
+        small_copy(k + 1).wait_send()
     for x in range(2):
+        normed_copy(x).wait_send()
         pair_copy(x).wait_send()
+    normed_across.wait_send()
     across_copy.wait_send()
 
 

time: 322 us -> 256 us (0.80)
  Pallas kernels: 301 us -> 234 us
    pallas_call x1, Pallas kernels: 111 us -> 78.4 us  [backward(): pl.pallas_call(backward_kernel, out_shape=out, in_specs=[vmem] * len(oper...]
    pallas_call x1, Pallas kernels: 110 us -> 80.3 us  [forward(): pl.pallas_call(forward_kernel, out_shape=out, in_specs=[vmem] * 6, out_sp...]
    pallas_call x1, Pallas kernels: 80.2 us -> 75.8 us  [experts(): pl.pallas_call(expert_kernel, out_shape=out, in_specs=[vmem] * 9, out_spe...]
where the time goes in v4:
time: 256 us; the launch traced here: 253 us
  Pallas kernels  234 us (91%)
  local copies, waits for them, and re-layouts  15.8 us (6%)
    pallas_call x1, Pallas kernels, forward(): pl.pallas_call(forward_kernel, out_shape=out, in_specs=[vmem] * 6, out_sp...  80.3 us
    pallas_call x1, Pallas kernels, backward(): pl.pallas_call(backward_kernel, out_shape=out, in_specs=[vmem] * len(oper...  78.4 us
    pallas_call x1, Pallas kernels, experts(): pl.pallas_call(expert_kernel, out_shape=out, in_specs=[vmem] * 9, out_spe...  75.8 us

profile of v4, /device:TPU:8, one launch (start us, length us, event | category | flops | bytes accessed | tf_op | source)
XLA Modules:
  0.0 252.9 jit_solution(18077240397670439979)
XLA Ops:
  0.6 0.0 copy-start
  0.7 0.7 copy-done
  1.4 0.7 copy.29
  2.1 0.8 copy.30
  2.9 1.5 concatenate.6.packed_ref
  4.3 0.7 copy.32.routes_ref
  5.1 2.0 pad_maximum_fusion.blocks_ref
  7.1 80.3 %attention_forward.1 = (f32[128,1024]{1,0:T(8,128)}, bf16[128,1024]{1,0:T(8,128)(2,1)}, f32[128,128]{1,0:T(8,128)}, f32[32,128]{1,0:T(8,128)}, bf16[4,32,96,128]...) custom-call(bf16[32,896]{1,0:T(8,128)(2,1)} %concatenate.6.packed_re, ...), custom_call_target="tpu_custom_call" | custom-call | tf_op jit(solution)/shard_map/attention_forward/pallas_call | solution.py:379
  87.4 1.7 slice.33.tail_ref
  89.1 75.8 %experts.1 = (bf16[32,32,1024]{2,1,0:T(8,128)(2,1)}, f32[32,1,1024]{2,1,0:T(1,128)}, bf16[4,32,96,128]{3,2,1,0:T(8,128)(2,1)}, f32[128,1024]{1,0:T(8,128)}, f32[...) custom-call(bf16[128,1024]{1,0:T(8,128)(2,1)} %get-tuple-element.37.normed_two_ref, ...), custom_call_target="tpu_custom_call" | custom-call | tf_op jit(solution)/shard_map/experts/pallas_call | solution.py:658
  164.9 78.4 %attention_backward.1 = (bf16[128,1024]{1,0:T(8,128)(2,1)}, f32[128,1024]{1,0:T(8,128)}, f32[32,896]{1,0:T(8,128)}, f32[32,96,128]{2,1,0:T(8,128)}) custom-call(f32[128,1024]{1,0:T(8,128)} %get-tuple-element.45.grad_middle_ref, bf16[32,32,896]{2,1,0:T(8,128)(2,1)} %get-tuple-element.44.packed_all_ref, bf16[512,512]{1,0:T(8,128)(2,1)} %get-tuple-element.46.heads_ref, ...), custom_call_target="tpu_custom_call" | custom-call | tf_op jit(solution)/shard_map/attention_backward/pallas_call | solution.py:914
  243.2 1.5 slice_reduce_fusion
  244.7 1.3 slice.38
  246.1 1.3 fusion
  247.4 1.4 slice_bitcast_fusion.1
  248.8 0.0 copy-start.2
  248.8 0.0 copy-start.1
  248.8 2.6 %slice_bitcast_fusion = (f32[32,128,32]{1,2,0:T(8,128)}, f32[32,32,128]{2,1,0:T(8,128)}, f32[32,32,128]{2,1,0:T(8,128)}) fusion(f32[32,96,128]{2,1,0:T(8,128)} %get-tuple-element.61), kind=kLoop, calls=%fused_computation.1 | loop fusion | bytes 3145728 | tf_op jit(solution)/shard_map/transpose | solution.py:1009
  251.4 0.0 copy-done.2
  251.4 0.7 copy.35
  252.1 0.0 copy-done.1
  252.1 0.8 copy.36
  (2 shorter events, 0.0 us)
Async XLA Ops:
  0.6 0.7 copy-start
  248.8 2.6 %copy-start.2 = (bf16[128,1024]{1,0:T(8,128)(2,1)S(1)}, bf16[128,1024]{1,0:T(8,128)(2,1)}, u32[]{:S(2)}) copy-start(bf16[128,1024]{1,0:T(8,128)(2,1)} %get-tuple-element.83) | copy-start | bytes 786436
  248.8 3.3 %copy-start.1 = (f32[128,1024]{1,0:T(8,128)S(1)}, f32[128,1024]{1,0:T(8,128)}, u32[]{:S(2)}) copy-start(f32[128,1024]{1,0:T(8,128)} %get-tuple-element.84) | copy-start | bytes 1572868

commit v5 on v4

--- a/solution.py
+++ b/solution.py
@@ -139,7 +139,7 @@
     return (both == want).astype(BF16)
 
 
-def forward_kernel(
+def forward_part(
     packed_ref, inputs_ref, seg_ref, routes_ref, blocks_ref, cot_ref,
     middle_ref, normed_two_ref, gates_ref, slot_ref, weights_ref, cot_main_ref, cot_spare_ref,
     packed_all_ref, heads_ref, normed_all_ref, attended_ref, cos_ref, sin_ref,
@@ -310,6 +310,8 @@
     mine = pltpu.make_async_copy(blocks_in, weights_ref.at[tp], own_sem.at[3])
     mine.start()
 
+    for x in range(2):
+        branch_copy(x).wait_send()
     branch_across.wait_recv()
     middle = inputs_ref[...].astype(F32) + branch_out[tp].astype(F32)
     middle = middle + branch_in[near].astype(F32) + branch_in[3].astype(F32)
@@ -322,31 +324,37 @@
     grown = jnp.exp(logits - jnp.max(logits, axis=1, keepdims=True)) * member
     gates_ref[...] = grown / jnp.sum(grown, axis=1, keepdims=True)
 
-    first.wait_recv()
-    third.start()
-
-    def got(k):
-        main_copy(k).wait_recv()
-        spare_copy(k).wait_recv()
-
-    loop(1, FSDP, got)
-    second.wait_recv()
-    third.wait_recv()
-    mine.wait()
-
-    def gone(k):
-        packed_copy(k).wait_send()
-        blocks_copy(k).wait_send()
-        main_copy(k).wait_send()
-        spare_copy(k).wait_send()
-
-    loop(1, FSDP, gone)
-    for k in range(3):
-        inputs_copy(k).wait_send()
-    for x in range(2):
-        branch_copy(x).wait_send()
-    for copy in (branch_across, first, second, third):
-        copy.wait_send()
+    def pass_weights():
+        first.wait_recv()
+        third.start()
+
+    def weights_ready():
+        second.wait_recv()
+        third.wait_recv()
+        mine.wait()
+        for copy in (first, second, third):
+            copy.wait_send()
+
+    def cot_ready():
+        def got(k):
+            main_copy(k).wait_recv()
+            spare_copy(k).wait_recv()
+            main_copy(k).wait_send()
+
+        loop(1, FSDP, got)
+
+    def sent():
+        def gone(k):
+            packed_copy(k).wait_send()
+            blocks_copy(k).wait_send()
+            spare_copy(k).wait_send()
+
+        loop(1, FSDP, gone)
+        for k in range(3):
+            inputs_copy(k).wait_send()
+        branch_across.wait_send()
+
+    return pass_weights, weights_ready, cot_ready, sent
 
 
 def shape(dims, kind):
@@ -355,63 +363,6 @@
 
 def dma(count):
     return pltpu.SemaphoreType.DMA((count,))
-
-
-def forward(packed, inputs, seg, routes, blocks, cot):
-    rows, width = inputs.shape
-    total = seg.shape[1]
-    vmem = pl.BlockSpec(memory_space=pltpu.VMEM)
-    out = (
-        shape((rows, width), F32),
-        shape((rows, width), BF16),
-        shape((rows, 128), F32),
-        shape((EXPERTS, rows), F32),
-        shape((TP, *blocks.shape), BF16),
-        shape((FSDP, 32, width), BF16),
-        shape((FSDP, 1, width), F32),
-        shape((FSDP, *packed.shape), BF16),
-        shape((total, 512), BF16),
-        shape((total, width), BF16),
-        shape((total, 256), BF16),
-        shape((total, 128), F32),
-        shape((total, 128), F32),
-    )
-    return pl.pallas_call(
-        forward_kernel,
-        out_shape=out,
-        in_specs=[vmem] * 6,
-        out_specs=[vmem] * len(out),
-        scratch_shapes=[
-            pltpu.VMEM((TP, rows, width), BF16),
-            pltpu.VMEM(blocks.shape, BF16),
-            pltpu.VMEM((FSDP, 32, width), BF16),
-            pltpu.VMEM((FSDP, 1, width), F32),
-            pltpu.VMEM((TP, rows, width), BF16),
-            pltpu.VMEM((TP, rows, width), BF16),
-            *[dma(FSDP)] * 8,
-            *[dma(TP)] * 6,
-            dma(4),
-        ],
-        compiler_params=pltpu.CompilerParams(
-            collective_id=1, has_side_effects=True, vmem_limit_bytes=56 * 2**20
-        ),
-        name="attention_forward",
-    )(packed, inputs, seg, routes, blocks, cot)
-
-
-def greet_fsdp(me, tp):
-    barrier = pltpu.get_barrier_semaphore()
-    loop(
-        1,
-        FSDP,
-        lambda k: pl.semaphore_signal(
-            barrier,
-            inc=1,
-            device_id={"fsdp": peer(me, k), "tp": side(tp, k)},
-            device_id_type=MESH,
-        ),
-    )
-    pl.semaphore_wait(barrier, FSDP - 1)
 
 
 def to_column(table, count):
@@ -428,21 +379,23 @@
     return jnp.sum(jnp.where(mine, spread, 0.0).reshape(n, count, 128), axis=1)
 
 
-def expert_kernel(
+def expert_part(
+    pass_weights, weights_ready, cot_ready, start_pairs,
     normed_two_ref, gates_ref, slot_ref, weights_ref, cot_main_ref, cot_spare_ref,
-    middle_ref, cot_ref, tail_ref,
+    middle_ref, cot_ref, packed_all_ref,
     out_main_ref, out_spare_ref, grads_ref, grad_middle_ref, router_part_ref, second_ref,
     hot_main_ref, hot_spare_ref,
     gate_mat, up_mat, down_mat, gate_t, row_send, spare_send, row_in, spare_in,
     back_send, back_spare_send, back_in, back_spare_in,
     hidden_ref, dgate_ref, dup_ref, ghidden_ref, sel_ref, gg_ref,
+    out_in, out_spare_in,
     row_s, row_r, spare_s, spare_r, back_s, back_r, bspare_s, bspare_r,
+    out_s, out_r, out_spare_s, out_spare_r,
 ):
     me, tp = lax.axis_index("fsdp"), lax.axis_index("tp")
     half = (me // 4) % 2
     rows, width = normed_two_ref.shape
     main = FSDP * 32
-    greet_fsdp(me, tp)
 
     def row_copy(k):
         return to_side(
@@ -465,6 +418,21 @@
             back_spare_in.at[k],
             bspare_s.at[k],
             bspare_r.at[k],
+            giver(me, k),
+            side(tp, k),
+        )
+
+    def out_copy(k):
+        return to_side(
+            out_main_ref.at[k], out_in.at[k], out_s.at[k], out_r.at[k], giver(me, k), side(tp, k)
+        )
+
+    def out_spare_copy(k):
+        return to_side(
+            out_spare_ref.at[k],
+            out_spare_in.at[k],
+            out_spare_s.at[k],
+            out_spare_r.at[k],
             giver(me, k),
             side(tp, k),
         )
@@ -496,6 +464,9 @@
     row_in[0] = row_send[0]
     spare_in[0] = spare_send[0]
 
+    pass_weights()
+    weights_ready()
+
     def side_by_side(i):
         at = pl.ds(pl.multiple_of(128 * i, 128), 128)
         swap = 2 * lax.rem(half + i, 2)
@@ -507,6 +478,8 @@
             down_mat[at, cols] = block[:, 64:96].reshape(128, 128)
 
     loop(0, 8, side_by_side)
+
+    cot_ready()
 
     def hidden_grads(i):
         cot_rows = cot_main_ref[pl.ds(8 * i, 8)].reshape(256, width)
@@ -560,14 +533,20 @@
     back_in[0] = back_send[0]
     back_spare_in[0] = back_spare_send[0]
 
+    loop(1, FSDP, lambda k: row_copy(k).wait_send())
+
     def outputs(i):
         out = nt(hidden_ref[pl.ds(256 * i, 256), :], down_mat[...])
         out_main_ref[pl.ds(8 * i, 8)] = out.astype(BF16).reshape(8, 32, width)
+        loop(jnp.maximum(8 * i, 1), 8 * i + 8, lambda k: out_copy(k).start())
 
     loop(0, 4, outputs)
     out = nt(hidden_ref[pl.ds(main, FSDP), :], down_mat[...])
     for k in range(FSDP):
         out_spare_ref[k] = out[k : k + 1]
+    loop(1, FSDP, lambda k: out_spare_copy(k).start())
+    out_in[0] = out_main_ref[0]
+    out_spare_in[0] = out_spare_ref[0]
 
     def weight_grads(i):
         at = pl.ds(pl.multiple_of(256 * i, 256), 256)
@@ -591,6 +570,8 @@
 
     loop(0, 4, weight_grads)
 
+    start_pairs()
+
     def back_got(k):
         back_copy(k).wait_recv()
         bspare_copy(k).wait_recv()
@@ -613,7 +594,7 @@
     gates = gates_ref[...]
     grad_chosen = gates * (grad_gates - jnp.sum(gates * grad_gates, axis=1, keepdims=True))
     grad_logits = grad_chosen.astype(BF16)
-    tail = tail_ref[...].reshape(width, 128)
+    tail = packed_all_ref[:, :, 768:896].reshape(width, 128)
     gain_two = jnp.transpose(tail.astype(F32))[EXPERTS + 1 : EXPERTS + 2]
     router_part_ref[...] = tn(normed_two_ref[...], grad_logits)
     dy = grad_rows + nt(grad_logits, tail)
@@ -631,60 +612,35 @@
         * jnp.mean(scaled * middle, axis=-1, keepdims=True)
     )
 
-    def gone(k):
-        row_copy(k).wait_send()
-        spare_copy(k).wait_send()
-        back_copy(k).wait_send()
-        bspare_copy(k).wait_send()
-
-    loop(1, FSDP, gone)
-
-
-def experts(normed_two, gates, slot, weights, cot_main, cot_spare, middle, cot, tail):
-    rows, width = normed_two.shape
-    hidden = 128 * TP
-    slots = FSDP * SPARE
-    vmem = pl.BlockSpec(memory_space=pltpu.VMEM)
-    out = (
-        shape((FSDP, 32, width), BF16),
-        shape((FSDP, 1, width), F32),
-        shape(weights.shape, BF16),
-        shape((rows, width), F32),
-        shape((width, 128), F32),
-        shape((1, width), F32),
-        shape((FSDP, 32, rows), BF16),
-        shape((FSDP, rows), F32),
-    )
-    return pl.pallas_call(
-        expert_kernel,
-        out_shape=out,
-        in_specs=[vmem] * 9,
-        out_specs=[vmem] * len(out),
-        scratch_shapes=[
-            *[pltpu.VMEM((width, hidden), BF16)] * 3,
-            pltpu.VMEM((EXPERTS, rows), F32),
-            *[pltpu.VMEM((FSDP, 32, width), BF16), pltpu.VMEM((FSDP, 1, width + 128), F32)] * 4,
-            *[pltpu.VMEM((slots, hidden), BF16)] * 3,
-            pltpu.VMEM((slots, hidden), F32),
-            pltpu.VMEM((FSDP, 128), F32),
-            pltpu.VMEM((128, 128), F32),
-            *[dma(FSDP)] * 8,
-        ],
-        compiler_params=pltpu.CompilerParams(
-            collective_id=2, has_side_effects=True, vmem_limit_bytes=56 * 2**20
-        ),
-        name="experts",
-    )(normed_two, gates, slot, weights, cot_main, cot_spare, middle, cot, tail)
-
-
-def backward_kernel(
+    def out_ready():
+        def got(k):
+            out_copy(k).wait_recv()
+            out_spare_copy(k).wait_recv()
+
+        loop(1, FSDP, got)
+
+    def sent():
+        def gone(k):
+            spare_copy(k).wait_send()
+            back_copy(k).wait_send()
+            bspare_copy(k).wait_send()
+            out_copy(k).wait_send()
+            out_spare_copy(k).wait_send()
+
+        loop(1, FSDP, gone)
+
+    return out_ready, sent
+
+
+def backward_part(
+    out_ready, pair_copy,
     grad_middle_ref, packed_all_ref, heads_ref, normed_all_ref, attended_ref, cos_ref, sin_ref,
-    seg_ref, out_main_ref, out_spare_ref, grads_ref, middle_ref, hot_main_ref, hot_spare_ref,
+    seg_ref, grads_ref, middle_ref, hot_main_ref, hot_spare_ref,
     inputs_ref, router_part_ref, second_ref,
     output_ref, grad_inputs_ref, sums_ref, weight_grads_ref,
     branch_own, branch_all, out_in, out_spare_in, pair_in, across_send, across_in, dw_send, dw_in,
     normed_send, normed_in, sums_send, sums_in, small_own, small_in,
-    branch_s, branch_r, out_s, out_r, spare_s, spare_r, pair_s, pair_r, across_s, across_r,
+    branch_s, branch_r, across_s, across_r,
     dw_s, dw_r, normed_s, normed_r, sums_s, sums_r, small_s, small_r,
 ):
     me, tp = lax.axis_index("fsdp"), lax.axis_index("tp")
@@ -693,32 +649,11 @@
     core = lax.rem(tp, 2)
     sibling = tp + 1 - 2 * core
     across = lax.rem(tp + 2, TP)
-    greet(me, tp)
 
     def branch_copy(k):
         block, where = ((tp, across), (tp, sibling), (across, sibling))[k]
         src = branch_own if k < 2 else branch_all.at[block]
         return to_tp(src, branch_all.at[block], branch_s.at[k], branch_r.at[k], where)
-
-    def out_copy(k):
-        return to_side(
-            out_main_ref.at[k], out_in.at[k], out_s.at[k], out_r.at[k], giver(me, k), side(tp, k)
-        )
-
-    def spare_copy(k):
-        return to_side(
-            out_spare_ref.at[k],
-            out_spare_in.at[k],
-            spare_s.at[k],
-            spare_r.at[k],
-            giver(me, k),
-            side(tp, k),
-        )
-
-    def pair_copy(x):
-        return to_tp(
-            grads_ref.at[2 * x + 1 - core], pair_in.at[x], pair_s.at[x], pair_r.at[x], sibling
-        )
 
     across_copy = to_tp(across_send, across_in, across_s.at[0], across_r.at[0], across)
 
@@ -750,19 +685,9 @@
     branch_own[...] = grad_middle.astype(BF16)
     branch_copy(0).start()
     branch_copy(1).start()
-    for x in range(2):
-        pair_copy(x).start()
-
-    def out_go(k):
-        out_copy(k).start()
-        spare_copy(k).start()
-
-    loop(1, FSDP, out_go)
     branch_all[tp] = branch_own[...]
     branch_copy(0).wait_recv()
     branch_copy(2).start()
-    out_in[0] = out_main_ref[0]
-    out_spare_in[0] = out_spare_ref[0]
 
     for x in range(2):
         pair_copy(x).wait_recv()
@@ -860,11 +785,7 @@
         * jnp.mean(scaled * wide, axis=-1, keepdims=True)
     )
 
-    def out_got(k):
-        out_copy(k).wait_recv()
-        spare_copy(k).wait_recv()
-
-    loop(1, FSDP, out_got)
+    out_ready()
     hot = hot_main_ref[...].reshape(FSDP * 32, rows)
     output_ref[...] = (
         middle_ref[...]
@@ -885,8 +806,6 @@
     sums_ref[:, 768:] = small_own[...] + small_in[1] + small_in[2] + small_in[3]
 
     def gone(k):
-        out_copy(k).wait_send()
-        spare_copy(k).wait_send()
         sums_copy(k).wait_send()
         dw_copy(k).wait_send()
 
@@ -901,35 +820,153 @@
     across_copy.wait_send()
 
 
-def backward(*operands):
-    grads, inputs, packed_all = operands[10], operands[14], operands[1]
+def layer_kernel(
+    packed_ref, inputs_ref, seg_ref, routes_ref, blocks_ref, cot_ref,
+    output_ref, grad_inputs_ref, sums_ref, weight_grads_ref,
+    middle, normed_two, gates, slot, weights, cot_main, cot_spare, packed_all, heads, normed_all,
+    attended, cosine, sine,
+    inputs_all, blocks_in, rows_out, spare_out, branch_out, branch_in,
+    router_part, second_part, hot_main, hot_spare, grad_middle, out_spare,
+    gate_mat, up_mat, down_mat, gate_t, row_send, spare_send, row_in, spare_in,
+    back_spare_send, back_in, back_spare_in,
+    hidden, dgate, dup, ghidden, sel, gate_grads, out_in, out_spare_in,
+    branch_own, branch_all, pair_in, across_send, across_in, dw_send, dw_in, normed_in,
+    sums_send, sums_in, small_own, small_in,
+    *sems,
+):
+    tp = lax.axis_index("tp")
+    sems = list(sems)
+
+    def take(count):
+        taken = sems[:count]
+        del sems[:count]
+        return taken
+
+    pass_weights, weights_ready, cot_ready, forward_sent = forward_part(
+        packed_ref, inputs_ref, seg_ref, routes_ref, blocks_ref, cot_ref,
+        middle, normed_two, gates, slot, weights, cot_main, cot_spare,
+        packed_all, heads, normed_all, attended, cosine, sine,
+        inputs_all, blocks_in, rows_out, spare_out, branch_out, branch_in,
+        *take(15),
+    )
+    core = lax.rem(tp, 2)
+    pair_s, pair_r = take(2)
+
+    def pair_copy(x):
+        return to_tp(
+            weights.at[2 * x + 1 - core],
+            pair_in.at[x],
+            pair_s.at[x],
+            pair_r.at[x],
+            tp + 1 - 2 * core,
+        )
+
+    def start_pairs():
+        for x in range(2):
+            pair_copy(x).start()
+
+    out_ready, expert_sent = expert_part(
+        pass_weights, weights_ready, cot_ready, start_pairs,
+        normed_two, gates, slot, weights, cot_main, cot_spare, middle, cot_ref,
+        packed_all,
+        row_send, out_spare, weights, grad_middle, router_part, second_part, hot_main, hot_spare,
+        gate_mat, up_mat, down_mat, gate_t, row_send, spare_send, row_in, spare_in,
+        rows_out, back_spare_send, back_in, back_spare_in,
+        hidden, dgate, dup, ghidden, sel, gate_grads, out_in, out_spare_in,
+        *take(12),
+    )
+    backward_part(
+        out_ready, pair_copy,
+        grad_middle, packed_all, heads, normed_all, attended, cosine, sine, seg_ref,
+        weights, middle, hot_main, hot_spare, inputs_ref, router_part, second_part,
+        output_ref, grad_inputs_ref, sums_ref, weight_grads_ref,
+        branch_own, branch_all, out_in, out_spare_in, pair_in, across_send, across_in,
+        dw_send, dw_in, branch_out, normed_in, sums_send, sums_in, small_own, small_in,
+        *take(12),
+    )
+    forward_sent()
+    expert_sent()
+
+
+def layer(packed, inputs, seg, routes, blocks, cot):
     rows, width = inputs.shape
+    total = seg.shape[1]
+    hidden = 128 * TP
+    slots = FSDP * SPARE
     vmem = pl.BlockSpec(memory_space=pltpu.VMEM)
     out = (
         shape((rows, width), BF16),
         shape((rows, width), F32),
-        shape(packed_all.shape[1:], F32),
-        shape(grads.shape[1:], F32),
-    )
+        shape(packed.shape, F32),
+        shape(blocks.shape, F32),
+    )
+    block = pltpu.VMEM((FSDP, 32, width), BF16)
+    spare = pltpu.VMEM((FSDP, 1, width), F32)
+    spare_wide = pltpu.VMEM((FSDP, 1, width + 128), F32)
+    four = pltpu.VMEM((TP, rows, width), BF16)
+    shards = pltpu.VMEM(blocks.shape, BF16)
+    packs = pltpu.VMEM((FSDP, *packed.shape), BF16)
     return pl.pallas_call(
-        backward_kernel,
+        layer_kernel,
         out_shape=out,
-        in_specs=[vmem] * len(operands),
+        in_specs=[vmem] * 6,
         out_specs=[vmem] * len(out),
         scratch_shapes=[
+            pltpu.VMEM((rows, width), F32),
             pltpu.VMEM((rows, width), BF16),
-            pltpu.VMEM((TP, rows, width), BF16),
-            pltpu.VMEM((FSDP, 32, width), BF16),
-            pltpu.VMEM((FSDP, 1, width), F32),
-            pltpu.VMEM((2, *grads.shape[1:]), BF16),
-            *[pltpu.VMEM(grads.shape[1:], BF16)] * 4,
-            *[pltpu.VMEM((TP, rows, width), BF16)] * 2,
-            *[pltpu.VMEM(packed_all.shape, BF16)] * 2,
+            pltpu.VMEM((rows, 128), F32),
+            pltpu.VMEM((EXPERTS, rows), F32),
+            pltpu.VMEM((TP, *blocks.shape), BF16),
+            block,
+            spare,
+            packs,
+            pltpu.VMEM((total, 512), BF16),
+            pltpu.VMEM((total, width), BF16),
+            pltpu.VMEM((total, 256), BF16),
+            pltpu.VMEM((total, 128), F32),
+            pltpu.VMEM((total, 128), F32),
+            four,
+            shards,
+            block,
+            spare,
+            four,
+            four,
+            pltpu.VMEM((width, 128), F32),
+            pltpu.VMEM((1, width), F32),
+            pltpu.VMEM((FSDP, 32, rows), BF16),
+            pltpu.VMEM((FSDP, rows), F32),
+            pltpu.VMEM((rows, width), F32),
+            spare,
+            *[pltpu.VMEM((width, hidden), BF16)] * 3,
+            pltpu.VMEM((EXPERTS, rows), F32),
+            block,
+            spare_wide,
+            block,
+            spare_wide,
+            spare_wide,
+            block,
+            spare_wide,
+            *[pltpu.VMEM((slots, hidden), BF16)] * 3,
+            pltpu.VMEM((slots, hidden), F32),
+            pltpu.VMEM((FSDP, 128), F32),
+            pltpu.VMEM((128, 128), F32),
+            block,
+            spare,
+            pltpu.VMEM((rows, width), BF16),
+            four,
+            pltpu.VMEM((2, *blocks.shape), BF16),
+            *[shards] * 4,
+            four,
+            packs,
+            packs,
             pltpu.VMEM((32, 128), F32),
             pltpu.VMEM((TP, 32, 128), F32),
+            *[dma(FSDP)] * 8,
+            *[dma(TP)] * 6,
+            dma(4),
+            *[dma(2)] * 2,
+            *[dma(FSDP)] * 12,
             *[dma(TP)] * 2,
-            *[dma(FSDP)] * 4,
-            *[dma(2)] * 2,
             *[dma(1)] * 2,
             *[dma(FSDP)] * 2,
             *[dma(TP)] * 2,
@@ -937,10 +974,10 @@
             *[dma(TP)] * 2,
         ],
         compiler_params=pltpu.CompilerParams(
-            collective_id=3, has_side_effects=True, vmem_limit_bytes=56 * 2**20
+            collective_id=1, has_side_effects=True, vmem_limit_bytes=62 * 2**20
         ),
-        name="attention_backward",
-    )(*operands)
+        name="layer",
+    )(packed, inputs, seg, routes, blocks, cot)
 
 
 def per_device(
@@ -982,17 +1019,8 @@
         [gate_weight, up_weight, jnp.transpose(down_weight, (0, 2, 1))], axis=1
     )
     my_routes = lax.dynamic_slice_in_dim(routes, my_offset, row_count, 0)
-    (
-        middle, normed_two, gates, slot, weights, cot_main, cot_spare,
-        packed_all, heads, normed_all, attended, cosine, sine,
-    ) = forward(packed, inputs, segments, my_routes, blocks, cotangent)
-    tail = packed_all[:, :, wide:]
-    (
-        out_main, out_spare, grads, grad_middle, router_part, second_part, hot_main, hot_spare
-    ) = experts(normed_two, gates, slot, weights, cot_main, cot_spare, middle, cotangent, tail)
-    output, grad_inputs, sums, weight_grads = backward(
-        grad_middle, packed_all, heads, normed_all, attended, cosine, sine, segments,
-        out_main, out_spare, grads, middle, hot_main, hot_spare, inputs, router_part, second_part,
+    output, grad_inputs, sums, weight_grads = layer(
+        packed, inputs, segments, my_routes, blocks, cotangent
     )
     return (
         output,

time: 256 us -> 230 us (0.90)
  Pallas kernels: 234 us -> 212 us
    pallas_call x3 -> x1, Pallas kernels: 234 us -> 212 us  [layer(): pl.pallas_call(layer_kernel, out_shape=out, in_specs=[vmem] * 6, out_spec...]
where the time goes in v5:
time: 230 us; the launch traced here: 228 us
  Pallas kernels  212 us (92%)
  local copies, waits for them, and re-layouts  14.1 us (6%)
    pallas_call x1, Pallas kernels, layer(): pl.pallas_call(layer_kernel, out_shape=out, in_specs=[vmem] * 6, out_spec...  212 us

profile of v5, /device:TPU:8, one launch (start us, length us, event | category | flops | bytes accessed | tf_op | source)
XLA Modules:
  0.0 228.4 jit_solution(18121347197296625782)
XLA Ops:
  0.6 0.0 copy-start
  0.7 0.7 copy-done
  1.4 0.7 copy.29
  2.1 0.8 copy.30
  2.9 1.5 concatenate.6.packed_ref
  4.3 0.7 copy.32.routes_ref
  5.1 2.1 pad_maximum_fusion.blocks_ref
  7.1 211.6 %layer.1 = (bf16[128,1024]{1,0:T(8,128)(2,1)}, f32[128,1024]{1,0:T(8,128)}, f32[32,896]{1,0:T(8,128)}, f32[32,96,128]{2,1,0:T(8,128)}) custom-call(bf16[32,896]{1,0:T(8,128)(2,1)} %concatenate.6.packed_ref, bf16[128,1024]{1,0:T(8,128)(2,1)} %inputs_ref.1, s32[1,512]{1,0:T(1,128)} %seg_ref.1, s32[128,8]{1,0:T(8,128)} %copy.32.routes_ref, ...), custom_call_target="tpu_custom_call" | custom-call | tf_op jit(solution)/shard_map/layer/pallas_call | solution.py:909
  218.8 1.5 slice_reduce_fusion
  220.3 1.3 slice.34
  221.6 1.3 fusion
  222.9 1.4 slice_bitcast_fusion.1
  224.3 0.0 copy-start.2
  224.3 0.0 copy-start.1
  224.3 2.6 %slice_bitcast_fusion = (f32[32,128,32]{1,2,0:T(8,128)}, f32[32,32,128]{2,1,0:T(8,128)}, f32[32,32,128]{2,1,0:T(8,128)}) fusion(f32[32,96,128]{2,1,0:T(8,128)} %get-tuple-element.19), kind=kLoop, calls=%fused_computation.1 | loop fusion | bytes 3145728 | tf_op jit(solution)/shard_map/transpose | solution.py:1037
  226.9 0.0 copy-done.2
  226.9 0.7 copy.35
  227.6 0.0 copy-done.1
  227.7 0.8 copy.36
  (2 shorter events, 0.0 us)
Async XLA Ops:
  0.6 0.7 copy-start
  224.3 2.6 %copy-start.2 = (bf16[128,1024]{1,0:T(8,128)(2,1)S(1)}, bf16[128,1024]{1,0:T(8,128)(2,1)}, u32[]{:S(2)}) copy-start(bf16[128,1024]{1,0:T(8,128)(2,1)} %get-tuple-element.41) | copy-start | bytes 786436
  224.3 3.3 %copy-start.1 = (f32[128,1024]{1,0:T(8,128)S(1)}, f32[128,1024]{1,0:T(8,128)}, u32[]{:S(2)}) copy-start(f32[128,1024]{1,0:T(8,128)} %get-tuple-element.42) | copy-start | bytes 1572868

commit v6 on v5

--- a/solution.py
+++ b/solution.py
@@ -22,18 +22,25 @@
 F32, BF16 = jnp.float32, jnp.bfloat16
 
 
+def offset(k):
+    a, b, c = k % 4, (k // 4) % 4, k // 16
+    return a, (b + c) % 2, (a + b) % 4
+
+
 def peer(me, k):
+    dz, dx, dy = offset(k)
     z, x, y = me // 8, (me // 4) % 2, me % 4
-    return ((z + k // 8) % 4 * 2 + (x + (k // 4) % 2) % 2) * 4 + (y + k % 4) % 4
+    return ((z + dz) % 4 * 2 + (x + dx) % 2) * 4 + (y + dy) % 4
 
 
 def giver(me, k):
+    dz, dx, dy = offset(k)
     z, x, y = me // 8, (me // 4) % 2, me % 4
-    return ((z + 4 - k // 8) % 4 * 2 + (x + (k // 4) % 2) % 2) * 4 + (y + 4 - k % 4) % 4
+    return ((z + 4 - dz) % 4 * 2 + (x + dx) % 2) * 4 + (y + 4 - dy) % 4
 
 
 def side(tp, k):
-    return lax.rem(tp + 2 * ((k // 4) % 2), TP)
+    return lax.rem(tp + 2 * offset(k)[1], TP)
 
 
 def loop(low, high, step):
@@ -47,21 +54,18 @@
 def greet(me, tp):
     barrier = pltpu.get_barrier_semaphore()
 
-    def signal(k):
-        for q in (tp, lax.rem(tp + 2, TP)):
-            pl.semaphore_signal(
-                barrier,
-                inc=1,
-                device_id={"fsdp": peer(me, k), "tp": q},
-                device_id_type=MESH,
-            )
-
-    loop(1, FSDP, signal)
+    def signal(k, q):
+        pl.semaphore_signal(
+            barrier, inc=1, device_id={"fsdp": peer(me, k), "tp": q}, device_id_type=MESH
+        )
+
+    loop(1, FSDP, lambda k: signal(k, tp))
+    loop(0, 16, lambda n: signal(n + 16 * ((n // 4 + 1) % 2), lax.rem(tp + 2, TP)))
     for k in range(1, TP):
         pl.semaphore_signal(
             barrier, inc=1, device_id={"tp": lax.rem(tp + k, TP)}, device_id_type=MESH
         )
-    pl.semaphore_wait(barrier, 2 * (FSDP - 1) + TP - 1)
+    pl.semaphore_wait(barrier, FSDP - 1 + 16 + TP - 1)
 
 
 def to_fsdp(src, dst, send, recv, where):
@@ -140,17 +144,34 @@
 
 
 def forward_part(
-    packed_ref, inputs_ref, seg_ref, routes_ref, blocks_ref, cot_ref,
+    query_ref, key_ref, value_ref, out_weight_ref, router_ref, first_gain_ref, second_gain_ref,
+    gate_ref, up_ref, down_ref, inputs_ref, seg_ref, routes_ref, cot_ref,
     middle_ref, normed_two_ref, gates_ref, slot_ref, weights_ref, cot_main_ref, cot_spare_ref,
-    packed_all_ref, heads_ref, normed_all_ref, attended_ref, cos_ref, sin_ref,
-    inputs_all, blocks_in, send_main, send_spare, branch_out, branch_in,
-    packed_send, packed_recv, blocks_send, blocks_recv, main_send, main_recv, spare_send, spare_recv,
+    packed_all_ref, out_all_ref, heads_ref, normed_all_ref, attended_ref, cos_ref, sin_ref,
+    packed_ref, blocks_ref, inputs_all, blocks_in, send_main, send_spare, branch_out, branch_in,
+    packed_send, packed_recv, outw_send, outw_recv, blocks_send, blocks_recv, main_send, main_recv, spare_send, spare_recv,
     inputs_send, inputs_recv, weights_send, weights_recv, branch_send, branch_recv, own_sem,
 ):
     me, tp = lax.axis_index("fsdp"), lax.axis_index("tp")
     rows, width = inputs_ref.shape
     total = seg_ref.shape[1]
+    packed_ref[...] = jnp.zeros_like(packed_ref)
+    packed_ref[:, 0:256] = query_ref[...]
+    packed_ref[:, 256:384] = key_ref[...]
+    packed_ref[:, 384:512] = value_ref[...]
+    packed_ref[:, 512:544] = router_ref[...]
+    shard = query_ref.shape[0]
+    same_place = rows_of((shard, shard)) == lanes((shard, shard))
+    for n, gain_ref in enumerate((first_gain_ref, second_gain_ref)):
+        gain = jnp.broadcast_to(gain_ref[...].astype(F32), (shard, shard))
+        column = jnp.sum(jnp.where(same_place, gain, 0.0), axis=1, keepdims=True)
+        packed_ref[:, 544 + n : 545 + n] = column.astype(BF16)
     greet(me, tp)
+
+    def outw_copy(k):
+        return to_fsdp(
+            out_weight_ref, out_all_ref.at[me], outw_send.at[k], outw_recv.at[k], peer(me, k)
+        )
 
     def packed_copy(k):
         return to_fsdp(
@@ -208,23 +229,29 @@
     inputs_copy(0).start()
     inputs_copy(1).start()
     loop(1, FSDP, lambda k: packed_copy(k).start())
+    blocks_ref[:, 0:32, :] = gate_ref[...]
+    blocks_ref[:, 32:64, :] = up_ref[...]
+    blocks_ref[:, 64:96, :] = down_ref[...]
+    loop(1, FSDP, lambda k: outw_copy(k).start())
     loop(1, FSDP, lambda k: blocks_copy(k).start())
     keep = [
         pltpu.make_async_copy(packed_ref, packed_all_ref.at[me], own_sem.at[0]),
         pltpu.make_async_copy(inputs_ref, inputs_all.at[tp], own_sem.at[1]),
         pltpu.make_async_copy(blocks_ref.at[me], blocks_in.at[me], own_sem.at[2]),
+        pltpu.make_async_copy(out_weight_ref, out_all_ref.at[me], own_sem.at[4]),
     ]
     for copy in keep:
         copy.start()
 
-    at = lanes((rows, 128))
-    member = jnp.zeros((rows, 128), F32)
+    mine = routes_ref[:, pl.ds(pl.multiple_of(tp * rows, rows), rows)]
+    at = rows_of((128, rows))
+    member_t = jnp.zeros((128, rows), F32)
     for k in range(TOP):
-        member = member + (routes_ref[:, k : k + 1] == at).astype(F32)
-    earlier = (rows_of((rows, rows)) > lanes((rows, rows))).astype(BF16)
-    slot = nn(earlier, member.astype(BF16))
-    slot = jnp.where(member > 0, slot, -1.0)
-    slot_ref[...] = jnp.transpose(slot)[:EXPERTS]
+        member_t = member_t + (mine[k : k + 1] == at).astype(F32)
+    earlier = (rows_of((rows, rows)) < lanes((rows, rows))).astype(BF16)
+    slot = nn(member_t.astype(BF16), earlier)
+    slot_ref[...] = jnp.where(member_t > 0, slot, -1.0)[:EXPERTS]
+    member = jnp.transpose(member_t)
 
     def some_rows(i):
         hot = pick(slot_ref, [peer(me, 4 * i + j) for j in range(4)], 40)
@@ -264,7 +291,7 @@
 
     loop(1, FSDP, lambda k: packed_copy(k).wait_recv())
     keep[0].wait()
-    tail = jnp.transpose(packed_all_ref[:, :, 768:896].reshape(width, 128).astype(F32))
+    tail = jnp.transpose(packed_all_ref[:, :, 512:640].reshape(width, 128).astype(F32))
     normed = (wide * inverse * tail[EXPERTS : EXPERTS + 1]).astype(BF16)
     normed_all_ref[...] = normed
     lin = nn(normed, packed_all_ref[:, :, 0:512].reshape(width, 512))
@@ -285,7 +312,9 @@
         outs.append(nn(shares, value))
     attended = jnp.concatenate(outs, axis=1).astype(BF16)
     attended_ref[...] = attended
-    branch = nt(attended, packed_all_ref[:, :, 512:768].reshape(width, 256))
+    loop(1, FSDP, lambda k: outw_copy(k).wait_recv())
+    keep[3].wait()
+    branch = nt(attended, out_all_ref[...].reshape(width, 256))
     branch_out[...] = branch.astype(BF16).reshape(TP, rows, width)
     for x in range(2):
         branch_copy(x).start()
@@ -319,7 +348,7 @@
     inverse_two = lax.rsqrt(jnp.mean(middle * middle, axis=-1, keepdims=True) + EPSILON)
     normed_two = (middle * inverse_two * tail[EXPERTS + 1 : EXPERTS + 2]).astype(BF16)
     normed_two_ref[...] = normed_two
-    logits = nn(normed_two, packed_all_ref[:, :, 768:896].reshape(width, 128))
+    logits = nn(normed_two, packed_all_ref[:, :, 512:640].reshape(width, 128))
     logits = jnp.where(member > 0, logits, MASKED)
     grown = jnp.exp(logits - jnp.max(logits, axis=1, keepdims=True)) * member
     gates_ref[...] = grown / jnp.sum(grown, axis=1, keepdims=True)
@@ -346,6 +375,7 @@
     def sent():
         def gone(k):
             packed_copy(k).wait_send()
+            outw_copy(k).wait_send()
             blocks_copy(k).wait_send()
             spare_copy(k).wait_send()
 
@@ -594,7 +624,7 @@
     gates = gates_ref[...]
     grad_chosen = gates * (grad_gates - jnp.sum(gates * grad_gates, axis=1, keepdims=True))
     grad_logits = grad_chosen.astype(BF16)
-    tail = packed_all_ref[:, :, 768:896].reshape(width, 128)
+    tail = packed_all_ref[:, :, 512:640].reshape(width, 128)
     gain_two = jnp.transpose(tail.astype(F32))[EXPERTS + 1 : EXPERTS + 2]
     router_part_ref[...] = tn(normed_two_ref[...], grad_logits)
     dy = grad_rows + nt(grad_logits, tail)
@@ -634,14 +664,15 @@
 
 def backward_part(
     out_ready, pair_copy,
-    grad_middle_ref, packed_all_ref, heads_ref, normed_all_ref, attended_ref, cos_ref, sin_ref,
+    grad_middle_ref, packed_all_ref, out_all_ref, heads_ref, normed_all_ref, attended_ref,
+    cos_ref, sin_ref,
     seg_ref, grads_ref, middle_ref, hot_main_ref, hot_spare_ref,
     inputs_ref, router_part_ref, second_ref,
-    output_ref, grad_inputs_ref, sums_ref, weight_grads_ref,
-    branch_own, branch_all, out_in, out_spare_in, pair_in, across_send, across_in, dw_send, dw_in,
-    normed_send, normed_in, sums_send, sums_in, small_own, small_in,
+    output_ref, grad_inputs_ref, sums_ref, out_sums_ref, dw_in,
+    branch_own, branch_all, out_in, out_spare_in, pair_in, across_send, across_in, dw_send,
+    normed_send, normed_in, sums_send, sums_in, outs_send, outs_in, small_own, small_in,
     branch_s, branch_r, across_s, across_r,
-    dw_s, dw_r, normed_s, normed_r, sums_s, sums_r, small_s, small_r,
+    dw_s, dw_r, normed_s, normed_r, sums_s, sums_r, outs_s, outs_r, small_s, small_r,
 ):
     me, tp = lax.axis_index("fsdp"), lax.axis_index("tp")
     rows, width = inputs_ref.shape
@@ -677,6 +708,10 @@
     def sums_copy(k):
         p = peer(me, k)
         return to_fsdp(sums_send.at[p], sums_in.at[k], sums_s.at[k], sums_r.at[k], p)
+
+    def outs_copy(k):
+        p = peer(me, k)
+        return to_fsdp(outs_send.at[p], outs_in.at[k], outs_s.at[k], outs_r.at[k], p)
 
     def small_copy(k):
         return to_tp(small_own, small_in.at[k], small_s.at[k], small_r.at[k], lax.rem(tp + k, TP))
@@ -708,7 +743,10 @@
     branch_copy(2).wait_recv()
     branch = branch_all[...].reshape(total, width)
     out_part = tn(branch, attended_ref[...])
-    grad_attended = nn(branch, packed_all_ref[:, :, 512:768].reshape(width, 256)).astype(BF16)
+    outs_send[...] = out_part.astype(BF16).reshape(FSDP, 32, 256)
+    loop(1, FSDP, lambda k: outs_copy(k).start())
+    outs_in[0] = outs_send[me]
+    grad_attended = nn(branch, out_all_ref[...].reshape(width, 256)).astype(BF16)
     scale = HEAD_SIZE ** (-0.5)
     dq, dk, dv = [], [], []
     for g in range(2):
@@ -732,6 +770,14 @@
             dv_sum = dv_one if dv_sum is None else dv_sum + dv_one
         dk.append(dk_sum)
         dv.append(dv_sum)
+        if g > 0:
+            continue
+        across_copy.wait_recv()
+        dw_send[...] = (
+            grads_ref[tp].astype(F32) + pair_in[near].astype(F32) + across_in[...].astype(F32)
+        ).astype(BF16)
+        loop(1, FSDP, lambda k: dw_copy(k).start())
+        dw_in[me] = dw_send[me]
     turned = jnp.concatenate(dq + dk, axis=1)
     turn = turned * wide_table(cos_ref[...], 384) - half_swap(turned) * wide_table(
         sin_ref[...], 384
@@ -741,18 +787,17 @@
     normed_send[...] = grad_normed.astype(BF16).reshape(TP, rows, width)
     for x in range(2):
         normed_copy(x).start()
-    gain_one = jnp.transpose(packed_all_ref[:, :, 768:896].reshape(width, 128).astype(F32))[
+    gain_one = jnp.transpose(packed_all_ref[:, :, 512:640].reshape(width, 128).astype(F32))[
         EXPERTS : EXPERTS + 1
     ]
     first = jnp.sum(grad_normed * normed_all_ref[...].astype(F32), axis=0, keepdims=True) / gain_one
 
     qkv_part = tn(normed_all_ref[...], grad_lin)
     sums_send[:, :, 0:512] = qkv_part.astype(BF16).reshape(FSDP, 32, 512)
-    sums_send[:, :, 512:768] = out_part.astype(BF16).reshape(FSDP, 32, 256)
     at = rows_of((128, width))
     gains = jnp.where(at == EXPERTS, first, 0.0) + jnp.where(at == EXPERTS + 1, second_ref[...], 0.0)
     small = router_part_ref[...] + jnp.transpose(gains)
-    sums_send[:, :, 768:896] = small.astype(BF16).reshape(FSDP, 32, 128)
+    sums_send[:, :, 512:640] = small.astype(BF16).reshape(FSDP, 32, 128)
     loop(1, FSDP, lambda k: sums_copy(k).start())
     sums_in[0] = sums_send[me]
 
@@ -762,13 +807,6 @@
         normed_send[across].astype(F32) + normed_in[far].astype(F32)
     ).astype(BF16)
     normed_across.start()
-
-    across_copy.wait_recv()
-    dw_send[...] = (
-        grads_ref[tp].astype(F32) + pair_in[near].astype(F32) + across_in[...].astype(F32)
-    ).astype(BF16)
-    loop(1, FSDP, lambda k: dw_copy(k).start())
-    dw_in[me] = dw_send[me]
 
     normed_across.wait_recv()
     dy = normed_send[tp].astype(F32) + normed_in[near].astype(F32) + normed_in[3].astype(F32)
@@ -795,18 +833,20 @@
 
     loop(1, FSDP, lambda k: sums_copy(k).wait_recv())
     sums = jnp.sum(sums_in[...].astype(F32), axis=0)
-    sums_ref[:, :768] = sums[:, :768]
-    small_own[...] = sums[:, 768:]
+    sums_ref[:, :512] = sums[:, :512]
+    small_own[...] = sums[:, 512:]
     for k in (2, 1, 3):
         small_copy(k).start()
     loop(1, FSDP, lambda k: dw_copy(k).wait_recv())
-    weight_grads_ref[...] = dw_in[...].astype(F32)
+    loop(1, FSDP, lambda k: outs_copy(k).wait_recv())
+    out_sums_ref[...] = jnp.sum(outs_in[...].astype(F32), axis=0)
     for k in range(1, TP):
         small_copy(k).wait_recv()
-    sums_ref[:, 768:] = small_own[...] + small_in[1] + small_in[2] + small_in[3]
+    sums_ref[:, 512:] = small_own[...] + small_in[1] + small_in[2] + small_in[3]
 
     def gone(k):
         sums_copy(k).wait_send()
+        outs_copy(k).wait_send()
         dw_copy(k).wait_send()
 
     loop(1, FSDP, gone)
@@ -821,17 +861,18 @@
 
 
 def layer_kernel(
-    packed_ref, inputs_ref, seg_ref, routes_ref, blocks_ref, cot_ref,
-    output_ref, grad_inputs_ref, sums_ref, weight_grads_ref,
-    middle, normed_two, gates, slot, weights, cot_main, cot_spare, packed_all, heads, normed_all,
-    attended, cosine, sine,
-    inputs_all, blocks_in, rows_out, spare_out, branch_out, branch_in,
+    query_ref, key_ref, value_ref, out_weight_ref, router_ref, first_gain_ref, second_gain_ref,
+    gate_ref, up_ref, down_ref, inputs_ref, seg_ref, routes_ref, cot_ref,
+    output_ref, grad_inputs_ref, sums_ref, out_sums_ref, weight_grads_ref,
+    middle, normed_two, gates, slot, weights, cot_main, cot_spare, packed_all, out_all,
+    heads, normed_all, attended, cosine, sine,
+    packed, blocks, inputs_all, blocks_in, rows_out, spare_out, branch_out, branch_in,
     router_part, second_part, hot_main, hot_spare, grad_middle, out_spare,
     gate_mat, up_mat, down_mat, gate_t, row_send, spare_send, row_in, spare_in,
     back_spare_send, back_in, back_spare_in,
     hidden, dgate, dup, ghidden, sel, gate_grads, out_in, out_spare_in,
-    branch_own, branch_all, pair_in, across_send, across_in, dw_send, dw_in, normed_in,
-    sums_send, sums_in, small_own, small_in,
+    branch_own, branch_all, pair_in, across_send, across_in, dw_send, normed_in,
+    sums_send, sums_in, outs_send, outs_in, small_own, small_in,
     *sems,
 ):
     tp = lax.axis_index("tp")
@@ -843,11 +884,12 @@
         return taken
 
     pass_weights, weights_ready, cot_ready, forward_sent = forward_part(
-        packed_ref, inputs_ref, seg_ref, routes_ref, blocks_ref, cot_ref,
+        query_ref, key_ref, value_ref, out_weight_ref, router_ref, first_gain_ref,
+        second_gain_ref, gate_ref, up_ref, down_ref, inputs_ref, seg_ref, routes_ref, cot_ref,
         middle, normed_two, gates, slot, weights, cot_main, cot_spare,
-        packed_all, heads, normed_all, attended, cosine, sine,
-        inputs_all, blocks_in, rows_out, spare_out, branch_out, branch_in,
-        *take(15),
+        packed_all, out_all, heads, normed_all, attended, cosine, sine,
+        packed, blocks, inputs_all, blocks_in, rows_out, spare_out, branch_out, branch_in,
+        *take(17),
     )
     core = lax.rem(tp, 2)
     pair_s, pair_r = take(2)
@@ -877,54 +919,62 @@
     )
     backward_part(
         out_ready, pair_copy,
-        grad_middle, packed_all, heads, normed_all, attended, cosine, sine, seg_ref,
+        grad_middle, packed_all, out_all, heads, normed_all, attended, cosine, sine, seg_ref,
         weights, middle, hot_main, hot_spare, inputs_ref, router_part, second_part,
-        output_ref, grad_inputs_ref, sums_ref, weight_grads_ref,
+        output_ref, grad_inputs_ref, sums_ref, out_sums_ref, weight_grads_ref,
         branch_own, branch_all, out_in, out_spare_in, pair_in, across_send, across_in,
-        dw_send, dw_in, branch_out, normed_in, sums_send, sums_in, small_own, small_in,
-        *take(12),
+        dw_send, branch_out, normed_in, sums_send, sums_in, outs_send, outs_in,
+        small_own, small_in,
+        *take(14),
     )
     forward_sent()
     expert_sent()
 
 
-def layer(packed, inputs, seg, routes, blocks, cot):
+def layer(*operands):
+    inputs, seg = operands[10], operands[11]
     rows, width = inputs.shape
     total = seg.shape[1]
+    packed_shape, out_shape, blocks_shape = (32, 640), (32, 256), (EXPERTS, 96, 128)
     hidden = 128 * TP
     slots = FSDP * SPARE
     vmem = pl.BlockSpec(memory_space=pltpu.VMEM)
     out = (
         shape((rows, width), BF16),
         shape((rows, width), F32),
-        shape(packed.shape, F32),
-        shape(blocks.shape, F32),
+        shape(packed_shape, F32),
+        shape(out_shape, F32),
+        shape(blocks_shape, BF16),
     )
     block = pltpu.VMEM((FSDP, 32, width), BF16)
     spare = pltpu.VMEM((FSDP, 1, width), F32)
     spare_wide = pltpu.VMEM((FSDP, 1, width + 128), F32)
     four = pltpu.VMEM((TP, rows, width), BF16)
-    shards = pltpu.VMEM(blocks.shape, BF16)
-    packs = pltpu.VMEM((FSDP, *packed.shape), BF16)
+    shards = pltpu.VMEM(blocks_shape, BF16)
+    packs = pltpu.VMEM((FSDP, *packed_shape), BF16)
+    outs = pltpu.VMEM((FSDP, *out_shape), BF16)
     return pl.pallas_call(
         layer_kernel,
         out_shape=out,
-        in_specs=[vmem] * 6,
+        in_specs=[vmem] * len(operands),
         out_specs=[vmem] * len(out),
         scratch_shapes=[
             pltpu.VMEM((rows, width), F32),
             pltpu.VMEM((rows, width), BF16),
             pltpu.VMEM((rows, 128), F32),
             pltpu.VMEM((EXPERTS, rows), F32),
-            pltpu.VMEM((TP, *blocks.shape), BF16),
+            pltpu.VMEM((TP, *blocks_shape), BF16),
             block,
             spare,
             packs,
+            outs,
             pltpu.VMEM((total, 512), BF16),
             pltpu.VMEM((total, width), BF16),
             pltpu.VMEM((total, 256), BF16),
             pltpu.VMEM((total, 128), F32),
             pltpu.VMEM((total, 128), F32),
+            pltpu.VMEM(packed_shape, BF16),
+            shards,
             four,
             shards,
             block,
@@ -954,30 +1004,77 @@
             spare,
             pltpu.VMEM((rows, width), BF16),
             four,
-            pltpu.VMEM((2, *blocks.shape), BF16),
-            *[shards] * 4,
+            pltpu.VMEM((2, *blocks_shape), BF16),
+            *[shards] * 3,
             four,
             packs,
             packs,
+            outs,
+            outs,
             pltpu.VMEM((32, 128), F32),
             pltpu.VMEM((TP, 32, 128), F32),
-            *[dma(FSDP)] * 8,
+            *[dma(FSDP)] * 10,
             *[dma(TP)] * 6,
-            dma(4),
+            dma(5),
             *[dma(2)] * 2,
             *[dma(FSDP)] * 12,
             *[dma(TP)] * 2,
             *[dma(1)] * 2,
             *[dma(FSDP)] * 2,
             *[dma(TP)] * 2,
-            *[dma(FSDP)] * 2,
+            *[dma(FSDP)] * 4,
             *[dma(TP)] * 2,
         ],
         compiler_params=pltpu.CompilerParams(
             collective_id=1, has_side_effects=True, vmem_limit_bytes=62 * 2**20
         ),
         name="layer",
-    )(packed, inputs, seg, routes, blocks, cot)
+    )(*operands)
+
+
+def finish_kernel(
+    output_in, grad_inputs_in, sums_ref, out_sums_ref, weight_grads_ref,
+    output_ref, grad_inputs_ref, query_ref, key_ref, value_ref, out_ref, router_ref,
+    gains_ref, gate_ref, up_ref, down_ref,
+):
+    output_ref[...] = output_in[...]
+    grad_inputs_ref[...] = grad_inputs_in[...]
+    query_ref[...] = sums_ref[:, 0:256]
+    key_ref[...] = sums_ref[:, 256:384]
+    value_ref[...] = sums_ref[:, 384:512]
+    out_ref[...] = out_sums_ref[...]
+    router_ref[...] = sums_ref[:, 512:544]
+    tail = jnp.concatenate([sums_ref[:, 512:640], jnp.zeros((96, 128), F32)], axis=0)
+    gains_ref[...] = jnp.transpose(tail)[EXPERTS : EXPERTS + 8, :32]
+    gate_ref[...] = weight_grads_ref[:, 0:32].astype(F32)
+    up_ref[...] = weight_grads_ref[:, 32:64].astype(F32)
+    down_ref[...] = weight_grads_ref[:, 64:96].astype(F32)
+
+
+def finish(*operands):
+    vmem = pl.BlockSpec(memory_space=pltpu.VMEM)
+    shard = shape((EXPERTS, 32, 128), F32)
+    out = (
+        shape(operands[0].shape, BF16),
+        shape(operands[1].shape, F32),
+        shape((32, 256), F32),
+        shape((32, 128), F32),
+        shape((32, 128), F32),
+        shape((32, 256), F32),
+        shape((32, 32), F32),
+        shape((8, 32), F32),
+        shard,
+        shard,
+        shard,
+    )
+    return pl.pallas_call(
+        finish_kernel,
+        out_shape=out,
+        in_specs=[vmem] * len(operands),
+        out_specs=[vmem] * len(out),
+        compiler_params=pltpu.CompilerParams(vmem_limit_bytes=32 * 2**20),
+        name="finish",
+    )(*operands)
 
 
 def per_device(
@@ -996,45 +1093,39 @@
     down_weight,
     cotangent,
 ):
-    row_count = inputs.shape[0]
-    my_offset = lax.axis_index("tp") * row_count
-    width_shard = query_weight.shape[0]
-    q_cols, k_cols, o_cols = query_weight.shape[1], key_projection_weight.shape[1], out_weight.shape[0]
-
-    wide = q_cols + 2 * k_cols + o_cols
-    packed = jnp.concatenate(
-        [
-            query_weight,
-            key_projection_weight,
-            value_projection_weight,
-            out_weight.T,
-            router_weight,
-            first_gain[:, None],
-            second_gain[:, None],
-            jnp.zeros((width_shard, 128 - EXPERTS - 2), BF16),
-        ],
-        axis=1,
-    )
-    blocks = jnp.concatenate(
-        [gate_weight, up_weight, jnp.transpose(down_weight, (0, 2, 1))], axis=1
-    )
-    my_routes = lax.dynamic_slice_in_dim(routes, my_offset, row_count, 0)
-    output, grad_inputs, sums, weight_grads = layer(
-        packed, inputs, segments, my_routes, blocks, cotangent
-    )
+    parts = layer(
+        query_weight,
+        key_projection_weight,
+        value_projection_weight,
+        out_weight.T,
+        router_weight,
+        first_gain[None, :],
+        second_gain[None, :],
+        gate_weight,
+        up_weight,
+        jnp.transpose(down_weight, (0, 2, 1)),
+        inputs,
+        segments,
+        routes.T,
+        cotangent,
+    )
+    (
+        output, grad_inputs, grad_query, grad_key, grad_value, grad_out, grad_router,
+        grad_gains, grad_gate, grad_up, grad_down,
+    ) = finish(*parts)
     return (
         output,
         grad_inputs,
-        sums[:, :q_cols],
-        sums[:, q_cols : q_cols + k_cols],
-        sums[:, q_cols + k_cols : q_cols + 2 * k_cols],
-        sums[:, q_cols + 2 * k_cols : wide].T,
-        sums[:, wide : wide + EXPERTS],
-        sums[:, wide + EXPERTS],
-        sums[:, wide + EXPERTS + 1],
-        weight_grads[:, :width_shard],
-        weight_grads[:, width_shard : 2 * width_shard],
-        jnp.transpose(weight_grads[:, 2 * width_shard :], (0, 2, 1)),
+        grad_query,
+        grad_key,
+        grad_value,
+        grad_out.T,
+        grad_router,
+        grad_gains[0],
+        grad_gains[1],
+        grad_gate,
+        grad_up,
+        jnp.transpose(grad_down, (0, 2, 1)),
     )
 
 

time: 230 us -> 209 us (0.909)
  Pallas kernels: 212 us -> 202 us
  local copies, waits for them, and re-layouts: 14.1 us -> 5.28 us
    pallas_call x1 -> x2, Pallas kernels: 212 us -> 202 us  [the longest x1 200 us: layer(): pl.pallas_call(layer_kernel, out_shape=out, in_specs=[vmem] * len(operand...]
    slice x3 -> x0, local copies, waits for them, and re-layouts: 4.17 us -> none  [the longest x1 1.5 us: per_device(): sums[:, wide + EXPERTS + 1]]
    transpose x2 -> x0, local copies, waits for them, and re-layouts: 4.01 us -> none  [the longest x1 2.61 us: per_device(): jnp.transpose(weight_grads[:, 2 * width_shard:], (0, 2, 1))]
    unnamed x9 -> x10, local copies, waits for them, and re-layouts: 2.94 us -> 4.76 us
where the time goes in v6:
time: 209 us; the launch traced here: 207 us
  Pallas kernels  202 us (97%)
  local copies, waits for them, and re-layouts  5.28 us (3%)
    pallas_call x1, Pallas kernels, layer(): pl.pallas_call(layer_kernel, out_shape=out, in_specs=[vmem] * len(operand...  200 us
    unnamed x10, local copies, waits for them, and re-layouts  4.76 us

profile of v6, /device:TPU:8, one launch (start us, length us, event | category | flops | bytes accessed | tf_op | source)
XLA Modules:
  0.0 207.5 jit_solution(10233367758810775811)
XLA Ops:
  0.6 200.0 %layer.1 = (bf16[128,1024]{1,0:T(8,128)(2,1)}, f32[128,1024]{1,0:T(8,128)}, f32[32,640]{1,0:T(8,128)}, f32[32,256]{1,0:T(8,128)}, bf16[32,96,128]{2,1,0:T(8,128)(2,1)}) custom-call(bf16[32,256]{1,0:T(8,128)(2,1)} %query_ref.1, bf16[32,128]{1,0:T(8,128)(2,1)} %key_ref.1, bf16[32,128]{1,0:T(8,128)(2,1)} %value_ref.1, bf16[32,256]{1,0:T(8,128)(2,1)} %bitcast.12, ...), custom_call_target="tpu_custom_call" | custom-call | tf_op jit(solution)/shard_map/layer/pallas_call | solution.py:956
  200.7 0.0 copy-start
  200.7 1.1 copy-done
  201.8 0.0 copy-start.1
  201.8 1.0 copy-done.1
  202.9 0.0 copy-start.2
  202.9 0.9 copy-done.2
  203.8 0.0 copy-start.3
  203.8 0.9 copy-done.3
  204.7 0.0 copy-start.4
  204.7 0.8 copy-done.4
  205.5 1.5 finish.1
  207.0 0.5 slice_bitcast_fusion
Async XLA Ops:
  200.7 1.1 copy-start
  201.8 1.0 copy-start.1
  202.9 0.9 copy-start.2
  203.8 0.9 copy-start.3
  204.7 0.8 copy-start.4

commit v7 on v6

--- a/solution.py
+++ b/solution.py
@@ -663,7 +663,7 @@
 
 
 def backward_part(
-    out_ready, pair_copy,
+    out_ready, pair_copy, packed_ref,
     grad_middle_ref, packed_all_ref, out_all_ref, heads_ref, normed_all_ref, attended_ref,
     cos_ref, sin_ref,
     seg_ref, grads_ref, middle_ref, hot_main_ref, hot_spare_ref,
@@ -743,7 +743,10 @@
     branch_copy(2).wait_recv()
     branch = branch_all[...].reshape(total, width)
     out_part = tn(branch, attended_ref[...])
-    outs_send[...] = out_part.astype(BF16).reshape(FSDP, 32, 256)
+    outs_send[:, :, 0:256] = out_part.astype(BF16).reshape(FSDP, 32, 256)
+    second = jnp.where(rows_of((128, width)) == EXPERTS + 1, second_ref[...], 0.0)
+    small = router_part_ref[...] + jnp.transpose(second)
+    outs_send[:, :, 256:384] = small.astype(BF16).reshape(FSDP, 32, 128)
     loop(1, FSDP, lambda k: outs_copy(k).start())
     outs_in[0] = outs_send[me]
     grad_attended = nn(branch, out_all_ref[...].reshape(width, 256)).astype(BF16)
@@ -783,6 +786,11 @@
         sin_ref[...], 384
     )
     grad_lin = jnp.concatenate([turn] + dv, axis=1).astype(BF16)
+    qkv_part = tn(normed_all_ref[...], grad_lin)
+    sums_send[...] = qkv_part.astype(BF16).reshape(FSDP, 32, 512)
+    loop(1, FSDP, lambda k: sums_copy(k).start())
+    sums_in[0] = sums_send[me]
+
     grad_normed = nt(grad_lin, packed_all_ref[:, :, 0:512].reshape(width, 512))
     normed_send[...] = grad_normed.astype(BF16).reshape(TP, rows, width)
     for x in range(2):
@@ -790,17 +798,6 @@
     gain_one = jnp.transpose(packed_all_ref[:, :, 512:640].reshape(width, 128).astype(F32))[
         EXPERTS : EXPERTS + 1
     ]
-    first = jnp.sum(grad_normed * normed_all_ref[...].astype(F32), axis=0, keepdims=True) / gain_one
-
-    qkv_part = tn(normed_all_ref[...], grad_lin)
-    sums_send[:, :, 0:512] = qkv_part.astype(BF16).reshape(FSDP, 32, 512)
-    at = rows_of((128, width))
-    gains = jnp.where(at == EXPERTS, first, 0.0) + jnp.where(at == EXPERTS + 1, second_ref[...], 0.0)
-    small = router_part_ref[...] + jnp.transpose(gains)
-    sums_send[:, :, 512:640] = small.astype(BF16).reshape(FSDP, 32, 128)
-    loop(1, FSDP, lambda k: sums_copy(k).start())
-    sums_in[0] = sums_send[me]
-
     for x in range(2):
         normed_copy(x).wait_recv()
     normed_in[2] = (
@@ -833,13 +830,16 @@
 
     loop(1, FSDP, lambda k: sums_copy(k).wait_recv())
     sums = jnp.sum(sums_in[...].astype(F32), axis=0)
-    sums_ref[:, :512] = sums[:, :512]
-    small_own[...] = sums[:, 512:]
+    sums_ref[:, :512] = sums
+    loop(1, FSDP, lambda k: outs_copy(k).wait_recv())
+    out_sums = jnp.sum(outs_in[...].astype(F32), axis=0)
+    out_sums_ref[...] = out_sums[:, :256]
+    first = jnp.sum(packed_ref[:, :512].astype(F32) * sums, axis=1, keepdims=True)
+    first = first / packed_ref[:, 544:545].astype(F32)
+    small_own[...] = out_sums[:, 256:] + jnp.where(lanes((32, 128)) == EXPERTS, first, 0.0)
     for k in (2, 1, 3):
         small_copy(k).start()
     loop(1, FSDP, lambda k: dw_copy(k).wait_recv())
-    loop(1, FSDP, lambda k: outs_copy(k).wait_recv())
-    out_sums_ref[...] = jnp.sum(outs_in[...].astype(F32), axis=0)
     for k in range(1, TP):
         small_copy(k).wait_recv()
     sums_ref[:, 512:] = small_own[...] + small_in[1] + small_in[2] + small_in[3]
@@ -918,7 +918,7 @@
         *take(12),
     )
     backward_part(
-        out_ready, pair_copy,
+        out_ready, pair_copy, packed,
         grad_middle, packed_all, out_all, heads, normed_all, attended, cosine, sine, seg_ref,
         weights, middle, hot_main, hot_spare, inputs_ref, router_part, second_part,
         output_ref, grad_inputs_ref, sums_ref, out_sums_ref, weight_grads_ref,
@@ -1007,10 +1007,8 @@
             pltpu.VMEM((2, *blocks_shape), BF16),
             *[shards] * 3,
             four,
-            packs,
-            packs,
-            outs,
-            outs,
+            *[pltpu.VMEM((FSDP, 32, 512), BF16)] * 2,
+            *[pltpu.VMEM((FSDP, 32, 384), BF16)] * 2,
             pltpu.VMEM((32, 128), F32),
             pltpu.VMEM((TP, 32, 128), F32),
             *[dma(FSDP)] * 10,
@@ -1072,7 +1070,7 @@
         out_shape=out,
         in_specs=[vmem] * len(operands),
         out_specs=[vmem] * len(out),
-        compiler_params=pltpu.CompilerParams(vmem_limit_bytes=32 * 2**20),
+        compiler_params=pltpu.CompilerParams(vmem_limit_bytes=60 * 2**20),
         name="finish",
     )(*operands)
 

time: 209 us -> 205 us (0.981)
  local copies, waits for them, and re-layouts: 5.28 us -> 1.27 us
    unnamed x10 -> x0, local copies, waits for them, and re-layouts: 4.76 us -> none
where the time goes in v7:
time: 205 us; the launch traced here: 204 us
  Pallas kernels  203 us (99%)
    pallas_call x1, Pallas kernels, layer(): pl.pallas_call(layer_kernel, out_shape=out, in_specs=[vmem] * len(operand...  200 us

profile of v7, /device:TPU:8, one launch (start us, length us, event | category | flops | bytes accessed | tf_op | source)
XLA Modules:
  0.0 204.5 jit_solution(13793823818934558058)
XLA Ops:
  0.6 199.7 %layer.1 = (bf16[128,1024]{1,0:T(8,128)(2,1)}, f32[128,1024]{1,0:T(8,128)}, f32[32,640]{1,0:T(8,128)}, f32[32,256]{1,0:T(8,128)}, bf16[32,96,128]{2,1,0:T(8,128)(2,1)}) custom-call(bf16[32,256]{1,0:T(8,128)(2,1)} %query_ref.1, bf16[32,128]{1,0:T(8,128)(2,1)} %key_ref.1, bf16[32,128]{1,0:T(8,128)(2,1)} %value_ref.1, bf16[32,256]{1,0:T(8,128)(2,1)} %bitcast.12, ...), custom_call_target="tpu_custom_call" | custom-call | tf_op jit(solution)/shard_map/layer/pallas_call | solution.py:956
  200.3 2.9 %finish.1 = (bf16[128,1024]{1,0:T(8,128)(2,1)}, f32[128,1024]{1,0:T(8,128)}, f32[32,256]{1,0:T(8,128)}, f32[32,128]{1,0:T(8,128)}, f32[32,128]{1,0:T(8,128)}, /*...) custom-call(bf16[128,1024]{1,0:T(8,128)(2,1)} %get-tuple-element.28., ...), custom_call_target="tpu_custom_call" | custom-call | tf_op jit(solution)/shard_map/finish/pallas_call | solution.py:1068
  203.2 1.3 slice_bitcast_fusion

commit v8 on v7

--- a/solution.py
+++ b/solution.py
@@ -568,13 +568,11 @@
     def outputs(i):
         out = nt(hidden_ref[pl.ds(256 * i, 256), :], down_mat[...])
         out_main_ref[pl.ds(8 * i, 8)] = out.astype(BF16).reshape(8, 32, width)
-        loop(jnp.maximum(8 * i, 1), 8 * i + 8, lambda k: out_copy(k).start())
 
     loop(0, 4, outputs)
     out = nt(hidden_ref[pl.ds(main, FSDP), :], down_mat[...])
     for k in range(FSDP):
         out_spare_ref[k] = out[k : k + 1]
-    loop(1, FSDP, lambda k: out_spare_copy(k).start())
     out_in[0] = out_main_ref[0]
     out_spare_in[0] = out_spare_ref[0]
 
@@ -607,6 +605,12 @@
         bspare_copy(k).wait_recv()
 
     loop(1, FSDP, back_got)
+
+    def out_go(k):
+        out_copy(k).start()
+        out_spare_copy(k).start()
+
+    loop(1, FSDP, out_go)
     hot = hot_main_ref[...].reshape(main, rows)
     hot_spare = hot_spare_ref[...]
     back_spare = back_spare_in[...].reshape(FSDP, 1152)
@@ -773,14 +777,6 @@
             dv_sum = dv_one if dv_sum is None else dv_sum + dv_one
         dk.append(dk_sum)
         dv.append(dv_sum)
-        if g > 0:
-            continue
-        across_copy.wait_recv()
-        dw_send[...] = (
-            grads_ref[tp].astype(F32) + pair_in[near].astype(F32) + across_in[...].astype(F32)
-        ).astype(BF16)
-        loop(1, FSDP, lambda k: dw_copy(k).start())
-        dw_in[me] = dw_send[me]
     turned = jnp.concatenate(dq + dk, axis=1)
     turn = turned * wide_table(cos_ref[...], 384) - half_swap(turned) * wide_table(
         sin_ref[...], 384
@@ -798,6 +794,14 @@
     gain_one = jnp.transpose(packed_all_ref[:, :, 512:640].reshape(width, 128).astype(F32))[
         EXPERTS : EXPERTS + 1
     ]
+
+    across_copy.wait_recv()
+    dw_send[...] = (
+        grads_ref[tp].astype(F32) + pair_in[near].astype(F32) + across_in[...].astype(F32)
+    ).astype(BF16)
+    loop(1, FSDP, lambda k: dw_copy(k).start())
+    dw_in[me] = dw_send[me]
+
     for x in range(2):
         normed_copy(x).wait_recv()
     normed_in[2] = (

time: 205 us -> 192 us (0.937); the launches traced: 204 us -> 189 us
  Pallas kernels: 203 us -> 187 us
    pallas_call x1, Pallas kernels: 200 us -> 184 us  [layer(): pl.pallas_call(layer_kernel, out_shape=out, in_specs=[vmem] * len(operand...]
where the time goes in v8:
time: 192 us; the launch traced here: 189 us
  Pallas kernels  187 us (97%)
    pallas_call x1, Pallas kernels, layer(): pl.pallas_call(layer_kernel, out_shape=out, in_specs=[vmem] * len(operand...  184 us

profile of v8, /device:TPU:8, one launch (start us, length us, event | category | flops | bytes accessed | tf_op | source)
XLA Modules:
  0.0 189.2 jit_solution(18283824930634884805)
XLA Ops:
  0.6 184.4 %layer.1 = (bf16[128,1024]{1,0:T(8,128)(2,1)}, f32[128,1024]{1,0:T(8,128)}, f32[32,640]{1,0:T(8,128)}, f32[32,256]{1,0:T(8,128)}, bf16[32,96,128]{2,1,0:T(8,128)(2,1)}) custom-call(bf16[32,256]{1,0:T(8,128)(2,1)} %query_ref.1, bf16[32,128]{1,0:T(8,128)(2,1)} %key_ref.1, bf16[32,128]{1,0:T(8,128)(2,1)} %value_ref.1, bf16[32,256]{1,0:T(8,128)(2,1)} %bitcast.12, ...), custom_call_target="tpu_custom_call" | custom-call | tf_op jit(solution)/shard_map/layer/pallas_call | solution.py:960
  185.0 2.9 %finish.1 = (bf16[128,1024]{1,0:T(8,128)(2,1)}, f32[128,1024]{1,0:T(8,128)}, f32[32,256]{1,0:T(8,128)}, f32[32,128]{1,0:T(8,128)}, f32[32,128]{1,0:T(8,128)}, /*...) custom-call(bf16[128,1024]{1,0:T(8,128)(2,1)} %get-tuple-element.28., ...), custom_call_target="tpu_custom_call" | custom-call | tf_op jit(solution)/shard_map/finish/pallas_call | solution.py:1072
  187.9 1.3 slice_bitcast_fusion
